TPU v7x, 32 devices: a whole 2x2x4 slice. The times are simulated.
32 devices in a mesh: blk: 2 (over y), grp: 16 (over z, x, core).
Axes of the slice: x: 2, y: 2, z: 4, core: 2. Of those that a mesh axis runs over, the one named last changes fastest.
Arguments:
- inputs: float32 [8, 4096], P(None, ('blk', 'grp')), may hold values from 0 to 1
- probes: float32 [16, 4096], P(None, ('blk', 'grp')), may hold values from -2 to 2
- lengths: float32 [8], replicated, may hold values from 0.2 to 0.6
- noise: float32 [1], replicated, may hold values from 0.1 to 1
- pivots: int32 [128], replicated, may hold values from 0 to 4095, as said below
Outputs:
- panel: float32 [128, 4096], P(None, ('blk', 'grp'))
- product: float32 [16, 4096], P(None, ('blk', 'grp'))
Inputs may be any that keep to these rules, and one draw needn't show every extreme that they name: `pivots`: the indices are distinct.
All inputs are finite; a program needn't handle non-finite values.
Results may differ from a plain program's by a relative error of at most 0.00027.
Values sent between devices are 32-bit elements; how exact they have to be, the bound alone decides.
No kernel may reach another device: no remote copies, remote signals or barrier semaphores. Data moves between devices by JAX's collectives and lax.ppermute only.
A program may use at most 64 MiB of HBM per device.

v0:
```python
import math

import jax
import jax.numpy as jnp
from jax import lax
from jax.sharding import PartitionSpec as P


def from_behind(value, axis, steps):
    count = lax.axis_size(axis)
    pairs = [(source, (source + steps) % count) for source in range(count)]
    return lax.ppermute(value, axis, pairs)


def kernel(left, right):
    cross = jnp.dot(
        left.T, right, precision=lax.Precision.HIGHEST, preferred_element_type=jnp.float32
    )
    dist = jnp.sum(left * left, 0)[:, None] + jnp.sum(right * right, 0)[None, :] - 2.0 * cross
    radius = jnp.sqrt(5.0 * jnp.maximum(dist, 0.0))
    return (1.0 + radius + radius * radius / 3.0) * jnp.exp(-radius)


def apply_block(total, rows_x, columns):
    dims = rows_x.shape[0]
    cols = columns.shape[1]
    width = math.gcd(cols, 2048)
    count = cols // width

    def step_tile(index, acc):
        tile = lax.dynamic_slice_in_dim(columns, index * width, width, 1)
        part_sum = jnp.dot(
            tile[dims:],
            kernel(tile[:dims], rows_x),
            precision=lax.Precision.HIGHEST,
            preferred_element_type=jnp.float32,
        )
        return acc + part_sum

    if count == 1:
        return step_tile(0, total)
    return lax.fori_loop(0, count, step_tile, total)


def sweep(total, item, visit):
    count = lax.axis_size("blk")
    current = item
    total = visit(total, current)
    for step in range(count - 1):
        current = from_behind(current, "blk", 1)
        total = visit(total, current)
    return total


def local(inputs, probes, lengths, noise, pivots):
    scaled = inputs / lengths[:, None]
    rows = scaled.shape[1]
    probe_count = probes.shape[0]
    position = lax.axis_index("blk") * lax.axis_size("grp") + lax.axis_index("grp")
    point_ids = position * rows + jnp.arange(rows, dtype=jnp.int32)
    onehot = (pivots[:, None] == point_ids[None, :]).astype(jnp.float32)
    local_pivots = jnp.dot(
        scaled, onehot.T, precision=lax.Precision.HIGHEST, preferred_element_type=jnp.float32
    )
    pivot_x = lax.psum(local_pivots, ("blk", "grp"))
    count = pivot_x.shape[1]
    inner = kernel(pivot_x, pivot_x) + noise[0] * jnp.eye(count, dtype=jnp.float32)
    lower = jnp.linalg.cholesky(inner)
    panel = lax.linalg.triangular_solve(lower, kernel(pivot_x, scaled), left_side=True, lower=True)
    combined = jnp.concatenate([scaled, probes], 0)
    total = jnp.zeros((probe_count, rows), jnp.float32)
    group_cols = lax.all_gather(combined, "grp", axis=1, tiled=True)

    def visit_block(acc, block):
        return apply_block(acc, scaled, block)

    total = sweep(total, group_cols, visit_block)
    product = total + noise[0] * probes
    return (panel, product)


def solution(mesh):
    in_specs = (P(None, ("blk", "grp")), P(None, ("blk", "grp")), P(), P(), P())
    out_specs = (P(None, ("blk", "grp")), P(None, ("blk", "grp")))
    return jax.shard_map(local, mesh=mesh, in_specs=in_specs, out_specs=out_specs, check_vma=False)
```

profile of v0, /device:TPU:0, one launch (start us, length us, event | category | flops | bytes accessed | tf_op | source)
XLA Modules:
  0.0 97.0 jit_solution(18121176042185370040)
XLA Ops:
  0.6 0.0 copy-start
  0.6 0.8 multiply_reduce_fusion.2
  1.4 0.0 copy-done
  1.4 23.6 %all_gather.3 = f32[24,2048]{1,0:T(8,128)S(1)} all-gather(f32[24,128]{1,0:T(8,128)S(1)} %pad_maximum_fusion), channel_id=1, replica_groups=mesh['blk'=2,'grp'=16] {'grp'}, dimensions={1}, use_global_device_ids=true | all-gather | bytes 208896 | tf_op jit(solution)/shard_map/all_gather | solution.py:72
  25.0 1.5 %collective-permute-start = (f32[24,2048]{1,0:T(8,128)S(1)}, f32[24,2048]{1,0:T(8,128)S(1)}, u32[]{:S(2)}, u32[]{:S(2)}) collective-permute-start(f32[24,2048]{1,0:T(8,128)S(1)} %all_gather.3), channel_id=1, source_target_pairs={{0,16},{16,0},{1,17},{17,1},{2,18},{18,2},{3,19},{19,3},{4,20},{20... | collective-permute-start | bytes 589832 | tf_op jit(solution)/shard_map/ppermute | solution.py:12
  26.6 0.0 copy-start.1
  26.6 0.6 copy-done.1
  27.2 0.2 fusion.50
  27.4 37.2 %psum.7 = f32[8,128]{1,0:T(8,128)S(1)} all-reduce(f32[8,128]{1,0:T(8,128)S(1)} %fusion.50), channel_id=1, replica_groups=mesh['blk'=2,'grp'=16] {'blk','grp'}, use_global_device_ids=true, to_apply=%region_0.0 | all-reduce | flops 1024 | bytes 8192 | tf_op jit(solution)/shard_map/psum | solution.py:65
  64.6 0.3 broadcast_add_fusion
  64.9 0.3 fusion.4
  65.2 2.1 %fusion.3 = f32[2048,128]{1,0:T(8,128)S(1)} fusion(f32[8,128]{1,0:T(8,128)S(1)} %get-tuple-element.3, f32[128]{0:T(128)S(1)} %get-tuple-element.2, f32[2048]{0:T(1024)S(1)} %multiply_reduce_fusion.1, f32[24,2048]{1,0:T(8,128)S(1)} %all_gather.3), kind=kOutput, calls=%fused_computation.5 | convolution fusion | flops 26476544 | bytes 1126912 | tf_op jit(solution)/shard_map/dot_general | solution.py:16
  67.4 0.8 fusion.18
  68.9 0.1 copy.10
  69.0 0.1 copy.8
  69.1 0.1 add_multiply_fusion
  69.2 11.7 %cholesky.16 = f32[128,128]{1,0:T(8,128)S(1)} custom-call(f32[128,128]{1,0:T(8,128)S(1)} %add_multiply_fusion), custom_call_target="Cholesky" | custom-call | tf_op jit(solution)/shard_map/jit(cholesky)/cholesky | solution.py:68
  80.9 0.6 compare_reduce_fusion
  81.6 0.7 fusion.36
  82.2 9.8 %custom-call.6 = f32[1,128,128]{1,2,0:T(8,128)S(1)} custom-call(f32[1,128,128]{2,1,0:T(8,128)S(1)} %fusion.36), custom_call_target="InvertDiagBlocksLowerTriangular" | custom-call | tf_op jit(solution)/shard_map/triangular_solve | solution.py:69
  92.1 0.1 copy.12
  92.2 0.9 fusion.37
  93.1 0.0 collective-permute-done
  93.1 1.8 %convolution_multiply_fusion = f32[2048,128]{1,0:T(8,128)S(1)} fusion(f32[8,128]{1,0:T(8,128)S(1)} %get-tuple-element.3, f32[24,2048]{1,0:T(8,128)S(1)} %collective-permute-done), kind=kOutput, calls=%fused_computation | convolution fusion | flops 25427968 | bytes 1118208 | tf_op jit(solution)/shard_map/dot_general | solution.py:16
  94.9 2.1 %fusion.5 = f32[16,128]{1,0:T(8,128)} fusion(f32[16,128]{1,0:T(8,128)S(1)} %fusion.18, f32[2048,128]{1,0:T(8,128)S(1)} %convolution_multiply_fusion, f32[2048]{0:T(1024)S(1)} %multiply_reduce_fusion, f32[128]{0:T(128)S(1)} %get-tuple-element.2, f32[24,2048]{1,0:T(8,128)S(1)} %collective-permute-done, f32[16,128]{1,0:T(8,128)S(1)} %copy-done, f32[]{:T(128)} %bitcast.18), kind=kOutput, calls=%fused_computation.10 | convolution fusion | flops 52959232 | bytes 1212932 | tf_op jit(solution)/shard_map/dot_general | solution.py:32
  (6 shorter events, 0.1 us)
Async XLA Ops:
  0.6 0.8 copy-start
  25.0 68.1 %collective-permute-start = (f32[24,2048]{1,0:T(8,128)S(1)}, f32[24,2048]{1,0:T(8,128)S(1)}, u32[]{:S(2)}, u32[]{:S(2)}) collective-permute-start(f32[24,2048]{1,0:T(8,128)S(1)} %all_gather.3), channel_id=1, source_target_pairs={{0,16},{16,0},{1,17},{17,1},{2,18},{18,2},{3,19},{19,3},{4,20},{20... | collective-permute-start | bytes 589832 | tf_op jit(solution)/shard_map/ppermute | solution.py:12
  26.6 0.7 copy-start.1
where the time goes:
time: 97.8 us; the launch traced here: 97 us
  blocking collectives  60.8 us (62%)
  other arithmetic  23.8 us (24%)
  matrix products  8.55 us (9%)
  starting transfers between devices  1.52 us (2%)
  between operations  1.42 us (1%)
    psum x1, blocking collectives, local(): pivot_x = lax.psum(local_pivots, ('blk', 'grp'))  37.2 us
    all_gather x1, blocking collectives, local(): group_cols = lax.all_gather(combined, 'grp', axis=1, tiled=True)  23.6 us
    another operation x3, other arithmetic, local(): lower = jnp.linalg.cholesky(inner)  12.4 us
    another operation x2, other arithmetic, local(): lax.linalg.triangular_solve(lower, kernel(pivot_x, scaled), left_side=Tru...  10.5 us
    dot_general x4, matrix products, kernel(): jnp.dot(left.T, right, precision=lax.Precision.HIGHEST, preferred_element...  4.54 us
    dot_general x2, matrix products, step_tile(): jnp.dot(tile[dims:], kernel(tile[:dims], rows_x), precision=lax.Precision...  2.9 us
  transfers between devices with their start and end apart: 1, of which 0 were waited for; matrix products, arithmetic and copies ran while one was open for 29% of the time, Pallas kernels for 0%

commit v1 on v0

v1 whole, which is shorter than its diff:
```python
import math

import jax
import jax.numpy as jnp
from jax import lax
from jax.experimental import pallas as pl
from jax.experimental.pallas import tpu as pltpu
from jax.sharding import PartitionSpec as P

F32 = jnp.float32
BF16 = jnp.bfloat16
LN2 = math.log(2.0)
SCALE = math.sqrt(5.0) / LN2
BLOCK = 16
CHUNK = 4
UNROLL = 32


def exchange_masks(groups, members):
    low = members.bit_length() - 1
    bits = [1 << bit for bit in range(low - 1, 1, -1)]
    bits += [1 << (low + bit) for bit in range(groups.bit_length() - 2, -1, -1)]
    bits += [2] if members > 2 else []
    return [bit | 1 for bit in bits] + [1]


def split3(value):
    high = value.astype(BF16).astype(F32)
    rest = value - high
    middle = rest.astype(BF16).astype(F32)
    return high, middle, rest - middle


def norm_tile(x, first):
    high, middle, low = split3(jnp.sum(x * x, axis=0, keepdims=True))
    row = lax.broadcasted_iota(jnp.int32, x.shape, 0)
    if not first:
        row = jnp.where(row < 3, row + 3, row - 3)
    tile = jnp.where(row < 6, 1.0, 0.0)
    tile = jnp.where(row == 0, high, tile)
    tile = jnp.where(row == 1, middle, tile)
    return jnp.where(row == 2, low, tile)


def left_stack(x):
    high, middle, low = split3(x)
    return jnp.concatenate(
        [high, high, high, middle, middle, low, norm_tile(x, True), jnp.zeros_like(x)], 0
    )


def right_stack(x):
    high, middle, low = split3(-2.0 * x)
    return jnp.concatenate(
        [high, middle, low, high, middle, high, norm_tile(x, False), jnp.zeros_like(x)], 0
    ).astype(BF16)


def matern(square):
    square = jnp.maximum(square, 1e-30)
    radius = square * lax.rsqrt(square)
    return (1.0 + LN2 * radius + (LN2 * LN2 / 3.0) * square) * jnp.exp2(-radius)


def rows_of(value, row):
    return jnp.broadcast_to(value[row : row + 1, :], value.shape)


def eliminate(a, b, panel_ref, step):
    tiles = BLOCK // 8
    base = step * BLOCK
    sub = lax.broadcasted_iota(jnp.int32, (8, 128), 0)
    ra = [a[8 * t : 8 * t + 8] for t in range(tiles)]
    rb = [b[8 * t : 8 * t + 8] for t in range(tiles)]
    cols = [
        [jnp.broadcast_to(ra[t][:, base + m : base + m + 1], (8, 128)) for t in range(tiles)]
        for m in range(BLOCK)
    ]
    out = [jnp.zeros((8, 128), F32) for t in range(tiles)]
    for j in range(BLOCK):
        v, s = divmod(j, 8)
        pivot = rows_of(cols[j][v], s)
        inverse = 1.0 / pivot
        out[v] = jnp.where(sub == s, rb[v] * lax.rsqrt(pivot), out[v])
        coef = list(cols[j])
        coef[v] = coef[v] - jnp.where(sub == s, 1.0, 0.0)
        row_a = rows_of(ra[v], s) * inverse
        row_b = rows_of(rb[v], s) * inverse
        for t in range(tiles):
            ra[t] = ra[t] - coef[t] * row_a
            rb[t] = rb[t] - coef[t] * row_b
        for m in range(j + 1, BLOCK):
            entry = rows_of(cols[m][v], s) * inverse
            for t in range(tiles):
                cols[m][t] = cols[m][t] - coef[t] * entry
    for t in range(tiles):
        panel_ref[base + 8 * t : base + 8 * t + 8, :] = out[t]
    if base + BLOCK == panel_ref.shape[0]:
        return None, None
    solved = jnp.concatenate(
        [jnp.concatenate(ra, 0), jnp.concatenate(rb, 0)], 1
    )
    w_high, w_middle, w_low = split3(solved)
    right = jnp.concatenate([w_high, w_middle, w_low, w_high, w_middle, w_high], 0).astype(BF16)
    l_high, l_middle, l_low = split3(a[BLOCK:, base : base + BLOCK])
    left = jnp.concatenate([l_high, l_high, l_high, l_middle, l_middle, l_low], 1).astype(BF16)
    change = jnp.dot(left, right, preferred_element_type=F32)
    return a[BLOCK:] - change[:, :128], b[BLOCK:] - change[:, 128:]


def make_body(masks, count, members):
    half = count // 2

    def owner(index):
        mask = 0
        for bit, value in enumerate(masks):
            mask = mask ^ (((index >> bit) & 1) * value)
        return mask

    def body(noise_ref, pivots_ref, own_ref, here_ref, there_ref, panel_ref, product_ref):
        me = lax.axis_index("blk") * members + lax.axis_index("grp")
        noise = noise_ref[0]
        rows = own_ref.shape[1]
        dims = own_ref.shape[0] - product_ref.shape[0]
        pivots = pivots_ref[...]
        points = lax.broadcasted_iota(jnp.int32, (rows, pivots.shape[1]), 0)

        def pick(total, ref, index, first):
            device = me ^ owner(index + first)
            hot = (points == pivots - device * rows).astype(F32).astype(BF16)
            parts = jnp.concatenate(split3(ref[index, :dims, :]), 0).astype(BF16)
            return total + jnp.dot(parts, hot, preferred_element_type=F32)

        picked = jnp.zeros((3 * dims, pivots.shape[1]), F32)
        for ref, first in ((here_ref, 0), (there_ref, half)):
            if half <= UNROLL:
                for index in range(half):
                    picked = pick(picked, ref, index, first)
            else:
                picked = lax.fori_loop(
                    0, half, lambda i, t, r=ref, f=first: pick(t, r, i, f), picked
                )
        pivot_x = picked[:dims] + picked[dims : 2 * dims] + picked[2 * dims :]
        own = own_ref[:dims, :]
        left_pivot = left_stack(pivot_x).T.astype(BF16)
        both = jnp.concatenate([right_stack(pivot_x), right_stack(own)], 1)
        values = matern(jnp.dot(left_pivot, both, preferred_element_type=F32))
        size = pivots.shape[1]
        eye = lax.broadcasted_iota(jnp.int32, (size, size), 0) == lax.broadcasted_iota(
            jnp.int32, (size, size), 1
        )
        a = values[:, :size] + jnp.where(eye, noise, 0.0)
        b = values[:, size:]
        left_own = left_stack(own).T.astype(BF16)
        nt = (((1,), (1,)), ((), ()))

        def add_chunk(carry, ref, index):
            wide, narrow = carry
            blocks = [ref[index + i] for i in range(CHUNK)]
            right = jnp.concatenate([right_stack(block[:dims]) for block in blocks], 1)
            probe = jnp.concatenate([block[dims:] for block in blocks], 1)
            probe_high = probe.astype(BF16)
            probe_low = (probe - probe_high.astype(F32)).astype(BF16)
            value = matern(jnp.dot(left_own, right, preferred_element_type=F32))
            value_high = value.astype(BF16)
            value_low = (value - value_high.astype(F32)).astype(BF16)
            wide = wide + lax.dot_general(
                value_high,
                jnp.concatenate([probe_high, probe_low], 0),
                nt,
                preferred_element_type=F32,
            )
            narrow = narrow + lax.dot_general(
                value_low, probe_high, nt, preferred_element_type=F32
            )
            return wide, narrow

        vectors = product_ref.shape[0]
        carry = (jnp.zeros((rows, 2 * vectors), F32), jnp.zeros((rows, vectors), F32))
        chunks = [(ref, i * CHUNK) for ref in (here_ref, there_ref) for i in range(half // CHUNK)]
        unrolled = half <= UNROLL
        steps = size // BLOCK
        for step in range(steps):
            a, b = eliminate(a, b, panel_ref, step)
            if unrolled:
                for ref, index in chunks[step::steps]:
                    carry = add_chunk(carry, ref, index)
        if not unrolled:
            for ref in (here_ref, there_ref):
                carry = lax.fori_loop(
                    0, half // CHUNK, lambda i, c, r=ref: add_chunk(c, r, i * CHUNK), carry
                )
        wide, narrow = carry
        total = wide[:, :vectors] + wide[:, vectors:] + narrow
        product_ref[...] = total.T + noise * own_ref[dims:, :]

    return body


def solution(mesh):
    groups, members = mesh.shape["blk"], mesh.shape["grp"]
    count = groups * members
    masks = exchange_masks(groups, members)

    def swap(value, mask):
        return lax.ppermute(value, ("blk", "grp"), [(i, i ^ mask) for i in range(count)])

    def local(inputs, probes, lengths, noise, pivots):
        rows = inputs.shape[1]
        own = jnp.concatenate([inputs * (SCALE / lengths)[:, None], probes], 0)
        here = own[None]
        for mask in masks[:-1]:
            here = jnp.concatenate([here, swap(here, mask)], 0)
        there = swap(here, masks[-1])
        vmem = pl.BlockSpec(memory_space=pltpu.VMEM)
        return pl.pallas_call(
            make_body(masks, count, members),
            out_shape=(
                jax.ShapeDtypeStruct((pivots.shape[0], rows), F32),
                jax.ShapeDtypeStruct(probes.shape, F32),
            ),
            in_specs=[pl.BlockSpec(memory_space=pltpu.SMEM)] + [vmem] * 4,
            out_specs=(vmem, vmem),
            compiler_params=pltpu.CompilerParams(vmem_limit_bytes=32 * 1024 * 1024),
        )(noise, pivots[None, :], own, here, there)

    in_specs = (P(None, ("blk", "grp")), P(None, ("blk", "grp")), P(), P(), P())
    out_specs = (P(None, ("blk", "grp")), P(None, ("blk", "grp")))
    return jax.shard_map(local, mesh=mesh, in_specs=in_specs, out_specs=out_specs, check_vma=False)
```

time: 97.8 us -> 26.4 us (0.27)
  blocking collectives: 60.8 us -> 0 us
  other arithmetic: 23.8 us -> 1.45 us
  matrix products: 8.55 us -> 0 us
  waiting for transfers between devices: 0.01 us -> 8.14 us
  starting transfers between devices: 1.52 us -> 9.33 us
  Pallas kernels: 0 us -> 5.26 us
    psum x1 -> x0, blocking collectives: 37.2 us -> none  [local(): pivot_x = lax.psum(local_pivots, ('blk', 'grp'))]
    all_gather x1 -> x0, blocking collectives: 23.6 us -> none  [local(): group_cols = lax.all_gather(combined, 'grp', axis=1, tiled=True)]
    another operation x5 -> x0, other arithmetic: 22.9 us -> none  [the longest x3 12.4 us: local(): lower = jnp.linalg.cholesky(inner)]
    ppermute x1 -> x5, waiting for transfers between devices: 0.01 us -> 8.14 us  [swap(): lax.ppermute(value, ('blk', 'grp'), [(i, i ^ mask) for i in range(count)])]
    ppermute x1 -> x5, starting transfers between devices: 1.52 us -> 9.33 us  [swap(): lax.ppermute(value, ('blk', 'grp'), [(i, i ^ mask) for i in range(count)])]
    dot_general x7 -> x0, matrix products: 7.63 us -> none  [the longest x4 4.54 us: kernel(): jnp.dot(left.T, right, precision=lax.Precision.HIGHEST, preferred_element...]
    pallas_call x0 -> x1, Pallas kernels: none -> 5.26 us  [local(): pl.pallas_call(make_body(masks, count, members), out_shape=(jax.ShapeDtyp...]
  transfers between devices with their start and end apart: 1 -> 5, of which waited for: 0 -> 5; matrix products, arithmetic and copies ran while one was open for 29% -> 0% of each run, Pallas kernels for 0% -> 0%
where the time goes in v1:
time: 26.4 us; the launch traced here: 26.2 us
  starting transfers between devices  9.33 us (35%)
  waiting for transfers between devices  8.14 us (31%)
  Pallas kernels  5.26 us (20%)
  other arithmetic  1.45 us (5%)
  between operations  1.3 us (5%)
  local copies, waits for them, and re-layouts  0.68 us (3%)
    ppermute x5, starting transfers between devices, swap(): lax.ppermute(value, ('blk', 'grp'), [(i, i ^ mask) for i in range(count)])  9.33 us
    ppermute x5, waiting for transfers between devices, swap(): lax.ppermute(value, ('blk', 'grp'), [(i, i ^ mask) for i in range(count)])  8.14 us
    pallas_call x1, Pallas kernels, local(): pl.pallas_call(make_body(masks, count, members), out_shape=(jax.ShapeDtyp...  5.26 us
    mul x1, other arithmetic, local(): own = jnp.concatenate([inputs * (SCALE / lengths)[:, None], probes], 0)  0.76 us
    unnamed x7, local copies, waits for them, and re-layouts  0.67 us
    div x1, other arithmetic, local(): own = jnp.concatenate([inputs * (SCALE / lengths)[:, None], probes], 0)  0.66 us
  transfers between devices with their start and end apart: 5, of which 5 were waited for; matrix products, arithmetic and copies ran while one was open for 0% of the time, Pallas kernels for 0%

profile of v1, /device:TPU:0, one launch (start us, length us, event | category | flops | bytes accessed | tf_op | source)
XLA Modules:
  0.0 26.2 jit_solution(17718700729134028187)
XLA Ops:
  0.6 0.0 copy-start.1
  0.6 0.7 %broadcast_divide_fusion = f32[8]{0:T(128)S(1)} fusion(f32[8]{0:T(128)} %param.7), kind=kLoop, calls=%fused_computation.10 | loop fusion | flops 8 | bytes 64 | tf_op jit(solution)/shard_map/div | solution.py:210
  1.3 0.8 %broadcast_multiply_fusion = f32[8,128]{1,0:T(8,128)S(1)} fusion(f32[8,128]{1,0:T(8,128)} %param.5, f32[8]{0:T(128)S(1)} %broadcast_divide_fusion), kind=kLoop, calls=%fused_computation.9 | loop fusion | flops 1024 | bytes 8224 | tf_op jit(solution)/shard_map/mul | solution.py:210
  2.1 0.0 copy-done.1
  2.1 3.5 %collective-permute-start = (f32[1,24,128]{2,1,0:T(8,128)S(1)}, f32[1,24,128]{2,1,0:T(8,128)S(1)}, u32[]{:S(2)}, u32[]{:S(2)}) collective-permute-start(f32[1,24,128]{2,1,0:T(8,128)S(1)} %get-tuple-element.2), channel_id=1, source_target_pairs={{0,9},{1,8},{2,11},{3,10},{4,13},{5,12},{6,15},{7,14},{8,1},{9,0},... | collective-permute-start | bytes 36872 | tf_op jit(solution)/shard_map/ppermute | solution.py:206
  5.6 1.4 %collective-permute-done = f32[1,24,128]{2,1,0:T(8,128)S(1)} collective-permute-done((f32[1,24,128]{2,1,0:T(8,128)S(1)}, f32[1,24,128]{2,1,0:T(8,128)S(1)}, u32[]{:S(2)}, u32[]{:S(2)}) %collective-permute-start) | collective-permute-done | bytes 12320 | tf_op jit(solution)/shard_map/ppermute | solution.py:206
  7.0 1.9 %collective-permute-start.1 = (f32[2,24,128]{2,1,0:T(8,128)S(1)}, f32[2,24,128]{2,1,0:T(8,128)S(1)}, u32[]{:S(2)}, u32[]{:S(2)}) collective-permute-start(f32[2,24,128]{2,1,0:T(8,128)S(1)} %pad_maximum_fusion.2), channel_id=1, source_target_pairs={{0,5},{1,4},{2,7},{3,6},{4,1},{5,0},{6,3},{7,2},{8,13},{9,12},{10,... | collective-permute-start | bytes 73736 | tf_op jit(solution)/shard_map/ppermute | solution.py:206
  8.9 1.5 %collective-permute-done.1 = f32[2,24,128]{2,1,0:T(8,128)S(1)} collective-permute-done((f32[2,24,128]{2,1,0:T(8,128)S(1)}, f32[2,24,128]{2,1,0:T(8,128)S(1)}, u32[]{:S(2)}, u32[]{:S(2)}) %collective-permute-start.1) | collective-permute-done | bytes 24608 | tf_op jit(solution)/shard_map/ppermute | solution.py:206
  10.4 1.7 %collective-permute-start.2 = (f32[4,24,128]{2,1,0:T(8,128)S(1)}, f32[4,24,128]{2,1,0:T(8,128)S(1)}, u32[]{:S(2)}, u32[]{:S(2)}) collective-permute-start(f32[4,24,128]{2,1,0:T(8,128)S(1)} %pad_maximum_fusion.1), channel_id=1, source_target_pairs={{0,17},{1,16},{2,19},{3,18},{4,21},{5,20},{6,23},{7,22},{8,25},{9,... | collective-permute-start | bytes 147464 | tf_op jit(solution)/shard_map/ppermute | solution.py:206
  12.1 1.8 %collective-permute-done.2 = f32[4,24,128]{2,1,0:T(8,128)S(1)} collective-permute-done((f32[4,24,128]{2,1,0:T(8,128)S(1)}, f32[4,24,128]{2,1,0:T(8,128)S(1)}, u32[]{:S(2)}, u32[]{:S(2)}) %collective-permute-start.2) | collective-permute-done | bytes 49184 | tf_op jit(solution)/shard_map/ppermute | solution.py:206
  13.9 1.9 %collective-permute-start.3 = (f32[8,24,128]{2,1,0:T(8,128)S(1)}, f32[8,24,128]{2,1,0:T(8,128)S(1)}, u32[]{:S(2)}, u32[]{:S(2)}) collective-permute-start(f32[8,24,128]{2,1,0:T(8,128)S(1)} %pad_maximum_fusion), channel_id=1, source_target_pairs={{0,3},{1,2},{2,1},{3,0},{4,7},{5,6},{6,5},{7,4},{8,11},{9,10},{10,... | collective-permute-start | bytes 294920 | tf_op jit(solution)/shard_map/ppermute | solution.py:206
  15.9 2.9 %collective-permute-done.3 = f32[8,24,128]{2,1,0:T(8,128)S(1)} collective-permute-done((f32[8,24,128]{2,1,0:T(8,128)S(1)}, f32[8,24,128]{2,1,0:T(8,128)S(1)}, u32[]{:S(2)}, u32[]{:S(2)}) %collective-permute-start.3) | collective-permute-done | bytes 98336 | tf_op jit(solution)/shard_map/ppermute | solution.py:206
  18.7 0.4 %collective-permute-start.4 = (f32[16,24,128]{2,1,0:T(8,128)S(1)}, f32[16,24,128]{2,1,0:T(8,128)S(1)}, u32[]{:S(2)}, u32[]{:S(2)}) collective-permute-start(f32[16,24,128]{2,1,0:T(8,128)S(1)} %constant_dynamic-update-slice_fusion.here_ref), channel_id=1, source_target_pairs={{0,1},{1,0},{2,3},{3,2},{4,5},{5,4},{6,7},{7,6},{8,9},{9,8},{10,11... | collective-permute-start | bytes 589832 | tf_op jit(solution)/shard_map/ppermute | solution.py:206
  19.7 0.5 %collective-permute-done.4.there_ref = f32[16,24,128]{2,1,0:T(8,128)S(1)} collective-permute-done((f32[16,24,128]{2,1,0:T(8,128)S(1)}, f32[16,24,128]{2,1,0:T(8,128)S(1)}, u32[]{:S(2)}, u32[]{:S(2)}) %collective-permute-start.4) | collective-permute-done | bytes 196640 | tf_op jit(solution)/shard_map/ppermute | solution.py:206
  20.2 0.0 copy-start
  20.3 0.7 %copy-done = s32[128]{0:T(128)S(1)} copy-done((s32[128]{0:T(128)S(1)}, s32[128]{0:T(128)}, u32[]{:S(2)}) %copy-start) | copy-done | bytes 536
  20.9 5.3 %shard_map.68 = (f32[128,128]{1,0:T(8,128)}, f32[16,128]{1,0:T(8,128)}) custom-call(f32[1]{0:T(128)S(6)} %copy.11.noise_ref, s32[1,128]{1,0:T(1,128)S(1)} %bitcast.4, f32[24,128]{1,0:T(8,128)S(1)} %get-tuple-element.3.own_ref, f32[16,24,128]{2,1,0:T(8,128)S(1)} %constant_dynamic-update-slice_fusion.here_ref, f32[16,24,128]{2,1,0:T(8,128)S(1)} %collective-permute-done.4.there_ref), custom_call_target="tpu_custom_call" | custom-call | tf_op jit(solution)/shard_map/pallas_call | solution.py:216
  (9 shorter events, 0.0 us)
Async XLA Ops:
  0.6 1.4 %copy-start.1 = (f32[16,128]{1,0:T(8,128)S(1)}, f32[16,128]{1,0:T(8,128)}, u32[]{:S(2)}) copy-start(f32[16,128]{1,0:T(8,128)} %param.6) | copy-start | bytes 24580
  2.1 4.9 %collective-permute-start = (f32[1,24,128]{2,1,0:T(8,128)S(1)}, f32[1,24,128]{2,1,0:T(8,128)S(1)}, u32[]{:S(2)}, u32[]{:S(2)}) collective-permute-start(f32[1,24,128]{2,1,0:T(8,128)S(1)} %get-tuple-element.2), channel_id=1, source_target_pairs={{0,9},{1,8},{2,11},{3,10},{4,13},{5,12},{6,15},{7,14},{8,1},{9,0},... | collective-permute-start | bytes 36872 | tf_op jit(solution)/shard_map/ppermute | solution.py:206
  7.0 3.4 %collective-permute-start.1 = (f32[2,24,128]{2,1,0:T(8,128)S(1)}, f32[2,24,128]{2,1,0:T(8,128)S(1)}, u32[]{:S(2)}, u32[]{:S(2)}) collective-permute-start(f32[2,24,128]{2,1,0:T(8,128)S(1)} %pad_maximum_fusion.2), channel_id=1, source_target_pairs={{0,5},{1,4},{2,7},{3,6},{4,1},{5,0},{6,3},{7,2},{8,13},{9,12},{10,... | collective-permute-start | bytes 73736 | tf_op jit(solution)/shard_map/ppermute | solution.py:206
  10.4 3.5 %collective-permute-start.2 = (f32[4,24,128]{2,1,0:T(8,128)S(1)}, f32[4,24,128]{2,1,0:T(8,128)S(1)}, u32[]{:S(2)}, u32[]{:S(2)}) collective-permute-start(f32[4,24,128]{2,1,0:T(8,128)S(1)} %pad_maximum_fusion.1), channel_id=1, source_target_pairs={{0,17},{1,16},{2,19},{3,18},{4,21},{5,20},{6,23},{7,22},{8,25},{9,... | collective-permute-start | bytes 147464 | tf_op jit(solution)/shard_map/ppermute | solution.py:206
  13.9 4.8 %collective-permute-start.3 = (f32[8,24,128]{2,1,0:T(8,128)S(1)}, f32[8,24,128]{2,1,0:T(8,128)S(1)}, u32[]{:S(2)}, u32[]{:S(2)}) collective-permute-start(f32[8,24,128]{2,1,0:T(8,128)S(1)} %pad_maximum_fusion), channel_id=1, source_target_pairs={{0,3},{1,2},{2,1},{3,0},{4,7},{5,6},{6,5},{7,4},{8,11},{9,10},{10,... | collective-permute-start | bytes 294920 | tf_op jit(solution)/shard_map/ppermute | solution.py:206
  18.7 1.5 %collective-permute-start.4 = (f32[16,24,128]{2,1,0:T(8,128)S(1)}, f32[16,24,128]{2,1,0:T(8,128)S(1)}, u32[]{:S(2)}, u32[]{:S(2)}) collective-permute-start(f32[16,24,128]{2,1,0:T(8,128)S(1)} %constant_dynamic-update-slice_fusion.here_ref), channel_id=1, source_target_pairs={{0,1},{1,0},{2,3},{3,2},{4,5},{5,4},{6,7},{7,6},{8,9},{9,8},{10,11... | collective-permute-start | bytes 589832 | tf_op jit(solution)/shard_map/ppermute | solution.py:206
  20.2 0.7 %copy-start = (s32[128]{0:T(128)S(1)}, s32[128]{0:T(128)}, u32[]{:S(2)}) copy-start(s32[128]{0:T(128)} %param.9) | copy-start | bytes 1540

commit v2 on v1

--- a/solution.py
+++ b/solution.py
@@ -21,7 +21,16 @@
     bits = [1 << bit for bit in range(low - 1, 1, -1)]
     bits += [1 << (low + bit) for bit in range(groups.bit_length() - 2, -1, -1)]
     bits += [2] if members > 2 else []
-    return [bit | 1 for bit in bits] + [1]
+    even = [bit | 1 for bit in bits]
+    odd = even[:-2] + even[:-3:-1]
+    return even + [1], odd + [1]
+
+
+def parity(index, count):
+    bits = 0
+    for bit in range(count.bit_length() - 1):
+        bits = bits ^ (index >> bit)
+    return bits & 1
 
 
 def split3(value):
@@ -111,37 +120,39 @@
 def make_body(masks, count, members):
     half = count // 2
 
-    def owner(index):
-        mask = 0
-        for bit, value in enumerate(masks):
-            mask = mask ^ (((index >> bit) & 1) * value)
-        return mask
-
-    def body(noise_ref, pivots_ref, own_ref, here_ref, there_ref, panel_ref, product_ref):
+    def owner(me, kind, index):
+        for bit, (even, odd) in enumerate(zip(masks[0][:-1], masks[1][:-1])):
+            me = me ^ (((index >> bit) & 1) * jnp.where(kind == 0, even, odd))
+        return me
+
+    def body(side_ref, own_ref, here_ref, there_ref, panel_ref, product_ref):
         me = lax.axis_index("blk") * members + lax.axis_index("grp")
-        noise = noise_ref[0]
         rows = own_ref.shape[1]
         dims = own_ref.shape[0] - product_ref.shape[0]
-        pivots = pivots_ref[...]
+        scale = side_ref[:dims, :]
+        noise = side_ref[dims : dims + 1, :]
+        pivots = side_ref[dims + 1 : dims + 2, :].astype(jnp.int32)
         points = lax.broadcasted_iota(jnp.int32, (rows, pivots.shape[1]), 0)
 
-        def pick(total, ref, index, first):
-            device = me ^ owner(index + first)
+        kind = parity(me, count)
+
+        def pick(total, ref, index, other):
+            device = owner(me ^ other, kind ^ other, index)
             hot = (points == pivots - device * rows).astype(F32).astype(BF16)
             parts = jnp.concatenate(split3(ref[index, :dims, :]), 0).astype(BF16)
             return total + jnp.dot(parts, hot, preferred_element_type=F32)
 
         picked = jnp.zeros((3 * dims, pivots.shape[1]), F32)
-        for ref, first in ((here_ref, 0), (there_ref, half)):
+        for ref, other in ((here_ref, 0), (there_ref, 1)):
             if half <= UNROLL:
                 for index in range(half):
-                    picked = pick(picked, ref, index, first)
+                    picked = pick(picked, ref, index, other)
             else:
                 picked = lax.fori_loop(
-                    0, half, lambda i, t, r=ref, f=first: pick(t, r, i, f), picked
+                    0, half, lambda i, t, r=ref, o=other: pick(t, r, i, o), picked
                 )
-        pivot_x = picked[:dims] + picked[dims : 2 * dims] + picked[2 * dims :]
-        own = own_ref[:dims, :]
+        pivot_x = (picked[:dims] + picked[dims : 2 * dims] + picked[2 * dims :]) * scale
+        own = own_ref[:dims, :] * scale
         left_pivot = left_stack(pivot_x).T.astype(BF16)
         both = jnp.concatenate([right_stack(pivot_x), right_stack(own)], 1)
         values = matern(jnp.dot(left_pivot, both, preferred_element_type=F32))
@@ -157,7 +168,7 @@
         def add_chunk(carry, ref, index):
             wide, narrow = carry
             blocks = [ref[index + i] for i in range(CHUNK)]
-            right = jnp.concatenate([right_stack(block[:dims]) for block in blocks], 1)
+            right = jnp.concatenate([right_stack(block[:dims] * scale) for block in blocks], 1)
             probe = jnp.concatenate([block[dims:] for block in blocks], 1)
             probe_high = probe.astype(BF16)
             probe_low = (probe - probe_high.astype(F32)).astype(BF16)
@@ -202,16 +213,26 @@
     count = groups * members
     masks = exchange_masks(groups, members)
 
-    def swap(value, mask):
-        return lax.ppermute(value, ("blk", "grp"), [(i, i ^ mask) for i in range(count)])
+    def swap(value, step):
+        pairs = [(i, i ^ masks[parity(i, count)][step]) for i in range(count)]
+        return lax.ppermute(value, ("blk", "grp"), pairs)
 
     def local(inputs, probes, lengths, noise, pivots):
         rows = inputs.shape[1]
-        own = jnp.concatenate([inputs * (SCALE / lengths)[:, None], probes], 0)
+        own = jnp.concatenate([inputs, probes], 0)
         here = own[None]
-        for mask in masks[:-1]:
-            here = jnp.concatenate([here, swap(here, mask)], 0)
-        there = swap(here, masks[-1])
+        for step in range(len(masks[0]) - 1):
+            if step == 1:
+                side = jnp.concatenate(
+                    [
+                        jnp.broadcast_to((SCALE / lengths)[:, None], inputs.shape),
+                        jnp.broadcast_to(noise[:, None], (1, rows)),
+                        pivots.astype(F32)[None, :],
+                    ],
+                    0,
+                )
+            here = jnp.concatenate([here, swap(here, step)], 0)
+        there = swap(here, len(masks[0]) - 1)
         vmem = pl.BlockSpec(memory_space=pltpu.VMEM)
         return pl.pallas_call(
             make_body(masks, count, members),
@@ -219,10 +240,10 @@
                 jax.ShapeDtypeStruct((pivots.shape[0], rows), F32),
                 jax.ShapeDtypeStruct(probes.shape, F32),
             ),
-            in_specs=[pl.BlockSpec(memory_space=pltpu.SMEM)] + [vmem] * 4,
+            in_specs=[vmem] * 4,
             out_specs=(vmem, vmem),
             compiler_params=pltpu.CompilerParams(vmem_limit_bytes=32 * 1024 * 1024),
-        )(noise, pivots[None, :], own, here, there)
+        )(side, own, here, there)
 
     in_specs = (P(None, ("blk", "grp")), P(None, ("blk", "grp")), P(), P(), P())
     out_specs = (P(None, ("blk", "grp")), P(None, ("blk", "grp")))

time: 26.4 us -> 24.4 us (0.924)
  other arithmetic: 1.45 us -> 0.17 us
  waiting for transfers between devices: 8.14 us -> 7.37 us
    ppermute x5, waiting for transfers between devices: 8.14 us -> 7.37 us  [swap(): return lax.ppermute(value, ('blk', 'grp'), pairs)]
    mul x1 -> x0, other arithmetic: 0.76 us -> none  [local(): own = jnp.concatenate([inputs * (SCALE / lengths)[:, None], probes], 0)]
    div x1, other arithmetic: 0.66 us -> 0.01 us  [local(): SCALE / lengths]
    unnamed x7 -> x11, local copies, waits for them, and re-layouts: 0.67 us -> 0.72 us
  transfers between devices with their start and end apart: 5 -> 5, of which waited for: 5 -> 5; matrix products, arithmetic and copies ran while one was open for 0% -> 1% of each run, Pallas kernels for 0% -> 0%
where the time goes in v2:
time: 24.4 us; the launch traced here: 24.2 us
  starting transfers between devices  9.31 us (38%)
  waiting for transfers between devices  7.37 us (30%)
  Pallas kernels  5.27 us (22%)
  between operations  1.34 us (5%)
  local copies, waits for them, and re-layouts  0.73 us (3%)
    ppermute x5, starting transfers between devices, swap(): return lax.ppermute(value, ('blk', 'grp'), pairs)  9.31 us
    ppermute x5, waiting for transfers between devices, swap(): return lax.ppermute(value, ('blk', 'grp'), pairs)  7.37 us
    pallas_call x1, Pallas kernels, local(): pl.pallas_call(make_body(masks, count, members), out_shape=(jax.ShapeDtyp...  5.27 us
    unnamed x11, local copies, waits for them, and re-layouts  0.72 us
  transfers between devices with their start and end apart: 5, of which 5 were waited for; matrix products, arithmetic and copies ran while one was open for 1% of the time, Pallas kernels for 0%

profile of v2, /device:TPU:0, one launch (start us, length us, event | category | flops | bytes accessed | tf_op | source)
XLA Modules:
  0.0 24.2 jit_solution(4361989091871152338)
XLA Ops:
  0.6 0.0 copy-start
  0.6 0.7 %constant_dynamic-update-slice_fusion.1 = f32[24,128]{1,0:T(8,128)S(1)} fusion(f32[8,128]{1,0:T(8,128)} %param.5), kind=kLoop, calls=%fused_computation.4 | loop fusion | bytes 8192
  1.3 0.0 copy-done
  1.3 0.0 copy-start.1
  1.3 3.5 %collective-permute-start = (f32[1,24,128]{2,1,0:T(8,128)S(1)}, f32[1,24,128]{2,1,0:T(8,128)S(1)}, u32[]{:S(2)}, u32[]{:S(2)}) collective-permute-start(f32[1,24,128]{2,1,0:T(8,128)S(1)} %bitcast.5), channel_id=1, source_target_pairs={{0,9},{1,8},{2,11},{3,10},{4,13},{5,12},{6,15},{7,14},{8,1},{9,0},... | collective-permute-start | bytes 36872 | tf_op jit(solution)/shard_map/ppermute | solution.py:218
  4.8 0.0 copy-done.1
  4.8 0.0 copy-start.2
  5.5 0.0 copy-done.2
  5.5 0.1 pad_maximum_fusion.4
  5.6 0.6 %collective-permute-done = f32[1,24,128]{2,1,0:T(8,128)S(1)} collective-permute-done((f32[1,24,128]{2,1,0:T(8,128)S(1)}, f32[1,24,128]{2,1,0:T(8,128)S(1)}, u32[]{:S(2)}, u32[]{:S(2)}) %collective-permute-start) | collective-permute-done | bytes 12320 | tf_op jit(solution)/shard_map/ppermute | solution.py:218
  6.2 1.9 %collective-permute-start.1 = (f32[2,24,128]{2,1,0:T(8,128)S(1)}, f32[2,24,128]{2,1,0:T(8,128)S(1)}, u32[]{:S(2)}, u32[]{:S(2)}) collective-permute-start(f32[2,24,128]{2,1,0:T(8,128)S(1)} %pad_maximum_fusion.2), channel_id=1, source_target_pairs={{0,5},{1,4},{2,7},{3,6},{4,1},{5,0},{6,3},{7,2},{8,13},{9,12},{10,... | collective-permute-start | bytes 73736 | tf_op jit(solution)/shard_map/ppermute | solution.py:218
  8.1 1.5 %collective-permute-done.1 = f32[2,24,128]{2,1,0:T(8,128)S(1)} collective-permute-done((f32[2,24,128]{2,1,0:T(8,128)S(1)}, f32[2,24,128]{2,1,0:T(8,128)S(1)}, u32[]{:S(2)}, u32[]{:S(2)}) %collective-permute-start.1) | collective-permute-done | bytes 24608 | tf_op jit(solution)/shard_map/ppermute | solution.py:218
  9.6 1.7 %collective-permute-start.2 = (f32[4,24,128]{2,1,0:T(8,128)S(1)}, f32[4,24,128]{2,1,0:T(8,128)S(1)}, u32[]{:S(2)}, u32[]{:S(2)}) collective-permute-start(f32[4,24,128]{2,1,0:T(8,128)S(1)} %pad_maximum_fusion.1), channel_id=1, source_target_pairs={{0,17},{1,2},{2,1},{3,18},{4,7},{5,20},{6,23},{7,4},{8,11},{9,24},... | collective-permute-start | bytes 147464 | tf_op jit(solution)/shard_map/ppermute | solution.py:218
  11.3 1.8 %collective-permute-done.2 = f32[4,24,128]{2,1,0:T(8,128)S(1)} collective-permute-done((f32[4,24,128]{2,1,0:T(8,128)S(1)}, f32[4,24,128]{2,1,0:T(8,128)S(1)}, u32[]{:S(2)}, u32[]{:S(2)}) %collective-permute-start.2) | collective-permute-done | bytes 49184 | tf_op jit(solution)/shard_map/ppermute | solution.py:218
  13.2 1.7 %collective-permute-start.3 = (f32[8,24,128]{2,1,0:T(8,128)S(1)}, f32[8,24,128]{2,1,0:T(8,128)S(1)}, u32[]{:S(2)}, u32[]{:S(2)}) collective-permute-start(f32[8,24,128]{2,1,0:T(8,128)S(1)} %pad_maximum_fusion), channel_id=1, source_target_pairs={{0,3},{1,16},{2,19},{3,0},{4,21},{5,6},{6,5},{7,22},{8,25},{9,10},... | collective-permute-start | bytes 294920 | tf_op jit(solution)/shard_map/ppermute | solution.py:218
  14.9 2.4 %collective-permute-done.3 = f32[8,24,128]{2,1,0:T(8,128)S(1)} collective-permute-done((f32[8,24,128]{2,1,0:T(8,128)S(1)}, f32[8,24,128]{2,1,0:T(8,128)S(1)}, u32[]{:S(2)}, u32[]{:S(2)}) %collective-permute-start.3) | collective-permute-done | bytes 98336 | tf_op jit(solution)/shard_map/ppermute | solution.py:218
  17.3 0.6 %collective-permute-start.4 = (f32[16,24,128]{2,1,0:T(8,128)S(1)}, f32[16,24,128]{2,1,0:T(8,128)S(1)}, u32[]{:S(2)}, u32[]{:S(2)}) collective-permute-start(f32[16,24,128]{2,1,0:T(8,128)S(1)} %constant_dynamic-update-slice_fusion.2.here_ref), channel_id=1, source_target_pairs={{0,1},{1,0},{2,3},{3,2},{4,5},{5,4},{6,7},{7,6},{8,9},{9,8},{10,11... | collective-permute-start | bytes 589832 | tf_op jit(solution)/shard_map/ppermute | solution.py:218
  17.8 0.1 pad_maximum_fusion.3.side_ref
  17.9 1.0 %collective-permute-done.4.there_ref = f32[16,24,128]{2,1,0:T(8,128)S(1)} collective-permute-done((f32[16,24,128]{2,1,0:T(8,128)S(1)}, f32[16,24,128]{2,1,0:T(8,128)S(1)}, u32[]{:S(2)}, u32[]{:S(2)}) %collective-permute-start.4) | collective-permute-done | bytes 196640 | tf_op jit(solution)/shard_map/ppermute | solution.py:218
  18.9 5.3 %shard_map.68 = (f32[128,128]{1,0:T(8,128)}, f32[16,128]{1,0:T(8,128)}) custom-call(f32[10,128]{1,0:T(8,128)S(1)} %pad_maximum_fusion.3.side_ref, f32[24,128]{1,0:T(8,128)S(1)} %constant_dynamic-update-slice_fusion.own_ref, f32[16,24,128]{2,1,0:T(8,128)S(1)} %constant_dynamic-update-slice_fusion.2.here_ref, f32[16,24,128]{2,1,0:T(8,128)S(1)} %collective-permute-done.4.there_ref), custom_call_target="tpu_custom_call" | custom-call | tf_op jit(solution)/shard_map/pallas_call | solution.py:237
  (11 shorter events, 0.0 us)
Async XLA Ops:
  0.6 0.7 %copy-start = (f32[16,128]{1,0:T(8,128)S(1)}, f32[16,128]{1,0:T(8,128)}, u32[]{:S(2)}) copy-start(f32[16,128]{1,0:T(8,128)} %param.6) | copy-start | bytes 24580
  1.3 3.5 %copy-start.1 = (f32[8]{0:T(128)S(1)}, f32[8]{0:T(128)}, u32[]{:S(2)}) copy-start(f32[8]{0:T(128)} %param.7) | copy-start | bytes 100
  1.3 4.9 %collective-permute-start = (f32[1,24,128]{2,1,0:T(8,128)S(1)}, f32[1,24,128]{2,1,0:T(8,128)S(1)}, u32[]{:S(2)}, u32[]{:S(2)}) collective-permute-start(f32[1,24,128]{2,1,0:T(8,128)S(1)} %bitcast.5), channel_id=1, source_target_pairs={{0,9},{1,8},{2,11},{3,10},{4,13},{5,12},{6,15},{7,14},{8,1},{9,0},... | collective-permute-start | bytes 36872 | tf_op jit(solution)/shard_map/ppermute | solution.py:218
  4.8 0.7 %copy-start.2 = (s32[128]{0:T(128)S(1)}, s32[128]{0:T(128)}, u32[]{:S(2)}) copy-start(s32[128]{0:T(128)} %param.9) | copy-start | bytes 1540
  6.2 3.4 %collective-permute-start.1 = (f32[2,24,128]{2,1,0:T(8,128)S(1)}, f32[2,24,128]{2,1,0:T(8,128)S(1)}, u32[]{:S(2)}, u32[]{:S(2)}) collective-permute-start(f32[2,24,128]{2,1,0:T(8,128)S(1)} %pad_maximum_fusion.2), channel_id=1, source_target_pairs={{0,5},{1,4},{2,7},{3,6},{4,1},{5,0},{6,3},{7,2},{8,13},{9,12},{10,... | collective-permute-start | bytes 73736 | tf_op jit(solution)/shard_map/ppermute | solution.py:218
  9.6 3.5 %collective-permute-start.2 = (f32[4,24,128]{2,1,0:T(8,128)S(1)}, f32[4,24,128]{2,1,0:T(8,128)S(1)}, u32[]{:S(2)}, u32[]{:S(2)}) collective-permute-start(f32[4,24,128]{2,1,0:T(8,128)S(1)} %pad_maximum_fusion.1), channel_id=1, source_target_pairs={{0,17},{1,2},{2,1},{3,18},{4,7},{5,20},{6,23},{7,4},{8,11},{9,24},... | collective-permute-start | bytes 147464 | tf_op jit(solution)/shard_map/ppermute | solution.py:218
  13.2 4.1 %collective-permute-start.3 = (f32[8,24,128]{2,1,0:T(8,128)S(1)}, f32[8,24,128]{2,1,0:T(8,128)S(1)}, u32[]{:S(2)}, u32[]{:S(2)}) collective-permute-start(f32[8,24,128]{2,1,0:T(8,128)S(1)} %pad_maximum_fusion), channel_id=1, source_target_pairs={{0,3},{1,16},{2,19},{3,0},{4,21},{5,6},{6,5},{7,22},{8,25},{9,10},... | collective-permute-start | bytes 294920 | tf_op jit(solution)/shard_map/ppermute | solution.py:218
  17.3 1.6 %collective-permute-start.4 = (f32[16,24,128]{2,1,0:T(8,128)S(1)}, f32[16,24,128]{2,1,0:T(8,128)S(1)}, u32[]{:S(2)}, u32[]{:S(2)}) collective-permute-start(f32[16,24,128]{2,1,0:T(8,128)S(1)} %constant_dynamic-update-slice_fusion.2.here_ref), channel_id=1, source_target_pairs={{0,1},{1,0},{2,3},{3,2},{4,5},{5,4},{6,7},{7,6},{8,9},{9,8},{10,11... | collective-permute-start | bytes 589832 | tf_op jit(solution)/shard_map/ppermute | solution.py:218

commit v3 on v2

v3 whole, which is shorter than its diff:
```python
import functools
import math

import jax
import jax.numpy as jnp
from jax import lax
from jax.experimental import pallas as pl
from jax.experimental.pallas import tpu as pltpu
from jax.sharding import PartitionSpec as P

F32 = jnp.float32
BF16 = jnp.bfloat16
LN2 = math.log(2.0)
SCALE = math.sqrt(5.0) / LN2
BLOCK = 16
CHUNK = 4
PICK = 2
UNROLL = 32


def exchange_masks(groups, members):
    low = members.bit_length() - 1
    bits = [1 << bit for bit in range(low - 1, 1, -1)]
    bits += [1 << (low + bit) for bit in range(groups.bit_length() - 2, -1, -1)]
    bits += [2] if members > 2 else []
    even = [bit | 1 for bit in bits]
    odd = even[:-2] + even[:-3:-1]
    return even + [1], odd + [1]


def parity(index, count):
    bits = 0
    for bit in range(count.bit_length() - 1):
        bits = bits ^ (index >> bit)
    return bits & 1


def split3(value):
    high = value.astype(BF16).astype(F32)
    rest = value - high
    middle = rest.astype(BF16).astype(F32)
    return high, middle, rest - middle


def norm_tile(x, first):
    high, middle, low = split3(jnp.sum(x * x, axis=0, keepdims=True))
    row = lax.broadcasted_iota(jnp.int32, x.shape, 0)
    if not first:
        row = jnp.where(row < 3, row + 3, row - 3)
    tile = jnp.where(row < 6, 1.0, 0.0)
    tile = jnp.where(row == 0, high, tile)
    tile = jnp.where(row == 1, middle, tile)
    return jnp.where(row == 2, low, tile)


def left_stack(x):
    high, middle, low = split3(x)
    return jnp.concatenate(
        [high, high, high, middle, middle, low, norm_tile(x, True), jnp.zeros_like(x)], 0
    )


def right_stack(x):
    high, middle, low = split3(-2.0 * x)
    return jnp.concatenate(
        [high, middle, low, high, middle, high, norm_tile(x, False), jnp.zeros_like(x)], 0
    ).astype(BF16)


def matern(square):
    square = jnp.maximum(square, 1e-30)
    radius = square * lax.rsqrt(square)
    return (1.0 + LN2 * radius + (LN2 * LN2 / 3.0) * square) * jnp.exp2(-radius)


def rows_of(value, row):
    return jnp.broadcast_to(value[row : row + 1, :], value.shape)


def eliminate(a, b, step):
    tiles = BLOCK // 8
    base, first = step * BLOCK, step * tiles
    later = first + 2 * tiles
    sub = lax.broadcasted_iota(jnp.int32, (8, 128), 0)

    def column(piece, m):
        return jnp.broadcast_to(piece[:, base + m : base + m + 1], (8, 128))

    ra, rb = a[first : first + tiles], b[first : first + tiles]
    cols = [[column(piece, m) for piece in ra] for m in range(BLOCK)]
    below = [[column(piece, m) for piece in a[first + tiles : later]] for m in range(BLOCK)]
    if later < len(a):
        l_high, l_middle, l_low = split3(
            jnp.concatenate([piece[:, base : base + BLOCK] for piece in a[later:]], 0)
        )
        left = jnp.concatenate([l_high, l_high, l_high, l_middle, l_middle, l_low], 1).astype(BF16)
    out = [jnp.zeros((8, 128), F32) for t in range(tiles)]
    for j in range(BLOCK):
        v, s = divmod(j, 8)
        pivot = rows_of(cols[j][v], s)
        inverse = 1.0 / pivot
        out[v] = jnp.where(sub == s, rb[v] * lax.rsqrt(pivot), out[v])
        coef = list(cols[j])
        coef[v] = coef[v] - jnp.where(sub == s, 1.0, 0.0)
        row_a = rows_of(ra[v], s) * inverse
        row_b = rows_of(rb[v], s) * inverse
        for t in range(tiles):
            ra[t] = ra[t] - coef[t] * row_a
            rb[t] = rb[t] - coef[t] * row_b
        for m in range(j + 1, BLOCK):
            entry = rows_of(cols[m][v], s) * inverse
            for t in range(tiles):
                cols[m][t] = cols[m][t] - coef[t] * entry
    for u in range(min(tiles, len(a) - first - tiles)):
        for values, rows in ((a, ra), (b, rb)):
            terms = [
                below[j][u] * rows_of(rows[j // 8], j % 8) for j in range(BLOCK)
            ]
            while len(terms) > 1:
                terms = [x + y for x, y in zip(terms[::2], terms[1::2])]
            values[first + tiles + u] = values[first + tiles + u] - terms[0]
    if later < len(a):
        solved = jnp.concatenate([jnp.concatenate(ra, 0), jnp.concatenate(rb, 0)], 1)
        w_high, w_middle, w_low = split3(solved)
        right = jnp.concatenate([w_high, w_middle, w_low, w_high, w_middle, w_high], 0)
        change = jnp.dot(left, right.astype(BF16), preferred_element_type=F32)
        for t in range(later, len(a)):
            rows = slice(8 * (t - later), 8 * (t - later) + 8)
            a[t] = a[t] - change[rows, :128]
            b[t] = b[t] - change[rows, 128:]
    return jnp.concatenate(out, 0)


NT = (((1,), (1,)), ((), ()))


class Gathered:
    def __init__(self, masks, count, members, side_ref, own_ref):
        self.masks, self.count = masks, count
        self.me = lax.axis_index("blk") * members + lax.axis_index("grp")
        self.kind = parity(self.me, count)
        self.rows = own_ref.shape[1]
        self.dims = side_ref.shape[0] - 2
        self.vectors = own_ref.shape[0] - self.dims
        self.scale = side_ref[: self.dims, :]
        self.noise = side_ref[self.dims : self.dims + 1, :]
        self.pivots = side_ref[self.dims + 1 : self.dims + 2, :].astype(jnp.int32)
        self.points = lax.broadcasted_iota(jnp.int32, (self.rows, self.pivots.shape[1]), 0)
        self.own = own_ref[: self.dims, :] * self.scale
        self.left_own = left_stack(self.own).T.astype(BF16)

    def start(self):
        wide = jnp.zeros((self.rows, 2 * self.vectors), F32)
        narrow = jnp.zeros((self.rows, self.vectors), F32)
        return wide, narrow, jnp.zeros((3 * self.dims, self.pivots.shape[1]), F32)

    def owner(self, index, other):
        device, kind = self.me ^ other, self.kind ^ other
        for bit, (even, odd) in enumerate(zip(self.masks[0][:-1], self.masks[1][:-1])):
            device = device ^ (((index >> bit) & 1) * jnp.where(kind == 0, even, odd))
        return device

    def pick(self, total, ref, index, place, other):
        hots, parts = [], []
        for i in range(PICK):
            device = self.owner(place + index + i, other)
            hots.append((self.points == self.pivots - device * self.rows).astype(F32).astype(BF16))
            parts.append(jnp.concatenate(split3(ref[index + i, : self.dims, :]), 0).astype(BF16))
        return total + jnp.dot(
            jnp.concatenate(parts, 1), jnp.concatenate(hots, 0), preferred_element_type=F32
        )

    def add(self, wide, narrow, ref, index):
        blocks = [ref[index + i] for i in range(CHUNK)]
        right = jnp.concatenate(
            [right_stack(block[: self.dims] * self.scale) for block in blocks], 1
        )
        probe = jnp.concatenate([block[self.dims :] for block in blocks], 1)
        probe_high = probe.astype(BF16)
        probe_low = (probe - probe_high.astype(F32)).astype(BF16)
        value = matern(jnp.dot(self.left_own, right, preferred_element_type=F32))
        value_high = value.astype(BF16)
        value_low = (value - value_high.astype(F32)).astype(BF16)
        both = jnp.concatenate([probe_high, probe_low], 0)
        wide = wide + lax.dot_general(value_high, both, NT, preferred_element_type=F32)
        narrow = narrow + lax.dot_general(value_low, probe_high, NT, preferred_element_type=F32)
        return wide, narrow


def over(ref, width, carry, visit):
    steps = ref.shape[0] // width
    if ref.shape[0] <= UNROLL:
        for i in range(steps):
            carry = visit(carry, i * width)
        return carry
    return lax.fori_loop(0, steps, lambda i, c: visit(c, i * width), carry)


def partial_body(layout, place, side_ref, own_ref, part_ref, *refs):
    work = Gathered(*layout, side_ref, own_ref)
    wide, narrow, picked = work.start()
    if len(refs) > 3:
        wide, narrow, picked = [ref[...] for ref in refs[:3]]
    picked = over(part_ref, PICK, picked, lambda c, i: work.pick(c, part_ref, i, place, 0))
    wide, narrow = over(
        part_ref, CHUNK, (wide, narrow), lambda c, i: work.add(*c, part_ref, i)
    )
    refs[-3][...], refs[-2][...], refs[-1][...] = wide, narrow, picked


def last_body(
    layout, side_ref, own_ref, there_ref, wide_ref, narrow_ref, picked_ref,
    panel_ref, product_ref, rows_ref, total_ref, sems, total_sem,
):
    work = Gathered(*layout, side_ref, own_ref)
    picked = over(
        there_ref, PICK, picked_ref[...], lambda c, i: work.pick(c, there_ref, i, 0, 1)
    )
    dims = work.dims
    pivot_x = (picked[:dims] + picked[dims : 2 * dims] + picked[2 * dims :]) * work.scale
    size = pivot_x.shape[1]
    left_pivot = left_stack(pivot_x).T.astype(BF16)
    both = jnp.concatenate([right_stack(pivot_x), right_stack(work.own)], 1)
    values = matern(jnp.dot(left_pivot, both, preferred_element_type=F32))
    eye = lax.broadcasted_iota(jnp.int32, (size, size), 0) == lax.broadcasted_iota(
        jnp.int32, (size, size), 1
    )
    inner = values[:, :size] + jnp.where(eye, work.noise, 0.0)
    a = [inner[i : i + 8] for i in range(0, size, 8)]
    b = [values[i : i + 8, size:] for i in range(0, size, 8)]

    wide, narrow = wide_ref[...], narrow_ref[...]
    unrolled = there_ref.shape[0] <= UNROLL
    chunks = range(0, there_ref.shape[0], CHUNK) if unrolled else range(0)
    steps = size // BLOCK
    copies = []
    for step in range(steps):
        rows = pl.ds(step * BLOCK, BLOCK)
        rows_ref[rows, :] = eliminate(a, b, step)
        copies.append(
            pltpu.make_async_copy(rows_ref.at[rows, :], panel_ref.at[rows, :], sems.at[step])
        )
        copies[-1].start()
        for index in chunks[step::steps]:
            wide, narrow = work.add(wide, narrow, there_ref, index)
    if not unrolled:
        wide, narrow = over(
            there_ref, CHUNK, (wide, narrow), lambda c, i: work.add(*c, there_ref, i)
        )
    vectors = work.vectors
    total = wide[:, :vectors] + wide[:, vectors:] + narrow
    total_ref[...] = total.T + work.noise * own_ref[dims:, :]
    copies.append(pltpu.make_async_copy(total_ref, product_ref, total_sem))
    copies[-1].start()
    for copy in copies:
        copy.wait()


VMEM = pl.BlockSpec(memory_space=pltpu.VMEM)
PARAMS = pltpu.CompilerParams(vmem_limit_bytes=32 * 1024 * 1024)


def cost(points, rows):
    return pl.CostEstimate(
        flops=points * rows * 60, bytes_accessed=points * 100, transcendentals=points * rows * 2
    )


def partial(layout, place, side, own, part, *carry):
    rows, vectors = own.shape[1], own.shape[0] - side.shape[0] + 2
    return pl.pallas_call(
        functools.partial(partial_body, layout, place),
        out_shape=(
            jax.ShapeDtypeStruct((rows, 2 * vectors), F32),
            jax.ShapeDtypeStruct((rows, vectors), F32),
            jax.ShapeDtypeStruct((3 * (side.shape[0] - 2), side.shape[1]), F32),
        ),
        in_specs=[VMEM] * (3 + len(carry)),
        out_specs=(VMEM,) * 3,
        cost_estimate=cost(part.shape[0] * rows, rows),
        compiler_params=PARAMS,
    )(side, own, part, *carry)


def finish(layout, side, own, there, *carry):
    size, rows = side.shape[1], own.shape[1]
    product = (own.shape[0] - side.shape[0] + 2, rows)
    return pl.pallas_call(
        functools.partial(last_body, layout),
        out_shape=(
            jax.ShapeDtypeStruct((size, rows), F32),
            jax.ShapeDtypeStruct(product, F32),
        ),
        in_specs=[VMEM] * (3 + len(carry)),
        out_specs=(pl.BlockSpec(memory_space=pl.ANY),) * 2,
        scratch_shapes=[
            pltpu.VMEM((size, rows), F32),
            pltpu.VMEM(product, F32),
            pltpu.SemaphoreType.DMA((size // BLOCK,)),
            pltpu.SemaphoreType.DMA,
        ],
        compiler_params=PARAMS,
    )(side, own, there, *carry)


def solution(mesh):
    groups, members = mesh.shape["blk"], mesh.shape["grp"]
    count = groups * members
    masks = exchange_masks(groups, members)

    def swap(value, step):
        pairs = [(i, i ^ masks[parity(i, count)][step]) for i in range(count)]
        return lax.ppermute(value, ("blk", "grp"), pairs)

    def local(inputs, probes, lengths, noise, pivots):
        rows = inputs.shape[1]
        own = jnp.concatenate([inputs, probes], 0)
        layout = (masks, count, members)
        last = len(masks[0]) - 1
        here = own[None]
        for step in range(last - 1):
            if step == 1:
                side = jnp.concatenate(
                    [
                        jnp.broadcast_to((SCALE / lengths)[:, None], inputs.shape),
                        jnp.broadcast_to(noise[:, None], (1, rows)),
                        pivots.astype(F32)[None, :],
                    ],
                    0,
                )
            here = jnp.concatenate([here, swap(here, step)], 0)
        arrived = swap(here, last - 1)
        carry = partial(layout, 0, side, own, here)
        arrived, *carry = lax.optimization_barrier((arrived, *carry))
        there = swap(jnp.concatenate([here, arrived], 0), last)
        carry = partial(layout, here.shape[0], side, own, arrived, *carry)
        return finish(layout, side, own, there, *carry)

    in_specs = (P(None, ("blk", "grp")), P(None, ("blk", "grp")), P(), P(), P())
    out_specs = (P(None, ("blk", "grp")), P(None, ("blk", "grp")))
    return jax.shard_map(local, mesh=mesh, in_specs=in_specs, out_specs=out_specs, check_vma=False)
```

time: 24.4 us -> 23.3 us (0.955)
  waiting for transfers between devices: 7.37 us -> 5.96 us
  Pallas kernels: 5.27 us -> 5.53 us
    ppermute x5, waiting for transfers between devices: 7.37 us -> 5.96 us  [swap(): return lax.ppermute(value, ('blk', 'grp'), pairs)]
    pallas_call x1 -> x3, Pallas kernels: 5.27 us -> 5.53 us  [the longest x1 4.15 us: finish(): pl.pallas_call(functools.partial(last_body, layout), out_shape=(jax.Shape...]
  transfers between devices with their start and end apart: 5 -> 5, of which waited for: 5 -> 5; matrix products, arithmetic and copies ran while one was open for 1% -> 1% of each run, Pallas kernels for 0% -> 6%
where the time goes in v3:
time: 23.3 us; the launch traced here: 23.1 us
  starting transfers between devices  9.31 us (40%)
  waiting for transfers between devices  5.96 us (26%)
  Pallas kernels  5.53 us (24%)
  between operations  1.36 us (6%)
  local copies, waits for them, and re-layouts  0.73 us (3%)
    ppermute x5, starting transfers between devices, swap(): return lax.ppermute(value, ('blk', 'grp'), pairs)  9.31 us
    ppermute x5, waiting for transfers between devices, swap(): return lax.ppermute(value, ('blk', 'grp'), pairs)  5.96 us
    pallas_call x1, Pallas kernels, finish(): pl.pallas_call(functools.partial(last_body, layout), out_shape=(jax.Shape...  4.15 us
    pallas_call x2, Pallas kernels, partial(): pl.pallas_call(functools.partial(partial_body, layout, place), out_shape=...  1.38 us
    unnamed x11, local copies, waits for them, and re-layouts  0.72 us
  transfers between devices with their start and end apart: 5, of which 5 were waited for; matrix products, arithmetic and copies ran while one was open for 1% of the time, Pallas kernels for 6%

profile of v3, /device:TPU:0, one launch (start us, length us, event | category | flops | bytes accessed | tf_op | source)
XLA Modules:
  0.0 23.1 jit_solution(14453678953008362622)
XLA Ops:
  0.6 0.0 copy-start
  0.6 0.7 %constant_dynamic-update-slice_fusion.1 = f32[24,128]{1,0:T(8,128)S(1)} fusion(f32[8,128]{1,0:T(8,128)} %param.5), kind=kLoop, calls=%fused_computation.4 | loop fusion | bytes 8192
  1.3 0.0 copy-done
  1.3 0.0 copy-start.1
  1.3 3.5 %collective-permute-start = (f32[1,24,128]{2,1,0:T(8,128)S(1)}, f32[1,24,128]{2,1,0:T(8,128)S(1)}, u32[]{:S(2)}, u32[]{:S(2)}) collective-permute-start(f32[1,24,128]{2,1,0:T(8,128)S(1)} %bitcast.5), channel_id=1, source_target_pairs={{0,9},{1,8},{2,11},{3,10},{4,13},{5,12},{6,15},{7,14},{8,1},{9,0},... | collective-permute-start | bytes 36872 | tf_op jit(solution)/shard_map/ppermute | solution.py:313
  4.8 0.0 copy-done.1
  4.8 0.0 copy-start.2
  5.5 0.0 copy-done.2
  5.5 0.1 pad_maximum_fusion.4
  5.6 0.1 pad_maximum_fusion.3.side_ref
  5.7 0.6 %collective-permute-done = f32[1,24,128]{2,1,0:T(8,128)S(1)} collective-permute-done((f32[1,24,128]{2,1,0:T(8,128)S(1)}, f32[1,24,128]{2,1,0:T(8,128)S(1)}, u32[]{:S(2)}, u32[]{:S(2)}) %collective-permute-start) | collective-permute-done | bytes 12320 | tf_op jit(solution)/shard_map/ppermute | solution.py:313
  6.2 1.9 %collective-permute-start.1 = (f32[2,24,128]{2,1,0:T(8,128)S(1)}, f32[2,24,128]{2,1,0:T(8,128)S(1)}, u32[]{:S(2)}, u32[]{:S(2)}) collective-permute-start(f32[2,24,128]{2,1,0:T(8,128)S(1)} %pad_maximum_fusion.2), channel_id=1, source_target_pairs={{0,5},{1,4},{2,7},{3,6},{4,1},{5,0},{6,3},{7,2},{8,13},{9,12},{10,... | collective-permute-start | bytes 73736 | tf_op jit(solution)/shard_map/ppermute | solution.py:313
  8.1 1.5 %collective-permute-done.1 = f32[2,24,128]{2,1,0:T(8,128)S(1)} collective-permute-done((f32[2,24,128]{2,1,0:T(8,128)S(1)}, f32[2,24,128]{2,1,0:T(8,128)S(1)}, u32[]{:S(2)}, u32[]{:S(2)}) %collective-permute-start.1) | collective-permute-done | bytes 24608 | tf_op jit(solution)/shard_map/ppermute | solution.py:313
  9.6 1.7 %collective-permute-start.2 = (f32[4,24,128]{2,1,0:T(8,128)S(1)}, f32[4,24,128]{2,1,0:T(8,128)S(1)}, u32[]{:S(2)}, u32[]{:S(2)}) collective-permute-start(f32[4,24,128]{2,1,0:T(8,128)S(1)} %pad_maximum_fusion.1), channel_id=1, source_target_pairs={{0,17},{1,2},{2,1},{3,18},{4,7},{5,20},{6,23},{7,4},{8,11},{9,24},... | collective-permute-start | bytes 147464 | tf_op jit(solution)/shard_map/ppermute | solution.py:313
  11.3 1.8 %collective-permute-done.2 = f32[4,24,128]{2,1,0:T(8,128)S(1)} collective-permute-done((f32[4,24,128]{2,1,0:T(8,128)S(1)}, f32[4,24,128]{2,1,0:T(8,128)S(1)}, u32[]{:S(2)}, u32[]{:S(2)}) %collective-permute-start.2) | collective-permute-done | bytes 49184 | tf_op jit(solution)/shard_map/ppermute | solution.py:313
  13.2 1.7 %collective-permute-start.3 = (f32[8,24,128]{2,1,0:T(8,128)S(1)}, f32[8,24,128]{2,1,0:T(8,128)S(1)}, u32[]{:S(2)}, u32[]{:S(2)}) collective-permute-start(f32[8,24,128]{2,1,0:T(8,128)S(1)} %pad_maximum_fusion.part_ref), channel_id=1, source_target_pairs={{0,3},{1,16},{2,19},{3,0},{4,21},{5,6},{6,5},{7,22},{8,25},{9,10},... | collective-permute-start | bytes 294920 | tf_op jit(solution)/shard_map/ppermute | solution.py:313
  14.9 0.6 %shard_map.68 = (f32[128,32]{1,0:T(8,128)S(1)}, f32[128,16]{1,0:T(8,128)S(1)}, f32[24,128]{1,0:T(8,128)S(1)}) custom-call(f32[10,128]{1,0:T(8,128)S(1)} %pad_maximum_fusion.3.side_ref, f32[24,128]{1,0:T(8,128)S(1)} %constant_dynamic-update-slice_fusion.own_ref, f32[8,24,128]{2,1,0:T(8,128)S(1)} %pad_maximum_fusion.part_ref), custom_call_target="tpu_custom_call" | custom-call | flops 7864320 | bytes 102400 | tf_op jit(solution)/shard_map/pallas_call | solution.py:271
  15.5 1.7 %collective-permute-done.3.part_ref = f32[8,24,128]{2,1,0:T(8,128)S(1)} collective-permute-done((f32[8,24,128]{2,1,0:T(8,128)S(1)}, f32[8,24,128]{2,1,0:T(8,128)S(1)}, u32[]{:S(2)}, u32[]{:S(2)}) %collective-permute-start.3) | collective-permute-done | bytes 98336 | tf_op jit(solution)/shard_map/ppermute | solution.py:313
  17.3 0.6 %collective-permute-start.4 = (f32[16,24,128]{2,1,0:T(8,128)S(1)}, f32[16,24,128]{2,1,0:T(8,128)S(1)}, u32[]{:S(2)}, u32[]{:S(2)}) collective-permute-start(f32[16,24,128]{2,1,0:T(8,128)S(1)} %constant_dynamic-update-slice_fusion.2), channel_id=1, source_target_pairs={{0,1},{1,0},{2,3},{3,2},{4,5},{5,4},{6,7},{7,6},{8,9},{9,8},{10,11... | collective-permute-start | bytes 589832 | tf_op jit(solution)/shard_map/ppermute | solution.py:313
  17.8 0.7 %shard_map.69 = (f32[128,32]{1,0:T(8,128)S(1)}, f32[128,16]{1,0:T(8,128)S(1)}, f32[24,128]{1,0:T(8,128)S(1)}) custom-call(f32[10,128]{1,0:T(8,128)S(1)} %pad_maximum_fusion.3.side_ref, f32[24,128]{1,0:T(8,128)S(1)} %constant_dynamic-update-slice_fusion.own_ref, f32[8,24,128]{2,1,0:T(8,128)S(1)} %collective-permute-done.3.part_ref, ...), custom_call_target="tpu_custom_call" | custom-call | flops 7864320 | bytes 102400 | tf_op jit(solution)/shard_map/pallas_call | solution.py:271
  18.6 0.3 %collective-permute-done.4.there_ref = f32[16,24,128]{2,1,0:T(8,128)S(1)} collective-permute-done((f32[16,24,128]{2,1,0:T(8,128)S(1)}, f32[16,24,128]{2,1,0:T(8,128)S(1)}, u32[]{:S(2)}, u32[]{:S(2)}) %collective-permute-start.4) | collective-permute-done | bytes 196640 | tf_op jit(solution)/shard_map/ppermute | solution.py:313
  18.9 4.1 %shard_map.70 = (f32[128,128]{1,0:T(8,128)}, f32[16,128]{1,0:T(8,128)}) custom-call(f32[10,128]{1,0:T(8,128)S(1)} %pad_maximum_fusion.3.side_ref, f32[24,128]{1,0:T(8,128)S(1)} %constant_dynamic-update-slice_fusion.own_ref, f32[16,24,128]{2,1,0:T(8,128)S(1)} %collective-permute-done.4.there_ref, f32[128,32]{1,0:T(8,128)S(1)} %get-tuple-element.19.wide_ref, ...), custom_call_target="tpu_custom_call" | custom-call | tf_op jit(solution)/shard_map/pallas_call | solution.py:288
  (11 shorter events, 0.0 us)
Async XLA Ops:
  0.6 0.7 %copy-start = (f32[16,128]{1,0:T(8,128)S(1)}, f32[16,128]{1,0:T(8,128)}, u32[]{:S(2)}) copy-start(f32[16,128]{1,0:T(8,128)} %param.6) | copy-start | bytes 24580
  1.3 3.5 %copy-start.1 = (s32[128]{0:T(128)S(1)}, s32[128]{0:T(128)}, u32[]{:S(2)}) copy-start(s32[128]{0:T(128)} %param.9) | copy-start | bytes 1540
  1.3 4.9 %collective-permute-start = (f32[1,24,128]{2,1,0:T(8,128)S(1)}, f32[1,24,128]{2,1,0:T(8,128)S(1)}, u32[]{:S(2)}, u32[]{:S(2)}) collective-permute-start(f32[1,24,128]{2,1,0:T(8,128)S(1)} %bitcast.5), channel_id=1, source_target_pairs={{0,9},{1,8},{2,11},{3,10},{4,13},{5,12},{6,15},{7,14},{8,1},{9,0},... | collective-permute-start | bytes 36872 | tf_op jit(solution)/shard_map/ppermute | solution.py:313
  4.8 0.7 %copy-start.2 = (f32[8]{0:T(128)S(1)}, f32[8]{0:T(128)}, u32[]{:S(2)}) copy-start(f32[8]{0:T(128)} %param.7) | copy-start | bytes 100
  6.2 3.4 %collective-permute-start.1 = (f32[2,24,128]{2,1,0:T(8,128)S(1)}, f32[2,24,128]{2,1,0:T(8,128)S(1)}, u32[]{:S(2)}, u32[]{:S(2)}) collective-permute-start(f32[2,24,128]{2,1,0:T(8,128)S(1)} %pad_maximum_fusion.2), channel_id=1, source_target_pairs={{0,5},{1,4},{2,7},{3,6},{4,1},{5,0},{6,3},{7,2},{8,13},{9,12},{10,... | collective-permute-start | bytes 73736 | tf_op jit(solution)/shard_map/ppermute | solution.py:313
  9.6 3.5 %collective-permute-start.2 = (f32[4,24,128]{2,1,0:T(8,128)S(1)}, f32[4,24,128]{2,1,0:T(8,128)S(1)}, u32[]{:S(2)}, u32[]{:S(2)}) collective-permute-start(f32[4,24,128]{2,1,0:T(8,128)S(1)} %pad_maximum_fusion.1), channel_id=1, source_target_pairs={{0,17},{1,2},{2,1},{3,18},{4,7},{5,20},{6,23},{7,4},{8,11},{9,24},... | collective-permute-start | bytes 147464 | tf_op jit(solution)/shard_map/ppermute | solution.py:313
  13.2 4.1 %collective-permute-start.3 = (f32[8,24,128]{2,1,0:T(8,128)S(1)}, f32[8,24,128]{2,1,0:T(8,128)S(1)}, u32[]{:S(2)}, u32[]{:S(2)}) collective-permute-start(f32[8,24,128]{2,1,0:T(8,128)S(1)} %pad_maximum_fusion.part_ref), channel_id=1, source_target_pairs={{0,3},{1,16},{2,19},{3,0},{4,21},{5,6},{6,5},{7,22},{8,25},{9,10},... | collective-permute-start | bytes 294920 | tf_op jit(solution)/shard_map/ppermute | solution.py:313
  17.3 1.6 %collective-permute-start.4 = (f32[16,24,128]{2,1,0:T(8,128)S(1)}, f32[16,24,128]{2,1,0:T(8,128)S(1)}, u32[]{:S(2)}, u32[]{:S(2)}) collective-permute-start(f32[16,24,128]{2,1,0:T(8,128)S(1)} %constant_dynamic-update-slice_fusion.2), channel_id=1, source_target_pairs={{0,1},{1,0},{2,3},{3,2},{4,5},{5,4},{6,7},{7,6},{8,9},{9,8},{10,11... | collective-permute-start | bytes 589832 | tf_op jit(solution)/shard_map/ppermute | solution.py:313

commit v4 on v3

--- a/solution.py
+++ b/solution.py
@@ -90,10 +90,10 @@
     cols = [[column(piece, m) for piece in ra] for m in range(BLOCK)]
     below = [[column(piece, m) for piece in a[first + tiles : later]] for m in range(BLOCK)]
     if later < len(a):
-        l_high, l_middle, l_low = split3(
-            jnp.concatenate([piece[:, base : base + BLOCK] for piece in a[later:]], 0)
-        )
-        left = jnp.concatenate([l_high, l_high, l_high, l_middle, l_middle, l_low], 1).astype(BF16)
+        l_high, l_middle, l_low = [
+            part.astype(BF16) for part in split3(jnp.concatenate(a[later:], 0))
+        ]
+        left = jnp.concatenate([l_high, l_middle], 1)
     out = [jnp.zeros((8, 128), F32) for t in range(tiles)]
     for j in range(BLOCK):
         v, s = divmod(j, 8)
@@ -102,28 +102,47 @@
         out[v] = jnp.where(sub == s, rb[v] * lax.rsqrt(pivot), out[v])
         coef = list(cols[j])
         coef[v] = coef[v] - jnp.where(sub == s, 1.0, 0.0)
-        row_a = rows_of(ra[v], s) * inverse
-        row_b = rows_of(rb[v], s) * inverse
+        coef = [piece * inverse for piece in coef]
+        row_a, row_b = rows_of(ra[v], s), rows_of(rb[v], s)
         for t in range(tiles):
             ra[t] = ra[t] - coef[t] * row_a
             rb[t] = rb[t] - coef[t] * row_b
         for m in range(j + 1, BLOCK):
-            entry = rows_of(cols[m][v], s) * inverse
+            entry = rows_of(cols[m][v], s)
             for t in range(tiles):
                 cols[m][t] = cols[m][t] - coef[t] * entry
-    for u in range(min(tiles, len(a) - first - tiles)):
+    if first + tiles < len(a):
         for values, rows in ((a, ra), (b, rb)):
-            terms = [
-                below[j][u] * rows_of(rows[j // 8], j % 8) for j in range(BLOCK)
-            ]
-            while len(terms) > 1:
-                terms = [x + y for x, y in zip(terms[::2], terms[1::2])]
-            values[first + tiles + u] = values[first + tiles + u] - terms[0]
+            sums = [[None, None] for u in range(tiles)]
+            for j in range(BLOCK):
+                row = rows_of(rows[j // 8], j % 8)
+                for u in range(tiles):
+                    term = below[j][u] * row
+                    before = sums[u][j % 2]
+                    sums[u][j % 2] = term if before is None else before + term
+            for u in range(tiles):
+                at = first + tiles + u
+                values[at] = values[at] - (sums[u][0] + sums[u][1])
     if later < len(a):
         solved = jnp.concatenate([jnp.concatenate(ra, 0), jnp.concatenate(rb, 0)], 1)
-        w_high, w_middle, w_low = split3(solved)
-        right = jnp.concatenate([w_high, w_middle, w_low, w_high, w_middle, w_high], 0)
-        change = jnp.dot(left, right.astype(BF16), preferred_element_type=F32)
+
+        def placed(value):
+            parts = [value.astype(BF16)]
+            if base:
+                parts.insert(0, jnp.zeros((base, value.shape[1]), BF16))
+            parts.append(jnp.zeros((8 * len(a) - base - BLOCK, value.shape[1]), BF16))
+            return jnp.concatenate(parts, 0)
+
+        w_high, w_middle, w_low = [placed(part) for part in split3(solved)]
+        change = (
+            jnp.dot(left, jnp.concatenate([w_high, w_high], 0), preferred_element_type=F32)
+            + jnp.dot(left, jnp.concatenate([w_middle, w_middle], 0), preferred_element_type=F32)
+            + jnp.dot(
+                jnp.concatenate([l_high, l_low], 1),
+                jnp.concatenate([w_low, w_high], 0),
+                preferred_element_type=F32,
+            )
+        )
         for t in range(later, len(a)):
             rows = slice(8 * (t - later), 8 * (t - later) + 8)
             a[t] = a[t] - change[rows, :128]
@@ -135,7 +154,7 @@
 
 
 class Gathered:
-    def __init__(self, masks, count, members, side_ref, own_ref):
+    def __init__(self, masks, count, members, side_ref, own_ref, *mate_refs):
         self.masks, self.count = masks, count
         self.me = lax.axis_index("blk") * members + lax.axis_index("grp")
         self.kind = parity(self.me, count)
@@ -147,11 +166,13 @@
         self.pivots = side_ref[self.dims + 1 : self.dims + 2, :].astype(jnp.int32)
         self.points = lax.broadcasted_iota(jnp.int32, (self.rows, self.pivots.shape[1]), 0)
         self.own = own_ref[: self.dims, :] * self.scale
-        self.left_own = left_stack(self.own).T.astype(BF16)
+        lefts = [left_stack(self.own)]
+        lefts += [left_stack(ref[: self.dims, :] * self.scale) for ref in mate_refs]
+        self.left_own = jnp.concatenate([left.T.astype(BF16) for left in lefts], 0)
 
     def start(self):
-        wide = jnp.zeros((self.rows, 2 * self.vectors), F32)
-        narrow = jnp.zeros((self.rows, self.vectors), F32)
+        wide = jnp.zeros((self.left_own.shape[0], 2 * self.vectors), F32)
+        narrow = jnp.zeros((self.left_own.shape[0], self.vectors), F32)
         return wide, narrow, jnp.zeros((3 * self.dims, self.pivots.shape[1]), F32)
 
     def owner(self, index, other):
@@ -187,25 +208,44 @@
         return wide, narrow
 
 
-def over(ref, width, carry, visit):
-    steps = ref.shape[0] // width
-    if ref.shape[0] <= UNROLL:
+def over(blocks, width, carry, visit):
+    steps = blocks // width
+    if blocks <= UNROLL:
         for i in range(steps):
             carry = visit(carry, i * width)
         return carry
     return lax.fori_loop(0, steps, lambda i, c: visit(c, i * width), carry)
 
 
-def partial_body(layout, place, side_ref, own_ref, part_ref, *refs):
+def gathered_sum(wide, narrow):
+    vectors = narrow.shape[1]
+    return (wide[:, :vectors] + wide[:, vectors:] + narrow).T
+
+
+def early_body(layout, side_ref, own_ref, mate_ref, part_ref, wide_ref, narrow_ref, picked_ref, parcel_ref):
+    work = Gathered(*layout, side_ref, own_ref, mate_ref)
+    wide, narrow, picked = work.start()
+    blocks, rows = part_ref.shape[0], work.rows
+    picked = over(blocks, PICK, picked, lambda c, i: work.pick(c, part_ref, i, 0, 0))
+    wide, narrow = over(blocks, CHUNK, (wide, narrow), lambda c, i: work.add(*c, part_ref, i))
+    wide_ref[...], narrow_ref[...], picked_ref[...] = wide[:rows], narrow[:rows], picked
+    parcel_ref[0, : work.vectors, :] = gathered_sum(wide[rows:], narrow[rows:])
+    parcel_ref[0, work.vectors :, :] = jnp.zeros((work.dims, rows), F32)
+    parcel_ref[1] = picked
+
+
+def middle_body(
+    layout, place, side_ref, own_ref, part_ref, wide_in, narrow_in, picked_in,
+    wide_ref, narrow_ref, picked_ref,
+):
     work = Gathered(*layout, side_ref, own_ref)
-    wide, narrow, picked = work.start()
-    if len(refs) > 3:
-        wide, narrow, picked = [ref[...] for ref in refs[:3]]
-    picked = over(part_ref, PICK, picked, lambda c, i: work.pick(c, part_ref, i, place, 0))
-    wide, narrow = over(
-        part_ref, CHUNK, (wide, narrow), lambda c, i: work.add(*c, part_ref, i)
-    )
-    refs[-3][...], refs[-2][...], refs[-1][...] = wide, narrow, picked
+    blocks = part_ref.shape[0]
+    picked_ref[...] = over(
+        blocks, PICK, picked_in[...], lambda c, i: work.pick(c, part_ref, i, place, 0)
+    )
+    wide_ref[...], narrow_ref[...] = over(
+        blocks, CHUNK, (wide_in[...], narrow_in[...]), lambda c, i: work.add(*c, part_ref, i)
+    )
 
 
 def last_body(
@@ -213,8 +253,12 @@
     panel_ref, product_ref, rows_ref, total_ref, sems, total_sem,
 ):
     work = Gathered(*layout, side_ref, own_ref)
+    blocks = there_ref.shape[0] - 2
     picked = over(
-        there_ref, PICK, picked_ref[...], lambda c, i: work.pick(c, there_ref, i, 0, 1)
+        blocks,
+        PICK,
+        picked_ref[...] + there_ref[blocks + 1],
+        lambda c, i: work.pick(c, there_ref, i, blocks, 1),
     )
     dims = work.dims
     pivot_x = (picked[:dims] + picked[dims : 2 * dims] + picked[2 * dims :]) * work.scale
@@ -230,8 +274,11 @@
     b = [values[i : i + 8, size:] for i in range(0, size, 8)]
 
     wide, narrow = wide_ref[...], narrow_ref[...]
-    unrolled = there_ref.shape[0] <= UNROLL
-    chunks = range(0, there_ref.shape[0], CHUNK) if unrolled else range(0)
+    chunks = range(0, blocks, CHUNK) if blocks <= UNROLL else range(0)
+    if blocks > UNROLL:
+        wide, narrow = over(
+            blocks, CHUNK, (wide, narrow), lambda c, i: work.add(*c, there_ref, i)
+        )
     steps = size // BLOCK
     copies = []
     for step in range(steps):
@@ -243,15 +290,11 @@
         copies[-1].start()
         for index in chunks[step::steps]:
             wide, narrow = work.add(wide, narrow, there_ref, index)
-    if not unrolled:
-        wide, narrow = over(
-            there_ref, CHUNK, (wide, narrow), lambda c, i: work.add(*c, there_ref, i)
-        )
-    vectors = work.vectors
-    total = wide[:, :vectors] + wide[:, vectors:] + narrow
-    total_ref[...] = total.T + work.noise * own_ref[dims:, :]
-    copies.append(pltpu.make_async_copy(total_ref, product_ref, total_sem))
-    copies[-1].start()
+        if step == min(len(chunks), steps - 1):
+            total = gathered_sum(wide, narrow) + there_ref[blocks, : work.vectors, :]
+            total_ref[...] = total + work.noise * own_ref[dims:, :]
+            copies.append(pltpu.make_async_copy(total_ref, product_ref, total_sem))
+            copies[-1].start()
     for copy in copies:
         copy.wait()
 
@@ -266,16 +309,33 @@
     )
 
 
-def partial(layout, place, side, own, part, *carry):
+def sums(side, own):
     rows, vectors = own.shape[1], own.shape[0] - side.shape[0] + 2
+    return (
+        jax.ShapeDtypeStruct((rows, 2 * vectors), F32),
+        jax.ShapeDtypeStruct((rows, vectors), F32),
+        jax.ShapeDtypeStruct((3 * (side.shape[0] - 2), side.shape[1]), F32),
+    )
+
+
+def early(layout, side, own, mate, part):
+    rows = own.shape[1]
     return pl.pallas_call(
-        functools.partial(partial_body, layout, place),
-        out_shape=(
-            jax.ShapeDtypeStruct((rows, 2 * vectors), F32),
-            jax.ShapeDtypeStruct((rows, vectors), F32),
-            jax.ShapeDtypeStruct((3 * (side.shape[0] - 2), side.shape[1]), F32),
-        ),
-        in_specs=[VMEM] * (3 + len(carry)),
+        functools.partial(early_body, layout),
+        out_shape=sums(side, own) + (jax.ShapeDtypeStruct((2,) + own.shape, F32),),
+        in_specs=[VMEM] * 4,
+        out_specs=(VMEM,) * 4,
+        cost_estimate=cost(part.shape[0] * rows, 2 * rows),
+        compiler_params=PARAMS,
+    )(side, own, mate, part)
+
+
+def middle(layout, place, side, own, part, *carry):
+    rows = own.shape[1]
+    return pl.pallas_call(
+        functools.partial(middle_body, layout, place),
+        out_shape=sums(side, own),
+        in_specs=[VMEM] * 6,
         out_specs=(VMEM,) * 3,
         cost_estimate=cost(part.shape[0] * rows, rows),
         compiler_params=PARAMS,
@@ -328,12 +388,14 @@
                     ],
                     0,
                 )
+            if step == 1:
+                mate = swap(lax.optimization_barrier((own, here))[0], last)
             here = jnp.concatenate([here, swap(here, step)], 0)
         arrived = swap(here, last - 1)
-        carry = partial(layout, 0, side, own, here)
-        arrived, *carry = lax.optimization_barrier((arrived, *carry))
-        there = swap(jnp.concatenate([here, arrived], 0), last)
-        carry = partial(layout, here.shape[0], side, own, arrived, *carry)
+        *carry, parcel = early(layout, side, own, mate, here)
+        arrived, parcel = lax.optimization_barrier((arrived, parcel))
+        there = swap(jnp.concatenate([arrived, parcel], 0), last)
+        carry = middle(layout, here.shape[0], side, own, arrived, *carry)
         return finish(layout, side, own, there, *carry)
 
     in_specs = (P(None, ("blk", "grp")), P(None, ("blk", "grp")), P(), P(), P())

time: 23.3 us -> 23.1 us (level)
  waiting for transfers between devices: 5.96 us -> 5.16 us
  starting transfers between devices: 9.31 us -> 9.67 us
  Pallas kernels: 5.53 us -> 5.81 us
    ppermute x5 -> x6, waiting for transfers between devices: 5.96 us -> 5.16 us  [swap(): return lax.ppermute(value, ('blk', 'grp'), pairs)]
    pallas_call x2, Pallas kernels: 1.38 us -> 1.78 us  [the longest x1 1.04 us: early(): pl.pallas_call(functools.partial(early_body, layout), out_shape=sums(side...]
    ppermute x5 -> x6, starting transfers between devices: 9.31 us -> 9.67 us  [swap(): return lax.ppermute(value, ('blk', 'grp'), pairs)]
    unnamed x11 -> x7, local copies, waits for them, and re-layouts: 0.72 us -> 0.71 us
  transfers between devices with their start and end apart: 5 -> 6, of which waited for: 5 -> 5; matrix products, arithmetic and copies ran while one was open for 1% -> 1% of each run, Pallas kernels for 6% -> 8%
where the time goes in v4:
time: 23.1 us; the launch traced here: 22.8 us
  starting transfers between devices  9.67 us (42%)
  Pallas kernels  5.81 us (25%)
  waiting for transfers between devices  5.16 us (22%)
  between operations  1.32 us (6%)
  local copies, waits for them, and re-layouts  0.71 us (3%)
    ppermute x6, starting transfers between devices, swap(): return lax.ppermute(value, ('blk', 'grp'), pairs)  9.67 us
    ppermute x6, waiting for transfers between devices, swap(): return lax.ppermute(value, ('blk', 'grp'), pairs)  5.16 us
    pallas_call x1, Pallas kernels, finish(): pl.pallas_call(functools.partial(last_body, layout), out_shape=(jax.Shape...  4.03 us
    pallas_call x1, Pallas kernels, early(): pl.pallas_call(functools.partial(early_body, layout), out_shape=sums(side...  1.04 us
    pallas_call x1, Pallas kernels, middle(): pl.pallas_call(functools.partial(middle_body, layout, place), out_shape=s...  0.74 us
    unnamed x7, local copies, waits for them, and re-layouts  0.71 us
  transfers between devices with their start and end apart: 6, of which 5 were waited for; matrix products, arithmetic and copies ran while one was open for 1% of the time, Pallas kernels for 8%

profile of v4, /device:TPU:0, one launch (start us, length us, event | category | flops | bytes accessed | tf_op | source)
XLA Modules:
  0.0 22.8 jit_solution(6322789189295760155)
XLA Ops:
  0.6 0.0 copy-start
  0.6 0.7 %constant_dynamic-update-slice_fusion.1 = f32[24,128]{1,0:T(8,128)S(1)} fusion(f32[8,128]{1,0:T(8,128)} %param.5), kind=kLoop, calls=%fused_computation.6 | loop fusion | bytes 8192
  1.3 0.0 copy-done
  1.3 0.0 copy-start.1
  1.3 3.5 %collective-permute-start = (f32[1,24,128]{2,1,0:T(8,128)S(1)}, f32[1,24,128]{2,1,0:T(8,128)S(1)}, u32[]{:S(2)}, u32[]{:S(2)}) collective-permute-start(f32[1,24,128]{2,1,0:T(8,128)S(1)} %bitcast.4), channel_id=1, source_target_pairs={{0,9},{1,8},{2,11},{3,10},{4,13},{5,12},{6,15},{7,14},{8,1},{9,0},... | collective-permute-start | bytes 36872 | tf_op jit(solution)/shard_map/ppermute | solution.py:373
  4.8 0.0 copy-done.1
  4.8 0.0 copy-start.2
  4.8 1.4 %collective-permute-done = f32[1,24,128]{2,1,0:T(8,128)S(1)} collective-permute-done((f32[1,24,128]{2,1,0:T(8,128)S(1)}, f32[1,24,128]{2,1,0:T(8,128)S(1)}, u32[]{:S(2)}, u32[]{:S(2)}) %collective-permute-start) | collective-permute-done | bytes 12320 | tf_op jit(solution)/shard_map/ppermute | solution.py:373
  6.2 1.9 %collective-permute-start.1 = (f32[2,24,128]{2,1,0:T(8,128)S(1)}, f32[2,24,128]{2,1,0:T(8,128)S(1)}, u32[]{:S(2)}, u32[]{:S(2)}) collective-permute-start(f32[2,24,128]{2,1,0:T(8,128)S(1)} %pad_maximum_fusion.3), channel_id=1, source_target_pairs={{0,5},{1,4},{2,7},{3,6},{4,1},{5,0},{6,3},{7,2},{8,13},{9,12},{10,... | collective-permute-start | bytes 73736 | tf_op jit(solution)/shard_map/ppermute | solution.py:373
  8.1 0.0 copy-done.2
  8.8 0.9 %collective-permute-done.1 = f32[2,24,128]{2,1,0:T(8,128)S(1)} collective-permute-done((f32[2,24,128]{2,1,0:T(8,128)S(1)}, f32[2,24,128]{2,1,0:T(8,128)S(1)}, u32[]{:S(2)}, u32[]{:S(2)}) %collective-permute-start.1) | collective-permute-done | bytes 24608 | tf_op jit(solution)/shard_map/ppermute | solution.py:373
  9.6 1.7 %collective-permute-start.2 = (f32[4,24,128]{2,1,0:T(8,128)S(1)}, f32[4,24,128]{2,1,0:T(8,128)S(1)}, u32[]{:S(2)}, u32[]{:S(2)}) collective-permute-start(f32[4,24,128]{2,1,0:T(8,128)S(1)} %pad_maximum_fusion.2), channel_id=1, source_target_pairs={{0,17},{1,2},{2,1},{3,18},{4,7},{5,20},{6,23},{7,4},{8,11},{9,24},... | collective-permute-start | bytes 147464 | tf_op jit(solution)/shard_map/ppermute | solution.py:373
  11.3 0.1 pad_maximum_fusion.5
  11.4 0.4 %collective-permute-start.4 = (f32[24,128]{1,0:T(8,128)S(1)}, f32[24,128]{1,0:T(8,128)S(1)}, u32[]{:S(2)}, u32[]{:S(2)}) collective-permute-start(f32[24,128]{1,0:T(8,128)S(1)} %constant_dynamic-update-slice_fusion.own_ref), channel_id=1, source_target_pairs={{0,1},{1,0},{2,3},{3,2},{4,5},{5,4},{6,7},{7,6},{8,9},{9,8},{10,11... | collective-permute-start | bytes 36872 | tf_op jit(solution)/shard_map/ppermute | solution.py:373
  11.8 1.4 %collective-permute-done.2 = f32[4,24,128]{2,1,0:T(8,128)S(1)} collective-permute-done((f32[4,24,128]{2,1,0:T(8,128)S(1)}, f32[4,24,128]{2,1,0:T(8,128)S(1)}, u32[]{:S(2)}, u32[]{:S(2)}) %collective-permute-start.2) | collective-permute-done | bytes 49184 | tf_op jit(solution)/shard_map/ppermute | solution.py:373
  13.2 1.7 %collective-permute-start.3 = (f32[8,24,128]{2,1,0:T(8,128)S(1)}, f32[8,24,128]{2,1,0:T(8,128)S(1)}, u32[]{:S(2)}, u32[]{:S(2)}) collective-permute-start(f32[8,24,128]{2,1,0:T(8,128)S(1)} %pad_maximum_fusion.1.part_ref), channel_id=1, source_target_pairs={{0,3},{1,16},{2,19},{3,0},{4,21},{5,6},{6,5},{7,22},{8,25},{9,10},... | collective-permute-start | bytes 294920 | tf_op jit(solution)/shard_map/ppermute | solution.py:373
  14.9 0.1 pad_maximum_fusion.4.side_ref
  14.9 0.0 collective-permute-done.4.mate_ref
  14.9 1.0 %shard_map.68 = (f32[128,32]{1,0:T(8,128)S(1)}, f32[128,16]{1,0:T(8,128)S(1)}, f32[24,128]{1,0:T(8,128)S(1)}, f32[2,24,128]{2,1,0:T(8,128)S(1)}) custom-call(f32[10,128]{1,0:T(8,128)S(1)} %pad_maximum_fusion.4.side_ref, f32[24,128]{1,0:T(8,128)S(1)} %constant_dynamic-update-slice_fusion.own_ref, f32[24,128]{1,0:T(8,128)S(1)} %collective-permute-done.4.mate_ref, ...), custom_call_target="tpu_custom_call" | custom-call | flops 15728640 | bytes 102400 | tf_op jit(solution)/shard_map/pallas_call | solution.py:323
  16.0 1.3 %collective-permute-done.3.part_ref = f32[8,24,128]{2,1,0:T(8,128)S(1)} collective-permute-done((f32[8,24,128]{2,1,0:T(8,128)S(1)}, f32[8,24,128]{2,1,0:T(8,128)S(1)}, u32[]{:S(2)}, u32[]{:S(2)}) %collective-permute-start.3) | collective-permute-done | bytes 98336 | tf_op jit(solution)/shard_map/ppermute | solution.py:373
  17.3 0.6 %collective-permute-start.5 = (f32[10,24,128]{2,1,0:T(8,128)S(1)}, f32[10,24,128]{2,1,0:T(8,128)S(1)}, u32[]{:S(2)}, u32[]{:S(2)}) collective-permute-start(f32[10,24,128]{2,1,0:T(8,128)S(1)} %pad_maximum_fusion), channel_id=1, source_target_pairs={{0,1},{1,0},{2,3},{3,2},{4,5},{5,4},{6,7},{7,6},{8,9},{9,8},{10,11... | collective-permute-start | bytes 368648 | tf_op jit(solution)/shard_map/ppermute | solution.py:373
  17.8 0.7 %shard_map.69 = (f32[128,32]{1,0:T(8,128)S(1)}, f32[128,16]{1,0:T(8,128)S(1)}, f32[24,128]{1,0:T(8,128)S(1)}) custom-call(f32[10,128]{1,0:T(8,128)S(1)} %pad_maximum_fusion.4.side_ref, f32[24,128]{1,0:T(8,128)S(1)} %constant_dynamic-update-slice_fusion.own_ref, f32[8,24,128]{2,1,0:T(8,128)S(1)} %collective-permute-done.3.part_ref, ...), custom_call_target="tpu_custom_call" | custom-call | flops 7864320 | bytes 102400 | tf_op jit(solution)/shard_map/pallas_call | solution.py:335
  18.6 0.2 %collective-permute-done.5.there_ref = f32[10,24,128]{2,1,0:T(8,128)S(1)} collective-permute-done((f32[10,24,128]{2,1,0:T(8,128)S(1)}, f32[10,24,128]{2,1,0:T(8,128)S(1)}, u32[]{:S(2)}, u32[]{:S(2)}) %collective-permute-start.5) | collective-permute-done | bytes 122912 | tf_op jit(solution)/shard_map/ppermute | solution.py:373
  18.8 4.0 %shard_map.70 = (f32[128,128]{1,0:T(8,128)}, f32[16,128]{1,0:T(8,128)}) custom-call(f32[10,128]{1,0:T(8,128)S(1)} %pad_maximum_fusion.4.side_ref, f32[24,128]{1,0:T(8,128)S(1)} %constant_dynamic-update-slice_fusion.own_ref, f32[10,24,128]{2,1,0:T(8,128)S(1)} %collective-permute-done.5.there_ref, f32[128,32]{1,0:T(8,128)S(1)} %get-tuple-element.19.wide_ref, ...), custom_call_target="tpu_custom_call" | custom-call | tf_op jit(solution)/shard_map/pallas_call | solution.py:348
  (7 shorter events, 0.0 us)
Async XLA Ops:
  0.6 0.7 %copy-start = (f32[16,128]{1,0:T(8,128)S(1)}, f32[16,128]{1,0:T(8,128)}, u32[]{:S(2)}) copy-start(f32[16,128]{1,0:T(8,128)} %param.6) | copy-start | bytes 24580
  1.3 3.5 %copy-start.1 = (f32[8]{0:T(128)S(1)}, f32[8]{0:T(128)}, u32[]{:S(2)}) copy-start(f32[8]{0:T(128)} %param.7) | copy-start | bytes 100
  1.3 4.9 %collective-permute-start = (f32[1,24,128]{2,1,0:T(8,128)S(1)}, f32[1,24,128]{2,1,0:T(8,128)S(1)}, u32[]{:S(2)}, u32[]{:S(2)}) collective-permute-start(f32[1,24,128]{2,1,0:T(8,128)S(1)} %bitcast.4), channel_id=1, source_target_pairs={{0,9},{1,8},{2,11},{3,10},{4,13},{5,12},{6,15},{7,14},{8,1},{9,0},... | collective-permute-start | bytes 36872 | tf_op jit(solution)/shard_map/ppermute | solution.py:373
  4.8 3.3 %copy-start.2 = (s32[128]{0:T(128)S(1)}, s32[128]{0:T(128)}, u32[]{:S(2)}) copy-start(s32[128]{0:T(128)} %param.9) | copy-start | bytes 1540
  6.2 3.4 %collective-permute-start.1 = (f32[2,24,128]{2,1,0:T(8,128)S(1)}, f32[2,24,128]{2,1,0:T(8,128)S(1)}, u32[]{:S(2)}, u32[]{:S(2)}) collective-permute-start(f32[2,24,128]{2,1,0:T(8,128)S(1)} %pad_maximum_fusion.3), channel_id=1, source_target_pairs={{0,5},{1,4},{2,7},{3,6},{4,1},{5,0},{6,3},{7,2},{8,13},{9,12},{10,... | collective-permute-start | bytes 73736 | tf_op jit(solution)/shard_map/ppermute | solution.py:373
  9.6 3.5 %collective-permute-start.2 = (f32[4,24,128]{2,1,0:T(8,128)S(1)}, f32[4,24,128]{2,1,0:T(8,128)S(1)}, u32[]{:S(2)}, u32[]{:S(2)}) collective-permute-start(f32[4,24,128]{2,1,0:T(8,128)S(1)} %pad_maximum_fusion.2), channel_id=1, source_target_pairs={{0,17},{1,2},{2,1},{3,18},{4,7},{5,20},{6,23},{7,4},{8,11},{9,24},... | collective-permute-start | bytes 147464 | tf_op jit(solution)/shard_map/ppermute | solution.py:373
  11.4 3.6 %collective-permute-start.4 = (f32[24,128]{1,0:T(8,128)S(1)}, f32[24,128]{1,0:T(8,128)S(1)}, u32[]{:S(2)}, u32[]{:S(2)}) collective-permute-start(f32[24,128]{1,0:T(8,128)S(1)} %constant_dynamic-update-slice_fusion.own_ref), channel_id=1, source_target_pairs={{0,1},{1,0},{2,3},{3,2},{4,5},{5,4},{6,7},{7,6},{8,9},{9,8},{10,11... | collective-permute-start | bytes 36872 | tf_op jit(solution)/shard_map/ppermute | solution.py:373
  13.2 4.1 %collective-permute-start.3 = (f32[8,24,128]{2,1,0:T(8,128)S(1)}, f32[8,24,128]{2,1,0:T(8,128)S(1)}, u32[]{:S(2)}, u32[]{:S(2)}) collective-permute-start(f32[8,24,128]{2,1,0:T(8,128)S(1)} %pad_maximum_fusion.1.part_ref), channel_id=1, source_target_pairs={{0,3},{1,16},{2,19},{3,0},{4,21},{5,6},{6,5},{7,22},{8,25},{9,10},... | collective-permute-start | bytes 294920 | tf_op jit(solution)/shard_map/ppermute | solution.py:373
  17.3 1.5 %collective-permute-start.5 = (f32[10,24,128]{2,1,0:T(8,128)S(1)}, f32[10,24,128]{2,1,0:T(8,128)S(1)}, u32[]{:S(2)}, u32[]{:S(2)}) collective-permute-start(f32[10,24,128]{2,1,0:T(8,128)S(1)} %pad_maximum_fusion), channel_id=1, source_target_pairs={{0,1},{1,0},{2,3},{3,2},{4,5},{5,4},{6,7},{7,6},{8,9},{9,8},{10,11... | collective-permute-start | bytes 368648 | tf_op jit(solution)/shard_map/ppermute | solution.py:373

commit v5 on v4

v5 whole, which is shorter than its diff:
```python
import functools
import math

import jax
import jax.numpy as jnp
from jax import lax
from jax.experimental import pallas as pl
from jax.experimental.pallas import tpu as pltpu
from jax.sharding import PartitionSpec as P

F32 = jnp.float32
BF16 = jnp.bfloat16
LN2 = math.log(2.0)
SCALE = math.sqrt(5.0) / LN2
BLOCK = 16
CHUNK = 4
PICK = 2
FIRST = 5
UNROLL = 32


def exchange_masks(groups, members):
    low = members.bit_length() - 1
    bits = [1 << bit for bit in range(low - 1, 1, -1)]
    bits += [1 << (low + bit) for bit in range(groups.bit_length() - 2, -1, -1)]
    bits += [2] if members > 2 else []
    even = [bit | 1 for bit in bits]
    odd = even[:-2] + even[:-3:-1]
    return even + [1], odd + [1]


def parity(index, count):
    bits = 0
    for bit in range(count.bit_length() - 1):
        bits = bits ^ (index >> bit)
    return bits & 1


def split3(value):
    high = value.astype(BF16).astype(F32)
    rest = value - high
    middle = rest.astype(BF16).astype(F32)
    return high, middle, rest - middle


def norm_tile(x, first):
    high, middle, low = split3(jnp.sum(x * x, axis=0, keepdims=True))
    row = lax.broadcasted_iota(jnp.int32, x.shape, 0)
    if not first:
        row = jnp.where(row < 3, row + 3, row - 3)
    tile = jnp.where(row < 6, 1.0, 0.0)
    tile = jnp.where(row == 0, high, tile)
    tile = jnp.where(row == 1, middle, tile)
    return jnp.where(row == 2, low, tile)


def left_stack(x):
    high, middle, low = split3(x)
    return jnp.concatenate(
        [high, high, high, middle, middle, low, norm_tile(x, True), jnp.zeros_like(x)], 0
    )


def right_stack(x):
    high, middle, low = split3(-2.0 * x)
    return jnp.concatenate(
        [high, middle, low, high, middle, high, norm_tile(x, False), jnp.zeros_like(x)], 0
    ).astype(BF16)


def matern(square):
    square = jnp.maximum(square, 1e-30)
    radius = square * lax.rsqrt(square)
    return (1.0 + LN2 * radius + (LN2 * LN2 / 3.0) * square) * jnp.exp2(-radius)


def rows_of(value, row):
    return jnp.broadcast_to(value[row : row + 1, :], value.shape)


def eliminate(a, b, step):
    tiles = BLOCK // 8
    base, first = step * BLOCK, step * tiles
    later = first + 2 * tiles
    sub = lax.broadcasted_iota(jnp.int32, (8, 128), 0)

    def column(piece, m):
        return jnp.broadcast_to(piece[:, base + m : base + m + 1], (8, 128))

    ra, rb = a[first : first + tiles], b[first : first + tiles]
    cols = [[column(piece, m) for piece in ra] for m in range(BLOCK)]
    below = [[column(piece, m) for piece in a[first + tiles : later]] for m in range(BLOCK)]
    if later < len(a):
        l_high, l_middle, l_low = [
            part.astype(BF16) for part in split3(jnp.concatenate(a[later:], 0))
        ]
        left = jnp.concatenate([l_high, l_middle], 1)
    out = [jnp.zeros((8, 128), F32) for t in range(tiles)]
    for j in range(0, BLOCK, 2):
        v, s = divmod(j, 8)
        one, two = cols[j], cols[j + 1]
        top, side, end = rows_of(one[v], s), rows_of(one[v], s + 1), rows_of(two[v], s + 1)
        det = top * end - side * side
        inverse = 1.0 / det
        row_a, next_a = rows_of(ra[v], s), rows_of(ra[v], s + 1)
        row_b, next_b = rows_of(rb[v], s), rows_of(rb[v], s + 1)
        root = lax.rsqrt(top)
        out[v] = jnp.where(sub == s, row_b * root, out[v])
        out[v] = jnp.where(
            sub == s + 1, (top * next_b - side * row_b) * (root * lax.rsqrt(det)), out[v]
        )
        one, two = list(one), list(two)
        one[v] = one[v] - jnp.where(sub == s, 1.0, 0.0)
        two[v] = two[v] - jnp.where(sub == s + 1, 1.0, 0.0)
        first_coef = [(x * end - y * side) * inverse for x, y in zip(one, two)]
        next_coef = [(y * top - x * side) * inverse for x, y in zip(one, two)]
        for t in range(tiles):
            ra[t] = ra[t] - first_coef[t] * row_a - next_coef[t] * next_a
            rb[t] = rb[t] - first_coef[t] * row_b - next_coef[t] * next_b
        for m in range(j + 2, BLOCK):
            entry, following = rows_of(cols[m][v], s), rows_of(cols[m][v], s + 1)
            for t in range(tiles):
                change = first_coef[t] * entry + next_coef[t] * following
                cols[m][t] = cols[m][t] - change
    if first + tiles < len(a):
        for values, rows in ((a, ra), (b, rb)):
            sums = [[None, None] for u in range(tiles)]
            for j in range(BLOCK):
                row = rows_of(rows[j // 8], j % 8)
                for u in range(tiles):
                    term = below[j][u] * row
                    before = sums[u][j % 2]
                    sums[u][j % 2] = term if before is None else before + term
            for u in range(tiles):
                at = first + tiles + u
                values[at] = values[at] - (sums[u][0] + sums[u][1])
    if later < len(a):
        solved = jnp.concatenate([jnp.concatenate(ra, 0), jnp.concatenate(rb, 0)], 1)

        def placed(value):
            parts = [value.astype(BF16)]
            if base:
                parts.insert(0, jnp.zeros((base, value.shape[1]), BF16))
            parts.append(jnp.zeros((8 * len(a) - base - BLOCK, value.shape[1]), BF16))
            return jnp.concatenate(parts, 0)

        w_high, w_middle, w_low = [placed(part) for part in split3(solved)]
        change = (
            jnp.dot(left, jnp.concatenate([w_high, w_high], 0), preferred_element_type=F32)
            + jnp.dot(left, jnp.concatenate([w_middle, w_middle], 0), preferred_element_type=F32)
            + jnp.dot(
                jnp.concatenate([l_high, l_low], 1),
                jnp.concatenate([w_low, w_high], 0),
                preferred_element_type=F32,
            )
        )
        for t in range(later, len(a)):
            rows = slice(8 * (t - later), 8 * (t - later) + 8)
            a[t] = a[t] - change[rows, :128]
            b[t] = b[t] - change[rows, 128:]
    return jnp.concatenate(out, 0)


NT = (((1,), (1,)), ((), ()))


class Gathered:
    def __init__(self, layout, side_ref, own_ref):
        self.masks, self.count, members = layout
        self.me = lax.axis_index("blk") * members + lax.axis_index("grp")
        self.kind = parity(self.me, self.count)
        self.dims, self.rows = own_ref.shape
        self.scale = side_ref[: self.dims, :]
        self.noise = side_ref[self.dims : self.dims + 1, :]
        self.pivots = side_ref[self.dims + 1 : self.dims + 2, :].astype(jnp.int32)
        self.points = lax.broadcasted_iota(jnp.int32, (self.rows, self.pivots.shape[1]), 0)
        self.own = own_ref[...] * self.scale

    def owner(self, index, other):
        device, kind = self.me ^ other, self.kind ^ other
        for bit, (even, odd) in enumerate(zip(self.masks[0][:-1], self.masks[1][:-1])):
            device = device ^ (((index >> bit) & 1) * jnp.where(kind == 0, even, odd))
        return device

    def pick(self, total, ref, other):
        def visit(total, index):
            hots, parts = [], []
            for i in range(PICK):
                device = self.owner(index + i, other)
                hot = self.points == self.pivots - device * self.rows
                hots.append(hot.astype(F32).astype(BF16))
                parts.append(jnp.concatenate(split3(ref[index + i]), 0).astype(BF16))
            return total + jnp.dot(
                jnp.concatenate(parts, 1), jnp.concatenate(hots, 0), preferred_element_type=F32
            )

        return over(ref.shape[0], PICK, total, visit)

    def left(self):
        return left_stack(self.own).T.astype(BF16)

    def product(self, carry, points_ref, probes_ref):
        left_own = self.left()

        def visit(carry, index):
            wide, narrow = carry
            places = [index + i for i in range(CHUNK)]
            right = jnp.concatenate(
                [right_stack(points_ref[place] * self.scale) for place in places], 1
            )
            probe = jnp.concatenate([probes_ref[place] for place in places], 1)
            probe_high = probe.astype(BF16)
            probe_low = (probe - probe_high.astype(F32)).astype(BF16)
            value = matern(jnp.dot(left_own, right, preferred_element_type=F32))
            value_high = value.astype(BF16)
            value_low = (value - value_high.astype(F32)).astype(BF16)
            both = jnp.concatenate([probe_high, probe_low], 0)
            wide = wide + lax.dot_general(value_high, both, NT, preferred_element_type=F32)
            narrow = narrow + lax.dot_general(value_low, probe_high, NT, preferred_element_type=F32)
            return wide, narrow

        return over(points_ref.shape[0], CHUNK, carry, visit)


def over(blocks, width, carry, visit):
    steps = blocks // width
    if blocks <= UNROLL:
        for i in range(steps):
            carry = visit(carry, i * width)
        return carry
    return lax.fori_loop(0, steps, lambda i, c: visit(c, i * width), carry)


def pick_body(layout, side_ref, own_ref, points_ref, picked_ref):
    work = Gathered(layout, side_ref, own_ref)
    zero = jnp.zeros((3 * work.dims, side_ref.shape[1]), F32)
    picked_ref[...] = work.pick(zero, points_ref, 0)


def pivot_body(layout, side_ref, own_ref, points_ref, picked_ref, a_ref, b_ref):
    work = Gathered(layout, side_ref, own_ref)
    picked = work.pick(picked_ref[...], points_ref, 1)
    dims = work.dims
    pivot_x = (picked[:dims] + picked[dims : 2 * dims] + picked[2 * dims :]) * work.scale
    size = pivot_x.shape[1]
    left_pivot = left_stack(pivot_x).T.astype(BF16)
    both = jnp.concatenate([right_stack(pivot_x), right_stack(work.own)], 1)
    values = matern(jnp.dot(left_pivot, both, preferred_element_type=F32))
    eye = lax.broadcasted_iota(jnp.int32, (size, size), 0) == lax.broadcasted_iota(
        jnp.int32, (size, size), 1
    )
    a_ref[...] = values[:, :size] + jnp.where(eye, work.noise, 0.0)
    b_ref[...] = values[:, size:]


def first_body(
    layout, side_ref, own_ref, points_ref, probes_ref, a_ref, b_ref,
    a_out, b_out, rows_ref, wide_ref, narrow_ref,
):
    work = Gathered(layout, side_ref, own_ref)
    vectors = probes_ref.shape[1]
    carry = jnp.zeros((work.rows, 2 * vectors), F32), jnp.zeros((work.rows, vectors), F32)
    wide_ref[...], narrow_ref[...] = work.product(carry, points_ref, probes_ref)
    size, done = a_ref.shape[0], rows_ref.shape[0]
    a = [a_ref[i : i + 8, :] for i in range(0, size, 8)]
    b = [b_ref[i : i + 8, :] for i in range(0, size, 8)]
    for step in range(done // BLOCK):
        rows_ref[step * BLOCK : (step + 1) * BLOCK, :] = eliminate(a, b, step)
    a_out[...] = jnp.concatenate(a[done // 8 :], 0)
    b_out[...] = jnp.concatenate(b[done // 8 :], 0)


def last_body(
    layout, side_ref, own_ref, points_ref, probes_ref, own_probes_ref,
    a_ref, b_ref, done_ref, wide_ref, narrow_ref,
    panel_ref, product_ref, rows_ref, total_ref, sems,
):
    done = done_ref.shape[0]
    copies = [pltpu.make_async_copy(done_ref, panel_ref.at[pl.ds(0, done), :], sems.at[0])]
    copies[-1].start()
    work = Gathered(layout, side_ref, own_ref)
    wide, narrow = work.product((wide_ref[...], narrow_ref[...]), points_ref, probes_ref)
    vectors = narrow.shape[1]
    total = (wide[:, :vectors] + wide[:, vectors:] + narrow).T
    total_ref[...] = total + work.noise * own_probes_ref[...]
    copies.append(pltpu.make_async_copy(total_ref, product_ref, sems.at[1]))
    left = rows_ref.shape[0]
    a = [None] * (done // 8) + [a_ref[i : i + 8, :] for i in range(0, left, 8)]
    b = [None] * (done // 8) + [b_ref[i : i + 8, :] for i in range(0, left, 8)]
    for step in range(left // BLOCK):
        rows_ref[step * BLOCK : (step + 1) * BLOCK, :] = eliminate(a, b, done // BLOCK + step)
        if step == left // BLOCK - 2:
            copies[-1].start()
    copies.append(
        pltpu.make_async_copy(rows_ref, panel_ref.at[pl.ds(done, left), :], sems.at[2])
    )
    copies[-1].start()
    for copy in copies:
        copy.wait()


VMEM = pl.BlockSpec(memory_space=pltpu.VMEM)
ANY = pl.BlockSpec(memory_space=pl.ANY)
PARAMS = pltpu.CompilerParams(vmem_limit_bytes=32 * 1024 * 1024)


def shapes(*dims):
    return tuple(jax.ShapeDtypeStruct(dim, F32) for dim in dims)


def run(body, layout, outs, args, work, spec=VMEM, scratch=()):
    cost = pl.CostEstimate(flops=work * 60, bytes_accessed=work // 4, transcendentals=work * 2)
    return pl.pallas_call(
        functools.partial(body, layout),
        out_shape=shapes(*outs),
        in_specs=[VMEM] * len(args),
        out_specs=(spec,) * len(outs),
        scratch_shapes=scratch,
        cost_estimate=cost,
        compiler_params=PARAMS,
    )(*args)


def solution(mesh):
    groups, members = mesh.shape["blk"], mesh.shape["grp"]
    count = groups * members
    masks = exchange_masks(groups, members)
    layout = (masks, count, members)
    last = len(masks[0]) - 1

    def swap(value, step):
        pairs = [(i, i ^ masks[parity(i, count)][step]) for i in range(count)]
        return lax.ppermute(value, ("blk", "grp"), pairs)

    def local(inputs, probes, lengths, noise, pivots):
        rows, vectors, size = inputs.shape[1], probes.shape[0], pivots.shape[0]
        points, vector = inputs[None], probes[None]
        for step in range(last):
            if step == 1:
                side = jnp.concatenate(
                    [
                        jnp.broadcast_to((SCALE / lengths)[:, None], inputs.shape),
                        jnp.broadcast_to(noise[:, None], (1, rows)),
                        pivots.astype(F32)[None, :],
                    ],
                    0,
                )
            came = swap(points, step)
            vector_came = swap(vector, step)
            points = jnp.concatenate([points, came], 0)
            if step < last - 1:
                vector = jnp.concatenate([vector, vector_came], 0)
                vector = lax.optimization_barrier((vector, came))[0]
        points_there = swap(points, last)
        picked, = run(
            pick_body, layout, [(3 * inputs.shape[0], size)], (side, inputs, points), size * rows
        )
        a, b = run(
            pivot_body, layout, [(size, size), (size, rows)],
            (side, inputs, points_there, picked), size * rows,
        )
        vector_came, a = lax.optimization_barrier((vector_came, a))
        vector = jnp.concatenate([vector, vector_came], 0)
        vector_there = swap(vector, last)
        done = FIRST * BLOCK
        a, b, done_rows, wide, narrow = run(
            first_body, layout,
            [(size - done, size), (size - done, rows), (done, rows), (rows, 2 * vectors), (rows, vectors)],
            (side, inputs, points, vector, a, b), size * rows * 16,
        )
        return run(
            last_body, layout, [(size, rows), (vectors, rows)],
            (side, inputs, points_there, vector_there, probes, a, b, done_rows, wide, narrow),
            size * rows * 16, ANY,
            [
                pltpu.VMEM((size - done, rows), F32),
                pltpu.VMEM((vectors, rows), F32),
                pltpu.SemaphoreType.DMA((3,)),
            ],
        )

    in_specs = (P(None, ("blk", "grp")), P(None, ("blk", "grp")), P(), P(), P())
    out_specs = (P(None, ("blk", "grp")), P(None, ("blk", "grp")))
    return jax.shard_map(local, mesh=mesh, in_specs=in_specs, out_specs=out_specs, check_vma=False)
```

time: 23.1 us -> 24.7 us (1.069)
  starting transfers between devices: 9.67 us -> 13.7 us
  waiting for transfers between devices: 5.16 us -> 2.09 us
  local copies, waits for them, and re-layouts: 0.71 us -> 1.28 us
    ppermute x6 -> x10, starting transfers between devices: 9.67 us -> 13.7 us  [swap(): return lax.ppermute(value, ('blk', 'grp'), pairs)]
    ppermute x6 -> x10, waiting for transfers between devices: 5.16 us -> 2.09 us  [swap(): return lax.ppermute(value, ('blk', 'grp'), pairs)]
    unnamed x7 -> x13, local copies, waits for them, and re-layouts: 0.71 us -> 1.27 us
    pallas_call x3 -> x4, Pallas kernels: 5.81 us -> 5.91 us  [run(): pl.pallas_call(functools.partial(body, layout), out_shape=shapes(*outs),...]
  transfers between devices with their start and end apart: 6 -> 10, of which waited for: 5 -> 7; matrix products, arithmetic and copies ran while one was open for 1% -> 1% of each run, Pallas kernels for 8% -> 14%
where the time goes in v5:
time: 24.7 us; the launch traced here: 24.5 us
  starting transfers between devices  13.7 us (55%)
  Pallas kernels  5.91 us (24%)
  waiting for transfers between devices  2.09 us (8%)
  between operations  1.35 us (5%)
  local copies, waits for them, and re-layouts  1.28 us (5%)
    ppermute x10, starting transfers between devices, swap(): return lax.ppermute(value, ('blk', 'grp'), pairs)  13.7 us
    pallas_call x4, Pallas kernels, run(): pl.pallas_call(functools.partial(body, layout), out_shape=shapes(*outs),...  5.91 us
    ppermute x10, waiting for transfers between devices, swap(): return lax.ppermute(value, ('blk', 'grp'), pairs)  2.09 us
    unnamed x13, local copies, waits for them, and re-layouts  1.27 us
  transfers between devices with their start and end apart: 10, of which 7 were waited for; matrix products, arithmetic and copies ran while one was open for 1% of the time, Pallas kernels for 14%

profile of v5, /device:TPU:0, one launch (start us, length us, event | category | flops | bytes accessed | tf_op | source)
XLA Modules:
  0.0 24.5 jit_solution(17389011714021771376)
XLA Ops:
  0.6 3.5 %collective-permute-start = (f32[1,8,128]{2,1,0:T(8,128)}, f32[1,8,128]{2,1,0:T(8,128)S(1)}, u32[]{:S(2)}, u32[]{:S(2)}) collective-permute-start(f32[1,8,128]{2,1,0:T(8,128)} %bitcast.6), channel_id=1, source_target_pairs={{0,9},{1,8},{2,11},{3,10},{4,13},{5,12},{6,15},{7,14},{8,1},{9,0},... | collective-permute-start | bytes 12296 | tf_op jit(solution)/shard_map/ppermute | solution.py:333
  4.2 0.0 copy-start.2
  4.2 0.1 collective-permute-start.5
  4.9 0.0 copy-done.2
  4.9 0.0 copy-start.3
  4.9 0.6 %copy-done.3 = s32[128]{0:T(128)S(1)} copy-done((s32[128]{0:T(128)S(1)}, s32[128]{0:T(128)}, u32[]{:S(2)}) %copy-start.3) | copy-done | bytes 536
  5.6 0.1 pad_maximum_fusion.7
  5.7 0.0 copy-start
  5.7 0.1 pad_maximum_fusion.5.side_ref
  5.7 0.6 %copy-done = f32[8,128]{1,0:T(8,128)S(1)} copy-done((f32[8,128]{1,0:T(8,128)S(1)}, f32[8,128]{1,0:T(8,128)}, u32[]{:S(2)}) %copy-start) | copy-done | bytes 4120
  6.3 0.0 copy-start.1
  6.4 0.0 collective-permute-done
  6.4 1.9 %collective-permute-start.1 = (f32[2,8,128]{2,1,0:T(8,128)S(1)}, f32[2,8,128]{2,1,0:T(8,128)S(1)}, u32[]{:S(2)}, u32[]{:S(2)}) collective-permute-start(f32[2,8,128]{2,1,0:T(8,128)S(1)} %pad_maximum_fusion.6), channel_id=1, source_target_pairs={{0,5},{1,4},{2,7},{3,6},{4,1},{5,0},{6,3},{7,2},{8,13},{9,12},{10,... | collective-permute-start | bytes 24584 | tf_op jit(solution)/shard_map/ppermute | solution.py:333
  8.3 0.1 collective-permute-done.5
  8.4 0.0 copy-done.1
  8.4 1.9 %collective-permute-start.6 = (f32[2,16,128]{2,1,0:T(8,128)S(1)}, f32[2,16,128]{2,1,0:T(8,128)S(1)}, u32[]{:S(2)}, u32[]{:S(2)}) collective-permute-start(f32[2,16,128]{2,1,0:T(8,128)S(1)} %pad_maximum_fusion.4), channel_id=1, source_target_pairs={{0,5},{1,4},{2,7},{3,6},{4,1},{5,0},{6,3},{7,2},{8,13},{9,12},{10,... | collective-permute-start | bytes 49160 | tf_op jit(solution)/shard_map/ppermute | solution.py:333
  10.2 0.0 collective-permute-done.1
  10.2 1.1 %collective-permute-start.2 = (f32[4,8,128]{2,1,0:T(8,128)S(1)}, f32[4,8,128]{2,1,0:T(8,128)S(1)}, u32[]{:S(2)}, u32[]{:S(2)}) collective-permute-start(f32[4,8,128]{2,1,0:T(8,128)S(1)} %pad_maximum_fusion.3), channel_id=1, source_target_pairs={{0,17},{1,2},{2,1},{3,18},{4,7},{5,20},{6,23},{7,4},{8,11},{9,24},... | collective-permute-start | bytes 49160 | tf_op jit(solution)/shard_map/ppermute | solution.py:333
  11.3 0.3 %collective-permute-done.6 = f32[2,16,128]{2,1,0:T(8,128)S(1)} collective-permute-done((f32[2,16,128]{2,1,0:T(8,128)S(1)}, f32[2,16,128]{2,1,0:T(8,128)S(1)}, u32[]{:S(2)}, u32[]{:S(2)}) %collective-permute-start.6) | collective-permute-done | bytes 16416 | tf_op jit(solution)/shard_map/ppermute | solution.py:333
  11.7 1.7 %collective-permute-start.7 = (f32[4,16,128]{2,1,0:T(8,128)S(1)}, f32[4,16,128]{2,1,0:T(8,128)S(1)}, u32[]{:S(2)}, u32[]{:S(2)}) collective-permute-start(f32[4,16,128]{2,1,0:T(8,128)S(1)} %pad_maximum_fusion.2), channel_id=1, source_target_pairs={{0,17},{1,2},{2,1},{3,18},{4,7},{5,20},{6,23},{7,4},{8,11},{9,24},... | collective-permute-start | bytes 98312 | tf_op jit(solution)/shard_map/ppermute | solution.py:333
  13.3 0.1 collective-permute-done.2
  13.4 1.2 %collective-permute-start.3 = (f32[8,8,128]{2,1,0:T(8,128)S(1)}, f32[8,8,128]{2,1,0:T(8,128)S(1)}, u32[]{:S(2)}, u32[]{:S(2)}) collective-permute-start(f32[8,8,128]{2,1,0:T(8,128)S(1)} %pad_maximum_fusion.1), channel_id=1, source_target_pairs={{0,3},{1,16},{2,19},{3,0},{4,21},{5,6},{6,5},{7,22},{8,25},{9,10},... | collective-permute-start | bytes 98312 | tf_op jit(solution)/shard_map/ppermute | solution.py:333
  14.6 0.4 %collective-permute-done.7 = f32[4,16,128]{2,1,0:T(8,128)S(1)} collective-permute-done((f32[4,16,128]{2,1,0:T(8,128)S(1)}, f32[4,16,128]{2,1,0:T(8,128)S(1)}, u32[]{:S(2)}, u32[]{:S(2)}) %collective-permute-start.7) | collective-permute-done | bytes 32800 | tf_op jit(solution)/shard_map/ppermute | solution.py:333
  15.0 1.6 %collective-permute-start.8 = (f32[8,16,128]{2,1,0:T(8,128)S(1)}, f32[8,16,128]{2,1,0:T(8,128)S(1)}, u32[]{:S(2)}, u32[]{:S(2)}) collective-permute-start(f32[8,16,128]{2,1,0:T(8,128)S(1)} %pad_maximum_fusion), channel_id=1, source_target_pairs={{0,3},{1,16},{2,19},{3,0},{4,21},{5,6},{6,5},{7,22},{8,25},{9,10},... | collective-permute-start | bytes 196616 | tf_op jit(solution)/shard_map/ppermute | solution.py:333
  16.7 0.1 collective-permute-done.3
  16.7 0.1 collective-permute-start.4
  16.9 0.2 %shard_map.68.picked_ref = f32[24,128]{1,0:T(8,128)S(1)} custom-call(f32[10,128]{1,0:T(8,128)S(1)} %pad_maximum_fusion.5.side_ref, f32[8,128]{1,0:T(8,128)S(1)} %copy-done, f32[16,8,128]{2,1,0:T(8,128)S(1)} %constant_dynamic-update-slice_fusion.points_ref), custom_call_target="tpu_custom_call" | custom-call | flops 983040 | bytes 4096 | tf_op jit(solution)/shard_map/pallas_call | solution.py:313
  17.1 0.9 %collective-permute-done.4.points_ref = f32[16,8,128]{2,1,0:T(8,128)S(1)} collective-permute-done((f32[16,8,128]{2,1,0:T(8,128)S(1)}, f32[16,8,128]{2,1,0:T(8,128)S(1)}, u32[]{:S(2)}, u32[]{:S(2)}) %collective-permute-start.4) | collective-permute-done | bytes 65568 | tf_op jit(solution)/shard_map/ppermute | solution.py:333
  18.0 0.5 %shard_map.69 = (f32[128,128]{1,0:T(8,128)S(1)}, f32[128,128]{1,0:T(8,128)S(1)}) custom-call(f32[10,128]{1,0:T(8,128)S(1)} %pad_maximum_fusion.5.side_ref, f32[8,128]{1,0:T(8,128)S(1)} %copy-done, f32[16,8,128]{2,1,0:T(8,128)S(1)} %collective-permute-done.4.points_ref, f32[24,128]{1,0:T(8,128)S(1)} %shard_map.68.picked_ref), custom_call_target="tpu_custom_call" | custom-call | flops 983040 | bytes 4096 | tf_op jit(solution)/shard_map/pallas_call | solution.py:313
  18.5 0.2 collective-permute-done.8
  18.7 0.5 %collective-permute-start.9 = (f32[16,16,128]{2,1,0:T(8,128)S(1)}, f32[16,16,128]{2,1,0:T(8,128)S(1)}, u32[]{:S(2)}, u32[]{:S(2)}) collective-permute-start(f32[16,16,128]{2,1,0:T(8,128)S(1)} %constant_dynamic-update-slice_fusion.5.probes_ref), channel_id=1, source_target_pairs={{0,1},{1,0},{2,3},{3,2},{4,5},{5,4},{6,7},{7,6},{8,9},{9,8},{10,11... | collective-permute-start | bytes 393224 | tf_op jit(solution)/shard_map/ppermute | solution.py:333
  19.3 2.7 %shard_map.70 = (f32[48,128]{1,0:T(8,128)S(1)}, f32[48,128]{1,0:T(8,128)S(1)}, f32[80,128]{1,0:T(8,128)S(1)}, f32[128,32]{1,0:T(8,128)S(1)}, f32[128,16]{1,0:T(8,128)S(1)}) custom-call(f32[10,128]{1,0:T(8,128)S(1)} %pad_maximum_fusion.5.side_ref, f32[8,128]{1,0:T(8,128)S(1)} %copy-done, f32[16,8,128]{2,1,0:T(8,128)S(1)} %constant_dynamic-update-slice_fusion.points_ref, ...), custom_call_target="tpu_custom_call" | custom-call | flops 15728640 | bytes 65536 | tf_op jit(solution)/shard_map/pallas_call | solution.py:313
  22.0 0.0 collective-permute-done.9.probes_ref
  22.0 2.5 %shard_map.71 = (f32[128,128]{1,0:T(8,128)}, f32[16,128]{1,0:T(8,128)}) custom-call(f32[10,128]{1,0:T(8,128)S(1)} %pad_maximum_fusion.5.side_ref, f32[8,128]{1,0:T(8,128)S(1)} %copy-done, f32[16,8,128]{2,1,0:T(8,128)S(1)} %collective-permute-done.4.points_ref, f32[16,16,128]{2,1,0:T(8,128)S(1)} %collective-permute-done.9.probes_ref, ...), custom_call_target="tpu_custom_call" | custom-call | flops 15728640 | bytes 65536 | tf_op jit(solution)/shard_map/pallas_call | solution.py:313
  (15 shorter events, 0.0 us)
Async XLA Ops:
  0.6 5.7 %collective-permute-start = (f32[1,8,128]{2,1,0:T(8,128)}, f32[1,8,128]{2,1,0:T(8,128)S(1)}, u32[]{:S(2)}, u32[]{:S(2)}) collective-permute-start(f32[1,8,128]{2,1,0:T(8,128)} %bitcast.6), channel_id=1, source_target_pairs={{0,9},{1,8},{2,11},{3,10},{4,13},{5,12},{6,15},{7,14},{8,1},{9,0},... | collective-permute-start | bytes 12296 | tf_op jit(solution)/shard_map/ppermute | solution.py:333
  4.2 0.7 %copy-start.2 = (f32[8]{0:T(128)S(1)}, f32[8]{0:T(128)}, u32[]{:S(2)}) copy-start(f32[8]{0:T(128)} %param.7) | copy-start | bytes 100
  4.2 4.2 %collective-permute-start.5 = (f32[1,16,128]{2,1,0:T(8,128)}, f32[1,16,128]{2,1,0:T(8,128)S(1)}, u32[]{:S(2)}, u32[]{:S(2)}) collective-permute-start(f32[1,16,128]{2,1,0:T(8,128)} %bitcast.10), channel_id=1, source_target_pairs={{0,9},{1,8},{2,11},{3,10},{4,13},{5,12},{6,15},{7,14},{8,1},{9,0},... | collective-permute-start | bytes 24584 | tf_op jit(solution)/shard_map/ppermute | solution.py:333
  4.9 0.7 %copy-start.3 = (s32[128]{0:T(128)S(1)}, s32[128]{0:T(128)}, u32[]{:S(2)}) copy-start(s32[128]{0:T(128)} %param.9) | copy-start | bytes 1540
  5.7 0.7 %copy-start = (f32[8,128]{1,0:T(8,128)S(1)}, f32[8,128]{1,0:T(8,128)}, u32[]{:S(2)}) copy-start(f32[8,128]{1,0:T(8,128)} %own_ref.7) | copy-start | bytes 12292
  6.3 2.0 %copy-start.1 = (f32[16,128]{1,0:T(8,128)S(1)}, f32[16,128]{1,0:T(8,128)}, u32[]{:S(2)}) copy-start(f32[16,128]{1,0:T(8,128)} %own_probes_ref.1) | copy-start | bytes 24580
  6.4 3.9 %collective-permute-start.1 = (f32[2,8,128]{2,1,0:T(8,128)S(1)}, f32[2,8,128]{2,1,0:T(8,128)S(1)}, u32[]{:S(2)}, u32[]{:S(2)}) collective-permute-start(f32[2,8,128]{2,1,0:T(8,128)S(1)} %pad_maximum_fusion.6), channel_id=1, source_target_pairs={{0,5},{1,4},{2,7},{3,6},{4,1},{5,0},{6,3},{7,2},{8,13},{9,12},{10,... | collective-permute-start | bytes 24584 | tf_op jit(solution)/shard_map/ppermute | solution.py:333
  8.4 3.3 %collective-permute-start.6 = (f32[2,16,128]{2,1,0:T(8,128)S(1)}, f32[2,16,128]{2,1,0:T(8,128)S(1)}, u32[]{:S(2)}, u32[]{:S(2)}) collective-permute-start(f32[2,16,128]{2,1,0:T(8,128)S(1)} %pad_maximum_fusion.4), channel_id=1, source_target_pairs={{0,5},{1,4},{2,7},{3,6},{4,1},{5,0},{6,3},{7,2},{8,13},{9,12},{10,... | collective-permute-start | bytes 49160 | tf_op jit(solution)/shard_map/ppermute | solution.py:333
  10.2 3.2 %collective-permute-start.2 = (f32[4,8,128]{2,1,0:T(8,128)S(1)}, f32[4,8,128]{2,1,0:T(8,128)S(1)}, u32[]{:S(2)}, u32[]{:S(2)}) collective-permute-start(f32[4,8,128]{2,1,0:T(8,128)S(1)} %pad_maximum_fusion.3), channel_id=1, source_target_pairs={{0,17},{1,2},{2,1},{3,18},{4,7},{5,20},{6,23},{7,4},{8,11},{9,24},... | collective-permute-start | bytes 49160 | tf_op jit(solution)/shard_map/ppermute | solution.py:333
  11.7 3.3 %collective-permute-start.7 = (f32[4,16,128]{2,1,0:T(8,128)S(1)}, f32[4,16,128]{2,1,0:T(8,128)S(1)}, u32[]{:S(2)}, u32[]{:S(2)}) collective-permute-start(f32[4,16,128]{2,1,0:T(8,128)S(1)} %pad_maximum_fusion.2), channel_id=1, source_target_pairs={{0,17},{1,2},{2,1},{3,18},{4,7},{5,20},{6,23},{7,4},{8,11},{9,24},... | collective-permute-start | bytes 98312 | tf_op jit(solution)/shard_map/ppermute | solution.py:333
  13.4 3.3 %collective-permute-start.3 = (f32[8,8,128]{2,1,0:T(8,128)S(1)}, f32[8,8,128]{2,1,0:T(8,128)S(1)}, u32[]{:S(2)}, u32[]{:S(2)}) collective-permute-start(f32[8,8,128]{2,1,0:T(8,128)S(1)} %pad_maximum_fusion.1), channel_id=1, source_target_pairs={{0,3},{1,16},{2,19},{3,0},{4,21},{5,6},{6,5},{7,22},{8,25},{9,10},... | collective-permute-start | bytes 98312 | tf_op jit(solution)/shard_map/ppermute | solution.py:333
  15.0 3.7 %collective-permute-start.8 = (f32[8,16,128]{2,1,0:T(8,128)S(1)}, f32[8,16,128]{2,1,0:T(8,128)S(1)}, u32[]{:S(2)}, u32[]{:S(2)}) collective-permute-start(f32[8,16,128]{2,1,0:T(8,128)S(1)} %pad_maximum_fusion), channel_id=1, source_target_pairs={{0,3},{1,16},{2,19},{3,0},{4,21},{5,6},{6,5},{7,22},{8,25},{9,10},... | collective-permute-start | bytes 196616 | tf_op jit(solution)/shard_map/ppermute | solution.py:333
  16.7 1.3 %collective-permute-start.4 = (f32[16,8,128]{2,1,0:T(8,128)S(1)}, f32[16,8,128]{2,1,0:T(8,128)S(1)}, u32[]{:S(2)}, u32[]{:S(2)}) collective-permute-start(f32[16,8,128]{2,1,0:T(8,128)S(1)} %constant_dynamic-update-slice_fusion.points_ref), channel_id=1, source_target_pairs={{0,1},{1,0},{2,3},{3,2},{4,5},{5,4},{6,7},{7,6},{8,9},{9,8},{10,11... | collective-permute-start | bytes 196616 | tf_op jit(solution)/shard_map/ppermute | solution.py:333
  18.7 3.3 %collective-permute-start.9 = (f32[16,16,128]{2,1,0:T(8,128)S(1)}, f32[16,16,128]{2,1,0:T(8,128)S(1)}, u32[]{:S(2)}, u32[]{:S(2)}) collective-permute-start(f32[16,16,128]{2,1,0:T(8,128)S(1)} %constant_dynamic-update-slice_fusion.5.probes_ref), channel_id=1, source_target_pairs={{0,1},{1,0},{2,3},{3,2},{4,5},{5,4},{6,7},{7,6},{8,9},{9,8},{10,11... | collective-permute-start | bytes 393224 | tf_op jit(solution)/shard_map/ppermute | solution.py:333

commit v6 on v4

--- a/solution.py
+++ b/solution.py
@@ -95,22 +95,32 @@
         ]
         left = jnp.concatenate([l_high, l_middle], 1)
     out = [jnp.zeros((8, 128), F32) for t in range(tiles)]
-    for j in range(BLOCK):
+    for j in range(0, BLOCK, 2):
         v, s = divmod(j, 8)
-        pivot = rows_of(cols[j][v], s)
-        inverse = 1.0 / pivot
-        out[v] = jnp.where(sub == s, rb[v] * lax.rsqrt(pivot), out[v])
-        coef = list(cols[j])
-        coef[v] = coef[v] - jnp.where(sub == s, 1.0, 0.0)
-        coef = [piece * inverse for piece in coef]
-        row_a, row_b = rows_of(ra[v], s), rows_of(rb[v], s)
+        one, two = cols[j], cols[j + 1]
+        top, side, end = rows_of(one[v], s), rows_of(one[v], s + 1), rows_of(two[v], s + 1)
+        det = top * end - side * side
+        inverse = 1.0 / det
+        row_a, next_a = rows_of(ra[v], s), rows_of(ra[v], s + 1)
+        row_b, next_b = rows_of(rb[v], s), rows_of(rb[v], s + 1)
+        root = lax.rsqrt(top)
+        out[v] = jnp.where(sub == s, row_b * root, out[v])
+        out[v] = jnp.where(
+            sub == s + 1, (top * next_b - side * row_b) * (root * lax.rsqrt(det)), out[v]
+        )
+        one, two = list(one), list(two)
+        one[v] = one[v] - jnp.where(sub == s, 1.0, 0.0)
+        two[v] = two[v] - jnp.where(sub == s + 1, 1.0, 0.0)
+        first_coef = [(x * end - y * side) * inverse for x, y in zip(one, two)]
+        next_coef = [(y * top - x * side) * inverse for x, y in zip(one, two)]
         for t in range(tiles):
-            ra[t] = ra[t] - coef[t] * row_a
-            rb[t] = rb[t] - coef[t] * row_b
-        for m in range(j + 1, BLOCK):
-            entry = rows_of(cols[m][v], s)
+            ra[t] = ra[t] - first_coef[t] * row_a - next_coef[t] * next_a
+            rb[t] = rb[t] - first_coef[t] * row_b - next_coef[t] * next_b
+        for m in range(j + 2, BLOCK):
+            entry, following = rows_of(cols[m][v], s), rows_of(cols[m][v], s + 1)
             for t in range(tiles):
-                cols[m][t] = cols[m][t] - coef[t] * entry
+                change = first_coef[t] * entry + next_coef[t] * following
+                cols[m][t] = cols[m][t] - change
     if first + tiles < len(a):
         for values, rows in ((a, ra), (b, rb)):
             sums = [[None, None] for u in range(tiles)]
@@ -274,11 +284,9 @@
     b = [values[i : i + 8, size:] for i in range(0, size, 8)]
 
     wide, narrow = wide_ref[...], narrow_ref[...]
-    chunks = range(0, blocks, CHUNK) if blocks <= UNROLL else range(0)
-    if blocks > UNROLL:
-        wide, narrow = over(
-            blocks, CHUNK, (wide, narrow), lambda c, i: work.add(*c, there_ref, i)
-        )
+    wide, narrow = over(blocks, CHUNK, (wide, narrow), lambda c, i: work.add(*c, there_ref, i))
+    total = gathered_sum(wide, narrow) + there_ref[blocks, : work.vectors, :]
+    total_ref[...] = total + work.noise * own_ref[dims:, :]
     steps = size // BLOCK
     copies = []
     for step in range(steps):
@@ -288,11 +296,7 @@
             pltpu.make_async_copy(rows_ref.at[rows, :], panel_ref.at[rows, :], sems.at[step])
         )
         copies[-1].start()
-        for index in chunks[step::steps]:
-            wide, narrow = work.add(wide, narrow, there_ref, index)
-        if step == min(len(chunks), steps - 1):
-            total = gathered_sum(wide, narrow) + there_ref[blocks, : work.vectors, :]
-            total_ref[...] = total + work.noise * own_ref[dims:, :]
+        if step == steps // 2:
             copies.append(pltpu.make_async_copy(total_ref, product_ref, total_sem))
             copies[-1].start()
     for copy in copies:
@@ -374,23 +378,23 @@
 
     def local(inputs, probes, lengths, noise, pivots):
         rows = inputs.shape[1]
-        own = jnp.concatenate([inputs, probes], 0)
         layout = (masks, count, members)
         last = len(masks[0]) - 1
-        here = own[None]
-        for step in range(last - 1):
-            if step == 1:
-                side = jnp.concatenate(
-                    [
-                        jnp.broadcast_to((SCALE / lengths)[:, None], inputs.shape),
-                        jnp.broadcast_to(noise[:, None], (1, rows)),
-                        pivots.astype(F32)[None, :],
-                    ],
-                    0,
-                )
+        own = jnp.concatenate([inputs, probes], 0)
+        came = [swap(inputs, 0), swap(probes, 0)]
+        here = jnp.stack([own, jnp.concatenate(came, 0)])
+        side = jnp.concatenate(
+            [
+                jnp.broadcast_to((SCALE / lengths)[:, None], inputs.shape),
+                jnp.broadcast_to(noise[:, None], (1, rows)),
+                pivots.astype(F32)[None, :],
+            ],
+            0,
+        )
+        for step in range(1, last - 1):
+            here = jnp.concatenate([here, swap(here, step)], 0)
             if step == 1:
                 mate = swap(lax.optimization_barrier((own, here))[0], last)
-            here = jnp.concatenate([here, swap(here, step)], 0)
         arrived = swap(here, last - 1)
         *carry, parcel = early(layout, side, own, mate, here)
         arrived, parcel = lax.optimization_barrier((arrived, parcel))

time: 23.1 us -> 25.2 us (1.091)
  waiting for transfers between devices: 5.16 us -> 6.89 us
  other arithmetic: 0.18 us -> 0.83 us
    ppermute x6 -> x7, waiting for transfers between devices: 5.16 us -> 6.89 us  [swap(): return lax.ppermute(value, ('blk', 'grp'), pairs)]
    div x1, other arithmetic: 0.01 us -> 0.66 us  [local(): SCALE / lengths]
    ppermute x6 -> x7, starting transfers between devices: 9.67 us -> 9.54 us  [swap(): return lax.ppermute(value, ('blk', 'grp'), pairs)]
    unnamed x7 -> x5, local copies, waits for them, and re-layouts: 0.71 us -> 0.7 us
  transfers between devices with their start and end apart: 6 -> 7, of which waited for: 5 -> 6; matrix products, arithmetic and copies ran while one was open for 1% -> 6% of each run, Pallas kernels for 8% -> 7%
where the time goes in v6:
time: 25.2 us; the launch traced here: 25 us
  starting transfers between devices  9.54 us (38%)
  waiting for transfers between devices  6.89 us (27%)
  Pallas kernels  5.74 us (23%)
  between operations  1.32 us (5%)
  other arithmetic  0.83 us (3%)
  local copies, waits for them, and re-layouts  0.7 us (3%)
    ppermute x7, starting transfers between devices, swap(): return lax.ppermute(value, ('blk', 'grp'), pairs)  9.54 us
    ppermute x7, waiting for transfers between devices, swap(): return lax.ppermute(value, ('blk', 'grp'), pairs)  6.89 us
    pallas_call x1, Pallas kernels, finish(): pl.pallas_call(functools.partial(last_body, layout), out_shape=(jax.Shape...  3.95 us
    pallas_call x1, Pallas kernels, early(): pl.pallas_call(functools.partial(early_body, layout), out_shape=sums(side...  1.04 us
    pallas_call x1, Pallas kernels, middle(): pl.pallas_call(functools.partial(middle_body, layout, place), out_shape=s...  0.74 us
    unnamed x5, local copies, waits for them, and re-layouts  0.7 us
    div x1, other arithmetic, local(): SCALE / lengths  0.66 us
  transfers between devices with their start and end apart: 7, of which 6 were waited for; matrix products, arithmetic and copies ran while one was open for 6% of the time, Pallas kernels for 7%

profile of v6, /device:TPU:0, one launch (start us, length us, event | category | flops | bytes accessed | tf_op | source)
XLA Modules:
  0.0 25.0 jit_solution(5863299402500437744)
XLA Ops:
  0.6 0.0 copy-start
  0.6 3.5 %collective-permute-start = (f32[8,128]{1,0:T(8,128)}, f32[8,128]{1,0:T(8,128)S(1)}, u32[]{:S(2)}, u32[]{:S(2)}) collective-permute-start(f32[8,128]{1,0:T(8,128)} %param.5), channel_id=1, source_target_pairs={{0,9},{1,8},{2,11},{3,10},{4,13},{5,12},{6,15},{7,14},{8,1},{9,0},... | collective-permute-start | bytes 12296 | tf_op jit(solution)/shard_map/ppermute | solution.py:377
  4.2 0.1 collective-permute-start.1
  4.3 0.7 %constant_dynamic-update-slice_fusion.1 = f32[24,128]{1,0:T(8,128)S(1)} fusion(f32[8,128]{1,0:T(8,128)} %param.5), kind=kLoop, calls=%fused_computation.7 | loop fusion | bytes 8192
  4.9 0.7 %broadcast_divide_fusion = f32[8]{0:T(128)S(1)} fusion(f32[8]{0:T(128)} %param.7), kind=kLoop, calls=%fused_computation.10 | loop fusion | flops 8 | bytes 64 | tf_op jit(solution)/shard_map/div | solution.py:388
  5.6 0.0 copy-done
  5.6 0.1 collective-permute-done
  5.7 2.6 %collective-permute-done.1 = f32[16,128]{1,0:T(8,128)S(1)} collective-permute-done((f32[16,128]{1,0:T(8,128)}, f32[16,128]{1,0:T(8,128)S(1)}, u32[]{:S(2)}, u32[]{:S(2)}) %collective-permute-start.1) | collective-permute-done | bytes 8224 | tf_op jit(solution)/shard_map/ppermute | solution.py:377
  8.4 0.0 copy-start.1
  8.4 1.9 %collective-permute-start.2 = (f32[2,24,128]{2,1,0:T(8,128)S(1)}, f32[2,24,128]{2,1,0:T(8,128)S(1)}, u32[]{:S(2)}, u32[]{:S(2)}) collective-permute-start(f32[2,24,128]{2,1,0:T(8,128)S(1)} %pad_maximum_fusion.3), channel_id=1, source_target_pairs={{0,5},{1,4},{2,7},{3,6},{4,1},{5,0},{6,3},{7,2},{8,13},{9,12},{10,... | collective-permute-start | bytes 73736 | tf_op jit(solution)/shard_map/ppermute | solution.py:377
  10.3 0.0 copy-done.1
  11.0 0.9 %collective-permute-done.2 = f32[2,24,128]{2,1,0:T(8,128)S(1)} collective-permute-done((f32[2,24,128]{2,1,0:T(8,128)S(1)}, f32[2,24,128]{2,1,0:T(8,128)S(1)}, u32[]{:S(2)}, u32[]{:S(2)}) %collective-permute-start.2) | collective-permute-done | bytes 24608 | tf_op jit(solution)/shard_map/ppermute | solution.py:377
  11.8 1.7 %collective-permute-start.3 = (f32[4,24,128]{2,1,0:T(8,128)S(1)}, f32[4,24,128]{2,1,0:T(8,128)S(1)}, u32[]{:S(2)}, u32[]{:S(2)}) collective-permute-start(f32[4,24,128]{2,1,0:T(8,128)S(1)} %pad_maximum_fusion.2), channel_id=1, source_target_pairs={{0,17},{1,2},{2,1},{3,18},{4,7},{5,20},{6,23},{7,4},{8,11},{9,24},... | collective-permute-start | bytes 147464 | tf_op jit(solution)/shard_map/ppermute | solution.py:377
  13.5 0.1 pad_maximum_fusion.5
  13.6 0.0 collective-permute-start.5
  13.6 1.8 %collective-permute-done.3 = f32[4,24,128]{2,1,0:T(8,128)S(1)} collective-permute-done((f32[4,24,128]{2,1,0:T(8,128)S(1)}, f32[4,24,128]{2,1,0:T(8,128)S(1)}, u32[]{:S(2)}, u32[]{:S(2)}) %collective-permute-start.3) | collective-permute-done | bytes 49184 | tf_op jit(solution)/shard_map/ppermute | solution.py:377
  15.4 1.7 %collective-permute-start.4 = (f32[8,24,128]{2,1,0:T(8,128)S(1)}, f32[8,24,128]{2,1,0:T(8,128)S(1)}, u32[]{:S(2)}, u32[]{:S(2)}) collective-permute-start(f32[8,24,128]{2,1,0:T(8,128)S(1)} %pad_maximum_fusion.1.part_ref), channel_id=1, source_target_pairs={{0,3},{1,16},{2,19},{3,0},{4,21},{5,6},{6,5},{7,22},{8,25},{9,10},... | collective-permute-start | bytes 294920 | tf_op jit(solution)/shard_map/ppermute | solution.py:377
  17.1 0.1 pad_maximum_fusion.4.side_ref
  17.1 0.0 collective-permute-done.5.mate_ref
  17.1 1.0 %shard_map.68 = (f32[128,32]{1,0:T(8,128)S(1)}, f32[128,16]{1,0:T(8,128)S(1)}, f32[24,128]{1,0:T(8,128)S(1)}, f32[2,24,128]{2,1,0:T(8,128)S(1)}) custom-call(f32[10,128]{1,0:T(8,128)S(1)} %pad_maximum_fusion.4.side_ref, f32[24,128]{1,0:T(8,128)S(1)} %constant_dynamic-update-slice_fusion.own_ref, f32[24,128]{1,0:T(8,128)S(1)} %collective-permute-done.5.mate_ref, ...), custom_call_target="tpu_custom_call" | custom-call | flops 15728640 | bytes 102400 | tf_op jit(solution)/shard_map/pallas_call | solution.py:327
  18.2 1.3 %collective-permute-done.4.part_ref = f32[8,24,128]{2,1,0:T(8,128)S(1)} collective-permute-done((f32[8,24,128]{2,1,0:T(8,128)S(1)}, f32[8,24,128]{2,1,0:T(8,128)S(1)}, u32[]{:S(2)}, u32[]{:S(2)}) %collective-permute-start.4) | collective-permute-done | bytes 98336 | tf_op jit(solution)/shard_map/ppermute | solution.py:377
  19.5 0.6 %collective-permute-start.6 = (f32[10,24,128]{2,1,0:T(8,128)S(1)}, f32[10,24,128]{2,1,0:T(8,128)S(1)}, u32[]{:S(2)}, u32[]{:S(2)}) collective-permute-start(f32[10,24,128]{2,1,0:T(8,128)S(1)} %pad_maximum_fusion), channel_id=1, source_target_pairs={{0,1},{1,0},{2,3},{3,2},{4,5},{5,4},{6,7},{7,6},{8,9},{9,8},{10,11... | collective-permute-start | bytes 368648 | tf_op jit(solution)/shard_map/ppermute | solution.py:377
  20.1 0.7 %shard_map.69 = (f32[128,32]{1,0:T(8,128)S(1)}, f32[128,16]{1,0:T(8,128)S(1)}, f32[24,128]{1,0:T(8,128)S(1)}) custom-call(f32[10,128]{1,0:T(8,128)S(1)} %pad_maximum_fusion.4.side_ref, f32[24,128]{1,0:T(8,128)S(1)} %constant_dynamic-update-slice_fusion.own_ref, f32[8,24,128]{2,1,0:T(8,128)S(1)} %collective-permute-done.4.part_ref, ...), custom_call_target="tpu_custom_call" | custom-call | flops 7864320 | bytes 102400 | tf_op jit(solution)/shard_map/pallas_call | solution.py:339
  20.8 0.2 collective-permute-done.6.there_ref
  21.1 4.0 %shard_map.70 = (f32[128,128]{1,0:T(8,128)}, f32[16,128]{1,0:T(8,128)}) custom-call(f32[10,128]{1,0:T(8,128)S(1)} %pad_maximum_fusion.4.side_ref, f32[24,128]{1,0:T(8,128)S(1)} %constant_dynamic-update-slice_fusion.own_ref, f32[10,24,128]{2,1,0:T(8,128)S(1)} %collective-permute-done.6.there_ref, f32[128,32]{1,0:T(8,128)S(1)} %get-tuple-element.19.wide_ref, ...), custom_call_target="tpu_custom_call" | custom-call | tf_op jit(solution)/shard_map/pallas_call | solution.py:352
  (7 shorter events, 0.0 us)
Async XLA Ops:
  0.6 5.0 %copy-start = (f32[16,128]{1,0:T(8,128)S(1)}, f32[16,128]{1,0:T(8,128)}, u32[]{:S(2)}) copy-start(f32[16,128]{1,0:T(8,128)} %param.6) | copy-start | bytes 24580
  0.6 5.1 %collective-permute-start = (f32[8,128]{1,0:T(8,128)}, f32[8,128]{1,0:T(8,128)S(1)}, u32[]{:S(2)}, u32[]{:S(2)}) collective-permute-start(f32[8,128]{1,0:T(8,128)} %param.5), channel_id=1, source_target_pairs={{0,9},{1,8},{2,11},{3,10},{4,13},{5,12},{6,15},{7,14},{8,1},{9,0},... | collective-permute-start | bytes 12296 | tf_op jit(solution)/shard_map/ppermute | solution.py:377
  4.2 4.2 %collective-permute-start.1 = (f32[16,128]{1,0:T(8,128)}, f32[16,128]{1,0:T(8,128)S(1)}, u32[]{:S(2)}, u32[]{:S(2)}) collective-permute-start(f32[16,128]{1,0:T(8,128)} %param.6), channel_id=1, source_target_pairs={{0,9},{1,8},{2,11},{3,10},{4,13},{5,12},{6,15},{7,14},{8,1},{9,0},... | collective-permute-start | bytes 24584 | tf_op jit(solution)/shard_map/ppermute | solution.py:377
  8.4 1.9 %copy-start.1 = (s32[128]{0:T(128)S(1)}, s32[128]{0:T(128)}, u32[]{:S(2)}) copy-start(s32[128]{0:T(128)} %param.9) | copy-start | bytes 1540
  8.4 3.4 %collective-permute-start.2 = (f32[2,24,128]{2,1,0:T(8,128)S(1)}, f32[2,24,128]{2,1,0:T(8,128)S(1)}, u32[]{:S(2)}, u32[]{:S(2)}) collective-permute-start(f32[2,24,128]{2,1,0:T(8,128)S(1)} %pad_maximum_fusion.3), channel_id=1, source_target_pairs={{0,5},{1,4},{2,7},{3,6},{4,1},{5,0},{6,3},{7,2},{8,13},{9,12},{10,... | collective-permute-start | bytes 73736 | tf_op jit(solution)/shard_map/ppermute | solution.py:377
  11.8 3.5 %collective-permute-start.3 = (f32[4,24,128]{2,1,0:T(8,128)S(1)}, f32[4,24,128]{2,1,0:T(8,128)S(1)}, u32[]{:S(2)}, u32[]{:S(2)}) collective-permute-start(f32[4,24,128]{2,1,0:T(8,128)S(1)} %pad_maximum_fusion.2), channel_id=1, source_target_pairs={{0,17},{1,2},{2,1},{3,18},{4,7},{5,20},{6,23},{7,4},{8,11},{9,24},... | collective-permute-start | bytes 147464 | tf_op jit(solution)/shard_map/ppermute | solution.py:377
  13.6 3.6 %collective-permute-start.5 = (f32[24,128]{1,0:T(8,128)S(1)}, f32[24,128]{1,0:T(8,128)S(1)}, u32[]{:S(2)}, u32[]{:S(2)}) collective-permute-start(f32[24,128]{1,0:T(8,128)S(1)} %constant_dynamic-update-slice_fusion.own_ref), channel_id=1, source_target_pairs={{0,1},{1,0},{2,3},{3,2},{4,5},{5,4},{6,7},{7,6},{8,9},{9,8},{10,11... | collective-permute-start | bytes 36872 | tf_op jit(solution)/shard_map/ppermute | solution.py:377
  15.4 4.1 %collective-permute-start.4 = (f32[8,24,128]{2,1,0:T(8,128)S(1)}, f32[8,24,128]{2,1,0:T(8,128)S(1)}, u32[]{:S(2)}, u32[]{:S(2)}) collective-permute-start(f32[8,24,128]{2,1,0:T(8,128)S(1)} %pad_maximum_fusion.1.part_ref), channel_id=1, source_target_pairs={{0,3},{1,16},{2,19},{3,0},{4,21},{5,6},{6,5},{7,22},{8,25},{9,10},... | collective-permute-start | bytes 294920 | tf_op jit(solution)/shard_map/ppermute | solution.py:377
  19.5 1.6 %collective-permute-start.6 = (f32[10,24,128]{2,1,0:T(8,128)S(1)}, f32[10,24,128]{2,1,0:T(8,128)S(1)}, u32[]{:S(2)}, u32[]{:S(2)}) collective-permute-start(f32[10,24,128]{2,1,0:T(8,128)S(1)} %pad_maximum_fusion), channel_id=1, source_target_pairs={{0,1},{1,0},{2,3},{3,2},{4,5},{5,4},{6,7},{7,6},{8,9},{9,8},{10,11... | collective-permute-start | bytes 368648 | tf_op jit(solution)/shard_map/ppermute | solution.py:377

commit v7 on v6

--- a/solution.py
+++ b/solution.py
@@ -378,23 +378,23 @@
 
     def local(inputs, probes, lengths, noise, pivots):
         rows = inputs.shape[1]
+        own = jnp.concatenate([inputs, probes], 0)
         layout = (masks, count, members)
         last = len(masks[0]) - 1
-        own = jnp.concatenate([inputs, probes], 0)
-        came = [swap(inputs, 0), swap(probes, 0)]
-        here = jnp.stack([own, jnp.concatenate(came, 0)])
-        side = jnp.concatenate(
-            [
-                jnp.broadcast_to((SCALE / lengths)[:, None], inputs.shape),
-                jnp.broadcast_to(noise[:, None], (1, rows)),
-                pivots.astype(F32)[None, :],
-            ],
-            0,
-        )
-        for step in range(1, last - 1):
-            here = jnp.concatenate([here, swap(here, step)], 0)
+        here = own[None]
+        for step in range(last - 1):
+            if step == 1:
+                side = jnp.concatenate(
+                    [
+                        jnp.broadcast_to((SCALE / lengths)[:, None], inputs.shape),
+                        jnp.broadcast_to(noise[:, None], (1, rows)),
+                        pivots.astype(F32)[None, :],
+                    ],
+                    0,
+                )
             if step == 1:
                 mate = swap(lax.optimization_barrier((own, here))[0], last)
+            here = jnp.concatenate([here, swap(here, step)], 0)
         arrived = swap(here, last - 1)
         *carry, parcel = early(layout, side, own, mate, here)
         arrived, parcel = lax.optimization_barrier((arrived, parcel))

time: 25.2 us -> 23 us (0.913)
  waiting for transfers between devices: 6.89 us -> 5.16 us
  other arithmetic: 0.83 us -> 0.18 us
    ppermute x7 -> x6, waiting for transfers between devices: 6.89 us -> 5.16 us  [swap(): return lax.ppermute(value, ('blk', 'grp'), pairs)]
    div x1, other arithmetic: 0.66 us -> 0.01 us  [local(): SCALE / lengths]
    ppermute x7 -> x6, starting transfers between devices: 9.54 us -> 9.67 us  [swap(): return lax.ppermute(value, ('blk', 'grp'), pairs)]
    unnamed x5 -> x7, local copies, waits for them, and re-layouts: 0.7 us -> 0.71 us
  transfers between devices with their start and end apart: 7 -> 6, of which waited for: 6 -> 5; matrix products, arithmetic and copies ran while one was open for 6% -> 1% of each run, Pallas kernels for 7% -> 8%
where the time goes in v7:
time: 23 us; the launch traced here: 22.8 us
  starting transfers between devices  9.67 us (42%)
  Pallas kernels  5.74 us (25%)
  waiting for transfers between devices  5.16 us (22%)
  between operations  1.32 us (6%)
  local copies, waits for them, and re-layouts  0.71 us (3%)
    ppermute x6, starting transfers between devices, swap(): return lax.ppermute(value, ('blk', 'grp'), pairs)  9.67 us
    ppermute x6, waiting for transfers between devices, swap(): return lax.ppermute(value, ('blk', 'grp'), pairs)  5.16 us
    pallas_call x1, Pallas kernels, finish(): pl.pallas_call(functools.partial(last_body, layout), out_shape=(jax.Shape...  3.96 us
    pallas_call x1, Pallas kernels, early(): pl.pallas_call(functools.partial(early_body, layout), out_shape=sums(side...  1.04 us
    pallas_call x1, Pallas kernels, middle(): pl.pallas_call(functools.partial(middle_body, layout, place), out_shape=s...  0.74 us
    unnamed x7, local copies, waits for them, and re-layouts  0.71 us
  transfers between devices with their start and end apart: 6, of which 5 were waited for; matrix products, arithmetic and copies ran while one was open for 1% of the time, Pallas kernels for 8%

profile of v7, /device:TPU:0, one launch (start us, length us, event | category | flops | bytes accessed | tf_op | source)
XLA Modules:
  0.0 22.8 jit_solution(8438586489499784590)
XLA Ops:
  0.6 0.0 copy-start
  0.6 0.7 %constant_dynamic-update-slice_fusion.1 = f32[24,128]{1,0:T(8,128)S(1)} fusion(f32[8,128]{1,0:T(8,128)} %param.5), kind=kLoop, calls=%fused_computation.6 | loop fusion | bytes 8192
  1.3 0.0 copy-done
  1.3 0.0 copy-start.1
  1.3 3.5 %collective-permute-start = (f32[1,24,128]{2,1,0:T(8,128)S(1)}, f32[1,24,128]{2,1,0:T(8,128)S(1)}, u32[]{:S(2)}, u32[]{:S(2)}) collective-permute-start(f32[1,24,128]{2,1,0:T(8,128)S(1)} %bitcast.4), channel_id=1, source_target_pairs={{0,9},{1,8},{2,11},{3,10},{4,13},{5,12},{6,15},{7,14},{8,1},{9,0},... | collective-permute-start | bytes 36872 | tf_op jit(solution)/shard_map/ppermute | solution.py:377
  4.8 0.0 copy-done.1
  4.8 0.0 copy-start.2
  4.8 1.4 %collective-permute-done = f32[1,24,128]{2,1,0:T(8,128)S(1)} collective-permute-done((f32[1,24,128]{2,1,0:T(8,128)S(1)}, f32[1,24,128]{2,1,0:T(8,128)S(1)}, u32[]{:S(2)}, u32[]{:S(2)}) %collective-permute-start) | collective-permute-done | bytes 12320 | tf_op jit(solution)/shard_map/ppermute | solution.py:377
  6.2 1.9 %collective-permute-start.1 = (f32[2,24,128]{2,1,0:T(8,128)S(1)}, f32[2,24,128]{2,1,0:T(8,128)S(1)}, u32[]{:S(2)}, u32[]{:S(2)}) collective-permute-start(f32[2,24,128]{2,1,0:T(8,128)S(1)} %pad_maximum_fusion.3), channel_id=1, source_target_pairs={{0,5},{1,4},{2,7},{3,6},{4,1},{5,0},{6,3},{7,2},{8,13},{9,12},{10,... | collective-permute-start | bytes 73736 | tf_op jit(solution)/shard_map/ppermute | solution.py:377
  8.1 0.0 copy-done.2
  8.8 0.9 %collective-permute-done.1 = f32[2,24,128]{2,1,0:T(8,128)S(1)} collective-permute-done((f32[2,24,128]{2,1,0:T(8,128)S(1)}, f32[2,24,128]{2,1,0:T(8,128)S(1)}, u32[]{:S(2)}, u32[]{:S(2)}) %collective-permute-start.1) | collective-permute-done | bytes 24608 | tf_op jit(solution)/shard_map/ppermute | solution.py:377
  9.6 1.7 %collective-permute-start.2 = (f32[4,24,128]{2,1,0:T(8,128)S(1)}, f32[4,24,128]{2,1,0:T(8,128)S(1)}, u32[]{:S(2)}, u32[]{:S(2)}) collective-permute-start(f32[4,24,128]{2,1,0:T(8,128)S(1)} %pad_maximum_fusion.2), channel_id=1, source_target_pairs={{0,17},{1,2},{2,1},{3,18},{4,7},{5,20},{6,23},{7,4},{8,11},{9,24},... | collective-permute-start | bytes 147464 | tf_op jit(solution)/shard_map/ppermute | solution.py:377
  11.3 0.1 pad_maximum_fusion.5
  11.4 0.4 %collective-permute-start.4 = (f32[24,128]{1,0:T(8,128)S(1)}, f32[24,128]{1,0:T(8,128)S(1)}, u32[]{:S(2)}, u32[]{:S(2)}) collective-permute-start(f32[24,128]{1,0:T(8,128)S(1)} %constant_dynamic-update-slice_fusion.own_ref), channel_id=1, source_target_pairs={{0,1},{1,0},{2,3},{3,2},{4,5},{5,4},{6,7},{7,6},{8,9},{9,8},{10,11... | collective-permute-start | bytes 36872 | tf_op jit(solution)/shard_map/ppermute | solution.py:377
  11.8 1.4 %collective-permute-done.2 = f32[4,24,128]{2,1,0:T(8,128)S(1)} collective-permute-done((f32[4,24,128]{2,1,0:T(8,128)S(1)}, f32[4,24,128]{2,1,0:T(8,128)S(1)}, u32[]{:S(2)}, u32[]{:S(2)}) %collective-permute-start.2) | collective-permute-done | bytes 49184 | tf_op jit(solution)/shard_map/ppermute | solution.py:377
  13.2 1.7 %collective-permute-start.3 = (f32[8,24,128]{2,1,0:T(8,128)S(1)}, f32[8,24,128]{2,1,0:T(8,128)S(1)}, u32[]{:S(2)}, u32[]{:S(2)}) collective-permute-start(f32[8,24,128]{2,1,0:T(8,128)S(1)} %pad_maximum_fusion.1.part_ref), channel_id=1, source_target_pairs={{0,3},{1,16},{2,19},{3,0},{4,21},{5,6},{6,5},{7,22},{8,25},{9,10},... | collective-permute-start | bytes 294920 | tf_op jit(solution)/shard_map/ppermute | solution.py:377
  14.9 0.1 pad_maximum_fusion.4.side_ref
  14.9 0.0 collective-permute-done.4.mate_ref
  14.9 1.0 %shard_map.68 = (f32[128,32]{1,0:T(8,128)S(1)}, f32[128,16]{1,0:T(8,128)S(1)}, f32[24,128]{1,0:T(8,128)S(1)}, f32[2,24,128]{2,1,0:T(8,128)S(1)}) custom-call(f32[10,128]{1,0:T(8,128)S(1)} %pad_maximum_fusion.4.side_ref, f32[24,128]{1,0:T(8,128)S(1)} %constant_dynamic-update-slice_fusion.own_ref, f32[24,128]{1,0:T(8,128)S(1)} %collective-permute-done.4.mate_ref, ...), custom_call_target="tpu_custom_call" | custom-call | flops 15728640 | bytes 102400 | tf_op jit(solution)/shard_map/pallas_call | solution.py:327
  16.0 1.3 %collective-permute-done.3.part_ref = f32[8,24,128]{2,1,0:T(8,128)S(1)} collective-permute-done((f32[8,24,128]{2,1,0:T(8,128)S(1)}, f32[8,24,128]{2,1,0:T(8,128)S(1)}, u32[]{:S(2)}, u32[]{:S(2)}) %collective-permute-start.3) | collective-permute-done | bytes 98336 | tf_op jit(solution)/shard_map/ppermute | solution.py:377
  17.3 0.6 %collective-permute-start.5 = (f32[10,24,128]{2,1,0:T(8,128)S(1)}, f32[10,24,128]{2,1,0:T(8,128)S(1)}, u32[]{:S(2)}, u32[]{:S(2)}) collective-permute-start(f32[10,24,128]{2,1,0:T(8,128)S(1)} %pad_maximum_fusion), channel_id=1, source_target_pairs={{0,1},{1,0},{2,3},{3,2},{4,5},{5,4},{6,7},{7,6},{8,9},{9,8},{10,11... | collective-permute-start | bytes 368648 | tf_op jit(solution)/shard_map/ppermute | solution.py:377
  17.8 0.7 %shard_map.69 = (f32[128,32]{1,0:T(8,128)S(1)}, f32[128,16]{1,0:T(8,128)S(1)}, f32[24,128]{1,0:T(8,128)S(1)}) custom-call(f32[10,128]{1,0:T(8,128)S(1)} %pad_maximum_fusion.4.side_ref, f32[24,128]{1,0:T(8,128)S(1)} %constant_dynamic-update-slice_fusion.own_ref, f32[8,24,128]{2,1,0:T(8,128)S(1)} %collective-permute-done.3.part_ref, ...), custom_call_target="tpu_custom_call" | custom-call | flops 7864320 | bytes 102400 | tf_op jit(solution)/shard_map/pallas_call | solution.py:339
  18.6 0.2 %collective-permute-done.5.there_ref = f32[10,24,128]{2,1,0:T(8,128)S(1)} collective-permute-done((f32[10,24,128]{2,1,0:T(8,128)S(1)}, f32[10,24,128]{2,1,0:T(8,128)S(1)}, u32[]{:S(2)}, u32[]{:S(2)}) %collective-permute-start.5) | collective-permute-done | bytes 122912 | tf_op jit(solution)/shard_map/ppermute | solution.py:377
  18.8 4.0 %shard_map.70 = (f32[128,128]{1,0:T(8,128)}, f32[16,128]{1,0:T(8,128)}) custom-call(f32[10,128]{1,0:T(8,128)S(1)} %pad_maximum_fusion.4.side_ref, f32[24,128]{1,0:T(8,128)S(1)} %constant_dynamic-update-slice_fusion.own_ref, f32[10,24,128]{2,1,0:T(8,128)S(1)} %collective-permute-done.5.there_ref, f32[128,32]{1,0:T(8,128)S(1)} %get-tuple-element.19.wide_ref, ...), custom_call_target="tpu_custom_call" | custom-call | tf_op jit(solution)/shard_map/pallas_call | solution.py:352
  (7 shorter events, 0.0 us)
Async XLA Ops:
  0.6 0.7 %copy-start = (f32[16,128]{1,0:T(8,128)S(1)}, f32[16,128]{1,0:T(8,128)}, u32[]{:S(2)}) copy-start(f32[16,128]{1,0:T(8,128)} %param.6) | copy-start | bytes 24580
  1.3 3.5 %copy-start.1 = (f32[8]{0:T(128)S(1)}, f32[8]{0:T(128)}, u32[]{:S(2)}) copy-start(f32[8]{0:T(128)} %param.7) | copy-start | bytes 100
  1.3 4.9 %collective-permute-start = (f32[1,24,128]{2,1,0:T(8,128)S(1)}, f32[1,24,128]{2,1,0:T(8,128)S(1)}, u32[]{:S(2)}, u32[]{:S(2)}) collective-permute-start(f32[1,24,128]{2,1,0:T(8,128)S(1)} %bitcast.4), channel_id=1, source_target_pairs={{0,9},{1,8},{2,11},{3,10},{4,13},{5,12},{6,15},{7,14},{8,1},{9,0},... | collective-permute-start | bytes 36872 | tf_op jit(solution)/shard_map/ppermute | solution.py:377
  4.8 3.3 %copy-start.2 = (s32[128]{0:T(128)S(1)}, s32[128]{0:T(128)}, u32[]{:S(2)}) copy-start(s32[128]{0:T(128)} %param.9) | copy-start | bytes 1540
  6.2 3.4 %collective-permute-start.1 = (f32[2,24,128]{2,1,0:T(8,128)S(1)}, f32[2,24,128]{2,1,0:T(8,128)S(1)}, u32[]{:S(2)}, u32[]{:S(2)}) collective-permute-start(f32[2,24,128]{2,1,0:T(8,128)S(1)} %pad_maximum_fusion.3), channel_id=1, source_target_pairs={{0,5},{1,4},{2,7},{3,6},{4,1},{5,0},{6,3},{7,2},{8,13},{9,12},{10,... | collective-permute-start | bytes 73736 | tf_op jit(solution)/shard_map/ppermute | solution.py:377
  9.6 3.5 %collective-permute-start.2 = (f32[4,24,128]{2,1,0:T(8,128)S(1)}, f32[4,24,128]{2,1,0:T(8,128)S(1)}, u32[]{:S(2)}, u32[]{:S(2)}) collective-permute-start(f32[4,24,128]{2,1,0:T(8,128)S(1)} %pad_maximum_fusion.2), channel_id=1, source_target_pairs={{0,17},{1,2},{2,1},{3,18},{4,7},{5,20},{6,23},{7,4},{8,11},{9,24},... | collective-permute-start | bytes 147464 | tf_op jit(solution)/shard_map/ppermute | solution.py:377
  11.4 3.6 %collective-permute-start.4 = (f32[24,128]{1,0:T(8,128)S(1)}, f32[24,128]{1,0:T(8,128)S(1)}, u32[]{:S(2)}, u32[]{:S(2)}) collective-permute-start(f32[24,128]{1,0:T(8,128)S(1)} %constant_dynamic-update-slice_fusion.own_ref), channel_id=1, source_target_pairs={{0,1},{1,0},{2,3},{3,2},{4,5},{5,4},{6,7},{7,6},{8,9},{9,8},{10,11... | collective-permute-start | bytes 36872 | tf_op jit(solution)/shard_map/ppermute | solution.py:377
  13.2 4.1 %collective-permute-start.3 = (f32[8,24,128]{2,1,0:T(8,128)S(1)}, f32[8,24,128]{2,1,0:T(8,128)S(1)}, u32[]{:S(2)}, u32[]{:S(2)}) collective-permute-start(f32[8,24,128]{2,1,0:T(8,128)S(1)} %pad_maximum_fusion.1.part_ref), channel_id=1, source_target_pairs={{0,3},{1,16},{2,19},{3,0},{4,21},{5,6},{6,5},{7,22},{8,25},{9,10},... | collective-permute-start | bytes 294920 | tf_op jit(solution)/shard_map/ppermute | solution.py:377
  17.3 1.5 %collective-permute-start.5 = (f32[10,24,128]{2,1,0:T(8,128)S(1)}, f32[10,24,128]{2,1,0:T(8,128)S(1)}, u32[]{:S(2)}, u32[]{:S(2)}) collective-permute-start(f32[10,24,128]{2,1,0:T(8,128)S(1)} %pad_maximum_fusion), channel_id=1, source_target_pairs={{0,1},{1,0},{2,3},{3,2},{4,5},{5,4},{6,7},{7,6},{8,9},{9,8},{10,11... | collective-permute-start | bytes 368648 | tf_op jit(solution)/shard_map/ppermute | solution.py:377

commit v8 on v7

--- a/solution.py
+++ b/solution.py
@@ -13,8 +13,8 @@
 LN2 = math.log(2.0)
 SCALE = math.sqrt(5.0) / LN2
 BLOCK = 16
-CHUNK = 4
-PICK = 2
+CHUNK = 8
+PICK = 4
 UNROLL = 32
 
 
@@ -123,16 +123,11 @@
                 cols[m][t] = cols[m][t] - change
     if first + tiles < len(a):
         for values, rows in ((a, ra), (b, rb)):
-            sums = [[None, None] for u in range(tiles)]
             for j in range(BLOCK):
                 row = rows_of(rows[j // 8], j % 8)
                 for u in range(tiles):
-                    term = below[j][u] * row
-                    before = sums[u][j % 2]
-                    sums[u][j % 2] = term if before is None else before + term
-            for u in range(tiles):
-                at = first + tiles + u
-                values[at] = values[at] - (sums[u][0] + sums[u][1])
+                    at = first + tiles + u
+                    values[at] = values[at] - below[j][u] * row
     if later < len(a):
         solved = jnp.concatenate([jnp.concatenate(ra, 0), jnp.concatenate(rb, 0)], 1)
 

time: 23 us -> 22.9 us (level)
  Pallas kernels: 5.74 us -> 5.41 us
  transfers between devices with their start and end apart: 6 -> 6, of which waited for: 5 -> 5; matrix products, arithmetic and copies ran while one was open for 1% -> 1% of each run, Pallas kernels for 8% -> 7%
where the time goes in v8:
time: 22.9 us; the launch traced here: 22.6 us
  starting transfers between devices  9.67 us (42%)
  Pallas kernels  5.41 us (24%)
  waiting for transfers between devices  5.32 us (23%)
  between operations  1.32 us (6%)
  local copies, waits for them, and re-layouts  0.71 us (3%)
    ppermute x6, starting transfers between devices, swap(): return lax.ppermute(value, ('blk', 'grp'), pairs)  9.67 us
    ppermute x6, waiting for transfers between devices, swap(): return lax.ppermute(value, ('blk', 'grp'), pairs)  5.32 us
    pallas_call x1, Pallas kernels, finish(): pl.pallas_call(functools.partial(last_body, layout), out_shape=(jax.Shape...  3.78 us
    pallas_call x1, Pallas kernels, early(): pl.pallas_call(functools.partial(early_body, layout), out_shape=sums(side...  1.01 us
    unnamed x7, local copies, waits for them, and re-layouts  0.71 us
    pallas_call x1, Pallas kernels, middle(): pl.pallas_call(functools.partial(middle_body, layout, place), out_shape=s...  0.62 us
  transfers between devices with their start and end apart: 6, of which 5 were waited for; matrix products, arithmetic and copies ran while one was open for 1% of the time, Pallas kernels for 7%

profile of v8, /device:TPU:0, one launch (start us, length us, event | category | flops | bytes accessed | tf_op | source)
XLA Modules:
  0.0 22.6 jit_solution(14886230556124491705)
XLA Ops:
  0.6 0.0 copy-start
  0.6 0.7 %constant_dynamic-update-slice_fusion.1 = f32[24,128]{1,0:T(8,128)S(1)} fusion(f32[8,128]{1,0:T(8,128)} %param.5), kind=kLoop, calls=%fused_computation.6 | loop fusion | bytes 8192
  1.3 0.0 copy-done
  1.3 0.0 copy-start.1
  1.3 3.5 %collective-permute-start = (f32[1,24,128]{2,1,0:T(8,128)S(1)}, f32[1,24,128]{2,1,0:T(8,128)S(1)}, u32[]{:S(2)}, u32[]{:S(2)}) collective-permute-start(f32[1,24,128]{2,1,0:T(8,128)S(1)} %bitcast.4), channel_id=1, source_target_pairs={{0,9},{1,8},{2,11},{3,10},{4,13},{5,12},{6,15},{7,14},{8,1},{9,0},... | collective-permute-start | bytes 36872 | tf_op jit(solution)/shard_map/ppermute | solution.py:372
  4.8 0.0 copy-done.1
  4.8 0.0 copy-start.2
  4.8 1.4 %collective-permute-done = f32[1,24,128]{2,1,0:T(8,128)S(1)} collective-permute-done((f32[1,24,128]{2,1,0:T(8,128)S(1)}, f32[1,24,128]{2,1,0:T(8,128)S(1)}, u32[]{:S(2)}, u32[]{:S(2)}) %collective-permute-start) | collective-permute-done | bytes 12320 | tf_op jit(solution)/shard_map/ppermute | solution.py:372
  6.2 1.9 %collective-permute-start.1 = (f32[2,24,128]{2,1,0:T(8,128)S(1)}, f32[2,24,128]{2,1,0:T(8,128)S(1)}, u32[]{:S(2)}, u32[]{:S(2)}) collective-permute-start(f32[2,24,128]{2,1,0:T(8,128)S(1)} %pad_maximum_fusion.3), channel_id=1, source_target_pairs={{0,5},{1,4},{2,7},{3,6},{4,1},{5,0},{6,3},{7,2},{8,13},{9,12},{10,... | collective-permute-start | bytes 73736 | tf_op jit(solution)/shard_map/ppermute | solution.py:372
  8.1 0.0 copy-done.2
  8.8 0.9 %collective-permute-done.1 = f32[2,24,128]{2,1,0:T(8,128)S(1)} collective-permute-done((f32[2,24,128]{2,1,0:T(8,128)S(1)}, f32[2,24,128]{2,1,0:T(8,128)S(1)}, u32[]{:S(2)}, u32[]{:S(2)}) %collective-permute-start.1) | collective-permute-done | bytes 24608 | tf_op jit(solution)/shard_map/ppermute | solution.py:372
  9.6 1.7 %collective-permute-start.2 = (f32[4,24,128]{2,1,0:T(8,128)S(1)}, f32[4,24,128]{2,1,0:T(8,128)S(1)}, u32[]{:S(2)}, u32[]{:S(2)}) collective-permute-start(f32[4,24,128]{2,1,0:T(8,128)S(1)} %pad_maximum_fusion.2), channel_id=1, source_target_pairs={{0,17},{1,2},{2,1},{3,18},{4,7},{5,20},{6,23},{7,4},{8,11},{9,24},... | collective-permute-start | bytes 147464 | tf_op jit(solution)/shard_map/ppermute | solution.py:372
  11.3 0.1 pad_maximum_fusion.5
  11.4 0.4 %collective-permute-start.4 = (f32[24,128]{1,0:T(8,128)S(1)}, f32[24,128]{1,0:T(8,128)S(1)}, u32[]{:S(2)}, u32[]{:S(2)}) collective-permute-start(f32[24,128]{1,0:T(8,128)S(1)} %constant_dynamic-update-slice_fusion.own_ref), channel_id=1, source_target_pairs={{0,1},{1,0},{2,3},{3,2},{4,5},{5,4},{6,7},{7,6},{8,9},{9,8},{10,11... | collective-permute-start | bytes 36872 | tf_op jit(solution)/shard_map/ppermute | solution.py:372
  11.8 1.4 %collective-permute-done.2 = f32[4,24,128]{2,1,0:T(8,128)S(1)} collective-permute-done((f32[4,24,128]{2,1,0:T(8,128)S(1)}, f32[4,24,128]{2,1,0:T(8,128)S(1)}, u32[]{:S(2)}, u32[]{:S(2)}) %collective-permute-start.2) | collective-permute-done | bytes 49184 | tf_op jit(solution)/shard_map/ppermute | solution.py:372
  13.2 1.7 %collective-permute-start.3 = (f32[8,24,128]{2,1,0:T(8,128)S(1)}, f32[8,24,128]{2,1,0:T(8,128)S(1)}, u32[]{:S(2)}, u32[]{:S(2)}) collective-permute-start(f32[8,24,128]{2,1,0:T(8,128)S(1)} %pad_maximum_fusion.1.part_ref), channel_id=1, source_target_pairs={{0,3},{1,16},{2,19},{3,0},{4,21},{5,6},{6,5},{7,22},{8,25},{9,10},... | collective-permute-start | bytes 294920 | tf_op jit(solution)/shard_map/ppermute | solution.py:372
  14.9 0.1 pad_maximum_fusion.4.side_ref
  14.9 0.0 collective-permute-done.4.mate_ref
  14.9 1.0 %shard_map.68 = (f32[128,32]{1,0:T(8,128)S(1)}, f32[128,16]{1,0:T(8,128)S(1)}, f32[24,128]{1,0:T(8,128)S(1)}, f32[2,24,128]{2,1,0:T(8,128)S(1)}) custom-call(f32[10,128]{1,0:T(8,128)S(1)} %pad_maximum_fusion.4.side_ref, f32[24,128]{1,0:T(8,128)S(1)} %constant_dynamic-update-slice_fusion.own_ref, f32[24,128]{1,0:T(8,128)S(1)} %collective-permute-done.4.mate_ref, ...), custom_call_target="tpu_custom_call" | custom-call | flops 15728640 | bytes 102400 | tf_op jit(solution)/shard_map/pallas_call | solution.py:322
  16.0 1.3 %collective-permute-done.3.part_ref = f32[8,24,128]{2,1,0:T(8,128)S(1)} collective-permute-done((f32[8,24,128]{2,1,0:T(8,128)S(1)}, f32[8,24,128]{2,1,0:T(8,128)S(1)}, u32[]{:S(2)}, u32[]{:S(2)}) %collective-permute-start.3) | collective-permute-done | bytes 98336 | tf_op jit(solution)/shard_map/ppermute | solution.py:372
  17.3 0.6 %collective-permute-start.5 = (f32[10,24,128]{2,1,0:T(8,128)S(1)}, f32[10,24,128]{2,1,0:T(8,128)S(1)}, u32[]{:S(2)}, u32[]{:S(2)}) collective-permute-start(f32[10,24,128]{2,1,0:T(8,128)S(1)} %pad_maximum_fusion), channel_id=1, source_target_pairs={{0,1},{1,0},{2,3},{3,2},{4,5},{5,4},{6,7},{7,6},{8,9},{9,8},{10,11... | collective-permute-start | bytes 368648 | tf_op jit(solution)/shard_map/ppermute | solution.py:372
  17.8 0.6 %shard_map.69 = (f32[128,32]{1,0:T(8,128)S(1)}, f32[128,16]{1,0:T(8,128)S(1)}, f32[24,128]{1,0:T(8,128)S(1)}) custom-call(f32[10,128]{1,0:T(8,128)S(1)} %pad_maximum_fusion.4.side_ref, f32[24,128]{1,0:T(8,128)S(1)} %constant_dynamic-update-slice_fusion.own_ref, f32[8,24,128]{2,1,0:T(8,128)S(1)} %collective-permute-done.3.part_ref, ...), custom_call_target="tpu_custom_call" | custom-call | flops 7864320 | bytes 102400 | tf_op jit(solution)/shard_map/pallas_call | solution.py:334
  18.5 0.4 %collective-permute-done.5.there_ref = f32[10,24,128]{2,1,0:T(8,128)S(1)} collective-permute-done((f32[10,24,128]{2,1,0:T(8,128)S(1)}, f32[10,24,128]{2,1,0:T(8,128)S(1)}, u32[]{:S(2)}, u32[]{:S(2)}) %collective-permute-start.5) | collective-permute-done | bytes 122912 | tf_op jit(solution)/shard_map/ppermute | solution.py:372
  18.8 3.8 %shard_map.70 = (f32[128,128]{1,0:T(8,128)}, f32[16,128]{1,0:T(8,128)}) custom-call(f32[10,128]{1,0:T(8,128)S(1)} %pad_maximum_fusion.4.side_ref, f32[24,128]{1,0:T(8,128)S(1)} %constant_dynamic-update-slice_fusion.own_ref, f32[10,24,128]{2,1,0:T(8,128)S(1)} %collective-permute-done.5.there_ref, f32[128,32]{1,0:T(8,128)S(1)} %get-tuple-element.19.wide_ref, ...), custom_call_target="tpu_custom_call" | custom-call | tf_op jit(solution)/shard_map/pallas_call | solution.py:347
  (7 shorter events, 0.0 us)
Async XLA Ops:
  0.6 0.7 %copy-start = (f32[16,128]{1,0:T(8,128)S(1)}, f32[16,128]{1,0:T(8,128)}, u32[]{:S(2)}) copy-start(f32[16,128]{1,0:T(8,128)} %param.6) | copy-start | bytes 24580
  1.3 3.5 %copy-start.1 = (f32[8]{0:T(128)S(1)}, f32[8]{0:T(128)}, u32[]{:S(2)}) copy-start(f32[8]{0:T(128)} %param.7) | copy-start | bytes 100
  1.3 4.9 %collective-permute-start = (f32[1,24,128]{2,1,0:T(8,128)S(1)}, f32[1,24,128]{2,1,0:T(8,128)S(1)}, u32[]{:S(2)}, u32[]{:S(2)}) collective-permute-start(f32[1,24,128]{2,1,0:T(8,128)S(1)} %bitcast.4), channel_id=1, source_target_pairs={{0,9},{1,8},{2,11},{3,10},{4,13},{5,12},{6,15},{7,14},{8,1},{9,0},... | collective-permute-start | bytes 36872 | tf_op jit(solution)/shard_map/ppermute | solution.py:372
  4.8 3.3 %copy-start.2 = (s32[128]{0:T(128)S(1)}, s32[128]{0:T(128)}, u32[]{:S(2)}) copy-start(s32[128]{0:T(128)} %param.9) | copy-start | bytes 1540
  6.2 3.4 %collective-permute-start.1 = (f32[2,24,128]{2,1,0:T(8,128)S(1)}, f32[2,24,128]{2,1,0:T(8,128)S(1)}, u32[]{:S(2)}, u32[]{:S(2)}) collective-permute-start(f32[2,24,128]{2,1,0:T(8,128)S(1)} %pad_maximum_fusion.3), channel_id=1, source_target_pairs={{0,5},{1,4},{2,7},{3,6},{4,1},{5,0},{6,3},{7,2},{8,13},{9,12},{10,... | collective-permute-start | bytes 73736 | tf_op jit(solution)/shard_map/ppermute | solution.py:372
  9.6 3.5 %collective-permute-start.2 = (f32[4,24,128]{2,1,0:T(8,128)S(1)}, f32[4,24,128]{2,1,0:T(8,128)S(1)}, u32[]{:S(2)}, u32[]{:S(2)}) collective-permute-start(f32[4,24,128]{2,1,0:T(8,128)S(1)} %pad_maximum_fusion.2), channel_id=1, source_target_pairs={{0,17},{1,2},{2,1},{3,18},{4,7},{5,20},{6,23},{7,4},{8,11},{9,24},... | collective-permute-start | bytes 147464 | tf_op jit(solution)/shard_map/ppermute | solution.py:372
  11.4 3.6 %collective-permute-start.4 = (f32[24,128]{1,0:T(8,128)S(1)}, f32[24,128]{1,0:T(8,128)S(1)}, u32[]{:S(2)}, u32[]{:S(2)}) collective-permute-start(f32[24,128]{1,0:T(8,128)S(1)} %constant_dynamic-update-slice_fusion.own_ref), channel_id=1, source_target_pairs={{0,1},{1,0},{2,3},{3,2},{4,5},{5,4},{6,7},{7,6},{8,9},{9,8},{10,11... | collective-permute-start | bytes 36872 | tf_op jit(solution)/shard_map/ppermute | solution.py:372
  13.2 4.1 %collective-permute-start.3 = (f32[8,24,128]{2,1,0:T(8,128)S(1)}, f32[8,24,128]{2,1,0:T(8,128)S(1)}, u32[]{:S(2)}, u32[]{:S(2)}) collective-permute-start(f32[8,24,128]{2,1,0:T(8,128)S(1)} %pad_maximum_fusion.1.part_ref), channel_id=1, source_target_pairs={{0,3},{1,16},{2,19},{3,0},{4,21},{5,6},{6,5},{7,22},{8,25},{9,10},... | collective-permute-start | bytes 294920 | tf_op jit(solution)/shard_map/ppermute | solution.py:372
  17.3 1.5 %collective-permute-start.5 = (f32[10,24,128]{2,1,0:T(8,128)S(1)}, f32[10,24,128]{2,1,0:T(8,128)S(1)}, u32[]{:S(2)}, u32[]{:S(2)}) collective-permute-start(f32[10,24,128]{2,1,0:T(8,128)S(1)} %pad_maximum_fusion), channel_id=1, source_target_pairs={{0,1},{1,0},{2,3},{3,2},{4,5},{5,4},{6,7},{7,6},{8,9},{9,8},{10,11... | collective-permute-start | bytes 368648 | tf_op jit(solution)/shard_map/ppermute | solution.py:372

commit v9 on v8

--- a/solution.py
+++ b/solution.py
@@ -291,7 +291,7 @@
             pltpu.make_async_copy(rows_ref.at[rows, :], panel_ref.at[rows, :], sems.at[step])
         )
         copies[-1].start()
-        if step == steps // 2:
+        if step == steps - 2:
             copies.append(pltpu.make_async_copy(total_ref, product_ref, total_sem))
             copies[-1].start()
     for copy in copies:

time: 22.9 us -> 22.9 us (level)
  no operation moved by 1% of the time
where the time goes in v9:
time: 22.9 us; the launch traced here: 22.6 us
  starting transfers between devices  9.67 us (42%)
  Pallas kernels  5.41 us (24%)
  waiting for transfers between devices  5.32 us (23%)
  between operations  1.32 us (6%)
  local copies, waits for them, and re-layouts  0.71 us (3%)
    ppermute x6, starting transfers between devices, swap(): return lax.ppermute(value, ('blk', 'grp'), pairs)  9.67 us
    ppermute x6, waiting for transfers between devices, swap(): return lax.ppermute(value, ('blk', 'grp'), pairs)  5.32 us
    pallas_call x1, Pallas kernels, finish(): pl.pallas_call(functools.partial(last_body, layout), out_shape=(jax.Shape...  3.78 us
    pallas_call x1, Pallas kernels, early(): pl.pallas_call(functools.partial(early_body, layout), out_shape=sums(side...  1.01 us
    unnamed x7, local copies, waits for them, and re-layouts  0.71 us
    pallas_call x1, Pallas kernels, middle(): pl.pallas_call(functools.partial(middle_body, layout, place), out_shape=s...  0.62 us
  transfers between devices with their start and end apart: 6, of which 5 were waited for; matrix products, arithmetic and copies ran while one was open for 1% of the time, Pallas kernels for 7%

profile of v9, /device:TPU:0, one launch (start us, length us, event | category | flops | bytes accessed | tf_op | source)
XLA Modules:
  0.0 22.6 jit_solution(15083445271336477136)
XLA Ops:
  0.6 0.0 copy-start
  0.6 0.7 %constant_dynamic-update-slice_fusion.1 = f32[24,128]{1,0:T(8,128)S(1)} fusion(f32[8,128]{1,0:T(8,128)} %param.5), kind=kLoop, calls=%fused_computation.6 | loop fusion | bytes 8192
  1.3 0.0 copy-done
  1.3 0.0 copy-start.1
  1.3 3.5 %collective-permute-start = (f32[1,24,128]{2,1,0:T(8,128)S(1)}, f32[1,24,128]{2,1,0:T(8,128)S(1)}, u32[]{:S(2)}, u32[]{:S(2)}) collective-permute-start(f32[1,24,128]{2,1,0:T(8,128)S(1)} %bitcast.4), channel_id=1, source_target_pairs={{0,9},{1,8},{2,11},{3,10},{4,13},{5,12},{6,15},{7,14},{8,1},{9,0},... | collective-permute-start | bytes 36872 | tf_op jit(solution)/shard_map/ppermute | solution.py:372
  4.8 0.0 copy-done.1
  4.8 0.0 copy-start.2
  4.8 1.4 %collective-permute-done = f32[1,24,128]{2,1,0:T(8,128)S(1)} collective-permute-done((f32[1,24,128]{2,1,0:T(8,128)S(1)}, f32[1,24,128]{2,1,0:T(8,128)S(1)}, u32[]{:S(2)}, u32[]{:S(2)}) %collective-permute-start) | collective-permute-done | bytes 12320 | tf_op jit(solution)/shard_map/ppermute | solution.py:372
  6.2 1.9 %collective-permute-start.1 = (f32[2,24,128]{2,1,0:T(8,128)S(1)}, f32[2,24,128]{2,1,0:T(8,128)S(1)}, u32[]{:S(2)}, u32[]{:S(2)}) collective-permute-start(f32[2,24,128]{2,1,0:T(8,128)S(1)} %pad_maximum_fusion.3), channel_id=1, source_target_pairs={{0,5},{1,4},{2,7},{3,6},{4,1},{5,0},{6,3},{7,2},{8,13},{9,12},{10,... | collective-permute-start | bytes 73736 | tf_op jit(solution)/shard_map/ppermute | solution.py:372
  8.1 0.0 copy-done.2
  8.8 0.9 %collective-permute-done.1 = f32[2,24,128]{2,1,0:T(8,128)S(1)} collective-permute-done((f32[2,24,128]{2,1,0:T(8,128)S(1)}, f32[2,24,128]{2,1,0:T(8,128)S(1)}, u32[]{:S(2)}, u32[]{:S(2)}) %collective-permute-start.1) | collective-permute-done | bytes 24608 | tf_op jit(solution)/shard_map/ppermute | solution.py:372
  9.6 1.7 %collective-permute-start.2 = (f32[4,24,128]{2,1,0:T(8,128)S(1)}, f32[4,24,128]{2,1,0:T(8,128)S(1)}, u32[]{:S(2)}, u32[]{:S(2)}) collective-permute-start(f32[4,24,128]{2,1,0:T(8,128)S(1)} %pad_maximum_fusion.2), channel_id=1, source_target_pairs={{0,17},{1,2},{2,1},{3,18},{4,7},{5,20},{6,23},{7,4},{8,11},{9,24},... | collective-permute-start | bytes 147464 | tf_op jit(solution)/shard_map/ppermute | solution.py:372
  11.3 0.1 pad_maximum_fusion.5
  11.4 0.4 %collective-permute-start.4 = (f32[24,128]{1,0:T(8,128)S(1)}, f32[24,128]{1,0:T(8,128)S(1)}, u32[]{:S(2)}, u32[]{:S(2)}) collective-permute-start(f32[24,128]{1,0:T(8,128)S(1)} %constant_dynamic-update-slice_fusion.own_ref), channel_id=1, source_target_pairs={{0,1},{1,0},{2,3},{3,2},{4,5},{5,4},{6,7},{7,6},{8,9},{9,8},{10,11... | collective-permute-start | bytes 36872 | tf_op jit(solution)/shard_map/ppermute | solution.py:372
  11.8 1.4 %collective-permute-done.2 = f32[4,24,128]{2,1,0:T(8,128)S(1)} collective-permute-done((f32[4,24,128]{2,1,0:T(8,128)S(1)}, f32[4,24,128]{2,1,0:T(8,128)S(1)}, u32[]{:S(2)}, u32[]{:S(2)}) %collective-permute-start.2) | collective-permute-done | bytes 49184 | tf_op jit(solution)/shard_map/ppermute | solution.py:372
  13.2 1.7 %collective-permute-start.3 = (f32[8,24,128]{2,1,0:T(8,128)S(1)}, f32[8,24,128]{2,1,0:T(8,128)S(1)}, u32[]{:S(2)}, u32[]{:S(2)}) collective-permute-start(f32[8,24,128]{2,1,0:T(8,128)S(1)} %pad_maximum_fusion.1.part_ref), channel_id=1, source_target_pairs={{0,3},{1,16},{2,19},{3,0},{4,21},{5,6},{6,5},{7,22},{8,25},{9,10},... | collective-permute-start | bytes 294920 | tf_op jit(solution)/shard_map/ppermute | solution.py:372
  14.9 0.1 pad_maximum_fusion.4.side_ref
  14.9 0.0 collective-permute-done.4.mate_ref
  14.9 1.0 %shard_map.68 = (f32[128,32]{1,0:T(8,128)S(1)}, f32[128,16]{1,0:T(8,128)S(1)}, f32[24,128]{1,0:T(8,128)S(1)}, f32[2,24,128]{2,1,0:T(8,128)S(1)}) custom-call(f32[10,128]{1,0:T(8,128)S(1)} %pad_maximum_fusion.4.side_ref, f32[24,128]{1,0:T(8,128)S(1)} %constant_dynamic-update-slice_fusion.own_ref, f32[24,128]{1,0:T(8,128)S(1)} %collective-permute-done.4.mate_ref, ...), custom_call_target="tpu_custom_call" | custom-call | flops 15728640 | bytes 102400 | tf_op jit(solution)/shard_map/pallas_call | solution.py:322
  16.0 1.3 %collective-permute-done.3.part_ref = f32[8,24,128]{2,1,0:T(8,128)S(1)} collective-permute-done((f32[8,24,128]{2,1,0:T(8,128)S(1)}, f32[8,24,128]{2,1,0:T(8,128)S(1)}, u32[]{:S(2)}, u32[]{:S(2)}) %collective-permute-start.3) | collective-permute-done | bytes 98336 | tf_op jit(solution)/shard_map/ppermute | solution.py:372
  17.3 0.6 %collective-permute-start.5 = (f32[10,24,128]{2,1,0:T(8,128)S(1)}, f32[10,24,128]{2,1,0:T(8,128)S(1)}, u32[]{:S(2)}, u32[]{:S(2)}) collective-permute-start(f32[10,24,128]{2,1,0:T(8,128)S(1)} %pad_maximum_fusion), channel_id=1, source_target_pairs={{0,1},{1,0},{2,3},{3,2},{4,5},{5,4},{6,7},{7,6},{8,9},{9,8},{10,11... | collective-permute-start | bytes 368648 | tf_op jit(solution)/shard_map/ppermute | solution.py:372
  17.8 0.6 %shard_map.69 = (f32[128,32]{1,0:T(8,128)S(1)}, f32[128,16]{1,0:T(8,128)S(1)}, f32[24,128]{1,0:T(8,128)S(1)}) custom-call(f32[10,128]{1,0:T(8,128)S(1)} %pad_maximum_fusion.4.side_ref, f32[24,128]{1,0:T(8,128)S(1)} %constant_dynamic-update-slice_fusion.own_ref, f32[8,24,128]{2,1,0:T(8,128)S(1)} %collective-permute-done.3.part_ref, ...), custom_call_target="tpu_custom_call" | custom-call | flops 7864320 | bytes 102400 | tf_op jit(solution)/shard_map/pallas_call | solution.py:334
  18.5 0.4 %collective-permute-done.5.there_ref = f32[10,24,128]{2,1,0:T(8,128)S(1)} collective-permute-done((f32[10,24,128]{2,1,0:T(8,128)S(1)}, f32[10,24,128]{2,1,0:T(8,128)S(1)}, u32[]{:S(2)}, u32[]{:S(2)}) %collective-permute-start.5) | collective-permute-done | bytes 122912 | tf_op jit(solution)/shard_map/ppermute | solution.py:372
  18.8 3.8 %shard_map.70 = (f32[128,128]{1,0:T(8,128)}, f32[16,128]{1,0:T(8,128)}) custom-call(f32[10,128]{1,0:T(8,128)S(1)} %pad_maximum_fusion.4.side_ref, f32[24,128]{1,0:T(8,128)S(1)} %constant_dynamic-update-slice_fusion.own_ref, f32[10,24,128]{2,1,0:T(8,128)S(1)} %collective-permute-done.5.there_ref, f32[128,32]{1,0:T(8,128)S(1)} %get-tuple-element.19.wide_ref, ...), custom_call_target="tpu_custom_call" | custom-call | tf_op jit(solution)/shard_map/pallas_call | solution.py:347
  (7 shorter events, 0.0 us)
Async XLA Ops:
  0.6 0.7 %copy-start = (f32[16,128]{1,0:T(8,128)S(1)}, f32[16,128]{1,0:T(8,128)}, u32[]{:S(2)}) copy-start(f32[16,128]{1,0:T(8,128)} %param.6) | copy-start | bytes 24580
  1.3 3.5 %copy-start.1 = (f32[8]{0:T(128)S(1)}, f32[8]{0:T(128)}, u32[]{:S(2)}) copy-start(f32[8]{0:T(128)} %param.7) | copy-start | bytes 100
  1.3 4.9 %collective-permute-start = (f32[1,24,128]{2,1,0:T(8,128)S(1)}, f32[1,24,128]{2,1,0:T(8,128)S(1)}, u32[]{:S(2)}, u32[]{:S(2)}) collective-permute-start(f32[1,24,128]{2,1,0:T(8,128)S(1)} %bitcast.4), channel_id=1, source_target_pairs={{0,9},{1,8},{2,11},{3,10},{4,13},{5,12},{6,15},{7,14},{8,1},{9,0},... | collective-permute-start | bytes 36872 | tf_op jit(solution)/shard_map/ppermute | solution.py:372
  4.8 3.3 %copy-start.2 = (s32[128]{0:T(128)S(1)}, s32[128]{0:T(128)}, u32[]{:S(2)}) copy-start(s32[128]{0:T(128)} %param.9) | copy-start | bytes 1540
  6.2 3.4 %collective-permute-start.1 = (f32[2,24,128]{2,1,0:T(8,128)S(1)}, f32[2,24,128]{2,1,0:T(8,128)S(1)}, u32[]{:S(2)}, u32[]{:S(2)}) collective-permute-start(f32[2,24,128]{2,1,0:T(8,128)S(1)} %pad_maximum_fusion.3), channel_id=1, source_target_pairs={{0,5},{1,4},{2,7},{3,6},{4,1},{5,0},{6,3},{7,2},{8,13},{9,12},{10,... | collective-permute-start | bytes 73736 | tf_op jit(solution)/shard_map/ppermute | solution.py:372
  9.6 3.5 %collective-permute-start.2 = (f32[4,24,128]{2,1,0:T(8,128)S(1)}, f32[4,24,128]{2,1,0:T(8,128)S(1)}, u32[]{:S(2)}, u32[]{:S(2)}) collective-permute-start(f32[4,24,128]{2,1,0:T(8,128)S(1)} %pad_maximum_fusion.2), channel_id=1, source_target_pairs={{0,17},{1,2},{2,1},{3,18},{4,7},{5,20},{6,23},{7,4},{8,11},{9,24},... | collective-permute-start | bytes 147464 | tf_op jit(solution)/shard_map/ppermute | solution.py:372
  11.4 3.6 %collective-permute-start.4 = (f32[24,128]{1,0:T(8,128)S(1)}, f32[24,128]{1,0:T(8,128)S(1)}, u32[]{:S(2)}, u32[]{:S(2)}) collective-permute-start(f32[24,128]{1,0:T(8,128)S(1)} %constant_dynamic-update-slice_fusion.own_ref), channel_id=1, source_target_pairs={{0,1},{1,0},{2,3},{3,2},{4,5},{5,4},{6,7},{7,6},{8,9},{9,8},{10,11... | collective-permute-start | bytes 36872 | tf_op jit(solution)/shard_map/ppermute | solution.py:372
  13.2 4.1 %collective-permute-start.3 = (f32[8,24,128]{2,1,0:T(8,128)S(1)}, f32[8,24,128]{2,1,0:T(8,128)S(1)}, u32[]{:S(2)}, u32[]{:S(2)}) collective-permute-start(f32[8,24,128]{2,1,0:T(8,128)S(1)} %pad_maximum_fusion.1.part_ref), channel_id=1, source_target_pairs={{0,3},{1,16},{2,19},{3,0},{4,21},{5,6},{6,5},{7,22},{8,25},{9,10},... | collective-permute-start | bytes 294920 | tf_op jit(solution)/shard_map/ppermute | solution.py:372
  17.3 1.5 %collective-permute-start.5 = (f32[10,24,128]{2,1,0:T(8,128)S(1)}, f32[10,24,128]{2,1,0:T(8,128)S(1)}, u32[]{:S(2)}, u32[]{:S(2)}) collective-permute-start(f32[10,24,128]{2,1,0:T(8,128)S(1)} %pad_maximum_fusion), channel_id=1, source_target_pairs={{0,1},{1,0},{2,3},{3,2},{4,5},{5,4},{6,7},{7,6},{8,9},{9,8},{10,11... | collective-permute-start | bytes 368648 | tf_op jit(solution)/shard_map/ppermute | solution.py:372

commit v10 on v8

--- a/solution.py
+++ b/solution.py
@@ -227,46 +227,43 @@
     return (wide[:, :vectors] + wide[:, vectors:] + narrow).T
 
 
-def early_body(layout, side_ref, own_ref, mate_ref, part_ref, wide_ref, narrow_ref, picked_ref, parcel_ref):
+def picked_sum(picked, dims):
+    return picked[:dims] + picked[dims : 2 * dims] + picked[2 * dims :]
+
+
+def early_body(layout, side_ref, own_ref, mate_ref, part_ref, share_ref, parcel_ref):
     work = Gathered(*layout, side_ref, own_ref, mate_ref)
     wide, narrow, picked = work.start()
-    blocks, rows = part_ref.shape[0], work.rows
+    blocks, rows, vectors = part_ref.shape[0], work.rows, work.vectors
     picked = over(blocks, PICK, picked, lambda c, i: work.pick(c, part_ref, i, 0, 0))
     wide, narrow = over(blocks, CHUNK, (wide, narrow), lambda c, i: work.add(*c, part_ref, i))
-    wide_ref[...], narrow_ref[...], picked_ref[...] = wide[:rows], narrow[:rows], picked
-    parcel_ref[0, : work.vectors, :] = gathered_sum(wide[rows:], narrow[rows:])
-    parcel_ref[0, work.vectors :, :] = jnp.zeros((work.dims, rows), F32)
-    parcel_ref[1] = picked
-
-
-def middle_body(
-    layout, place, side_ref, own_ref, part_ref, wide_in, narrow_in, picked_in,
-    wide_ref, narrow_ref, picked_ref,
-):
+    found = picked_sum(picked, work.dims)
+    share_ref[:vectors, :] = gathered_sum(wide[:rows], narrow[:rows])
+    share_ref[vectors:, :] = found
+    parcel_ref[0, :vectors, :] = gathered_sum(wide[rows:], narrow[rows:])
+    parcel_ref[0, vectors:, :] = found
+
+
+def middle_body(layout, place, side_ref, own_ref, part_ref, share_ref, out_ref):
     work = Gathered(*layout, side_ref, own_ref)
-    blocks = part_ref.shape[0]
-    picked_ref[...] = over(
-        blocks, PICK, picked_in[...], lambda c, i: work.pick(c, part_ref, i, place, 0)
-    )
-    wide_ref[...], narrow_ref[...] = over(
-        blocks, CHUNK, (wide_in[...], narrow_in[...]), lambda c, i: work.add(*c, part_ref, i)
-    )
+    wide, narrow, picked = work.start()
+    blocks, vectors = part_ref.shape[0], work.vectors
+    picked = over(blocks, PICK, picked, lambda c, i: work.pick(c, part_ref, i, place, 0))
+    wide, narrow = over(blocks, CHUNK, (wide, narrow), lambda c, i: work.add(*c, part_ref, i))
+    out_ref[:vectors, :] = share_ref[:vectors, :] + gathered_sum(wide, narrow)
+    out_ref[vectors:, :] = share_ref[vectors:, :] + picked_sum(picked, work.dims)
 
 
 def last_body(
-    layout, side_ref, own_ref, there_ref, wide_ref, narrow_ref, picked_ref,
+    layout, side_ref, own_ref, there_ref, share_ref,
     panel_ref, product_ref, rows_ref, total_ref, sems, total_sem,
 ):
     work = Gathered(*layout, side_ref, own_ref)
-    blocks = there_ref.shape[0] - 2
-    picked = over(
-        blocks,
-        PICK,
-        picked_ref[...] + there_ref[blocks + 1],
-        lambda c, i: work.pick(c, there_ref, i, blocks, 1),
-    )
-    dims = work.dims
-    pivot_x = (picked[:dims] + picked[dims : 2 * dims] + picked[2 * dims :]) * work.scale
+    blocks, dims, vectors = there_ref.shape[0] - 1, work.dims, work.vectors
+    wide, narrow, picked = work.start()
+    picked = over(blocks, PICK, picked, lambda c, i: work.pick(c, there_ref, i, blocks, 1))
+    found = share_ref[vectors:, :] + there_ref[blocks, vectors:, :]
+    pivot_x = (found + picked_sum(picked, dims)) * work.scale
     size = pivot_x.shape[1]
     left_pivot = left_stack(pivot_x).T.astype(BF16)
     both = jnp.concatenate([right_stack(pivot_x), right_stack(work.own)], 1)
@@ -278,9 +275,8 @@
     a = [inner[i : i + 8] for i in range(0, size, 8)]
     b = [values[i : i + 8, size:] for i in range(0, size, 8)]
 
-    wide, narrow = wide_ref[...], narrow_ref[...]
     wide, narrow = over(blocks, CHUNK, (wide, narrow), lambda c, i: work.add(*c, there_ref, i))
-    total = gathered_sum(wide, narrow) + there_ref[blocks, : work.vectors, :]
+    total = gathered_sum(wide, narrow) + there_ref[blocks, :vectors, :] + share_ref[:vectors, :]
     total_ref[...] = total + work.noise * own_ref[dims:, :]
     steps = size // BLOCK
     copies = []
@@ -308,37 +304,31 @@
     )
 
 
-def sums(side, own):
-    rows, vectors = own.shape[1], own.shape[0] - side.shape[0] + 2
-    return (
-        jax.ShapeDtypeStruct((rows, 2 * vectors), F32),
-        jax.ShapeDtypeStruct((rows, vectors), F32),
-        jax.ShapeDtypeStruct((3 * (side.shape[0] - 2), side.shape[1]), F32),
-    )
-
-
 def early(layout, side, own, mate, part):
     rows = own.shape[1]
     return pl.pallas_call(
         functools.partial(early_body, layout),
-        out_shape=sums(side, own) + (jax.ShapeDtypeStruct((2,) + own.shape, F32),),
+        out_shape=(
+            jax.ShapeDtypeStruct(own.shape, F32),
+            jax.ShapeDtypeStruct((1,) + own.shape, F32),
+        ),
         in_specs=[VMEM] * 4,
-        out_specs=(VMEM,) * 4,
+        out_specs=(VMEM,) * 2,
         cost_estimate=cost(part.shape[0] * rows, 2 * rows),
         compiler_params=PARAMS,
     )(side, own, mate, part)
 
 
-def middle(layout, place, side, own, part, *carry):
+def middle(layout, place, side, own, part, share):
     rows = own.shape[1]
     return pl.pallas_call(
         functools.partial(middle_body, layout, place),
-        out_shape=sums(side, own),
-        in_specs=[VMEM] * 6,
-        out_specs=(VMEM,) * 3,
+        out_shape=jax.ShapeDtypeStruct(own.shape, F32),
+        in_specs=[VMEM] * 4,
+        out_specs=VMEM,
         cost_estimate=cost(part.shape[0] * rows, rows),
         compiler_params=PARAMS,
-    )(side, own, part, *carry)
+    )(side, own, part, share)
 
 
 def finish(layout, side, own, there, *carry):
@@ -391,11 +381,11 @@
                 mate = swap(lax.optimization_barrier((own, here))[0], last)
             here = jnp.concatenate([here, swap(here, step)], 0)
         arrived = swap(here, last - 1)
-        *carry, parcel = early(layout, side, own, mate, here)
+        share, parcel = early(layout, side, own, mate, here)
         arrived, parcel = lax.optimization_barrier((arrived, parcel))
         there = swap(jnp.concatenate([arrived, parcel], 0), last)
-        carry = middle(layout, here.shape[0], side, own, arrived, *carry)
-        return finish(layout, side, own, there, *carry)
+        share = middle(layout, here.shape[0], side, own, arrived, share)
+        return finish(layout, side, own, there, share)
 
     in_specs = (P(None, ("blk", "grp")), P(None, ("blk", "grp")), P(), P(), P())
     out_specs = (P(None, ("blk", "grp")), P(None, ("blk", "grp")))

time: 22.9 us -> 22.9 us (level)
  transfers between devices with their start and end apart: 6 -> 6, of which waited for: 5 -> 5; matrix products, arithmetic and copies ran while one was open for 1% -> 1% of each run, Pallas kernels for 7% -> 8%
where the time goes in v10:
time: 22.9 us; the launch traced here: 22.6 us
  starting transfers between devices  9.67 us (42%)
  Pallas kernels  5.52 us (24%)
  waiting for transfers between devices  5.24 us (23%)
  between operations  1.31 us (6%)
  local copies, waits for them, and re-layouts  0.71 us (3%)
    ppermute x6, starting transfers between devices, swap(): return lax.ppermute(value, ('blk', 'grp'), pairs)  9.67 us
    ppermute x6, waiting for transfers between devices, swap(): return lax.ppermute(value, ('blk', 'grp'), pairs)  5.24 us
    pallas_call x1, Pallas kernels, finish(): pl.pallas_call(functools.partial(last_body, layout), out_shape=(jax.Shape...  3.82 us
    pallas_call x1, Pallas kernels, early(): pl.pallas_call(functools.partial(early_body, layout), out_shape=(jax.Shap...  0.98 us
    pallas_call x1, Pallas kernels, middle(): pl.pallas_call(functools.partial(middle_body, layout, place), out_shape=j...  0.72 us
    unnamed x7, local copies, waits for them, and re-layouts  0.71 us
  transfers between devices with their start and end apart: 6, of which 5 were waited for; matrix products, arithmetic and copies ran while one was open for 1% of the time, Pallas kernels for 8%

profile of v10, /device:TPU:0, one launch (start us, length us, event | category | flops | bytes accessed | tf_op | source)
XLA Modules:
  0.0 22.6 jit_solution(549826976043286804)
XLA Ops:
  0.6 0.0 copy-start
  0.6 0.7 %constant_dynamic-update-slice_fusion.1 = f32[24,128]{1,0:T(8,128)S(1)} fusion(f32[8,128]{1,0:T(8,128)} %param.5), kind=kLoop, calls=%fused_computation.6 | loop fusion | bytes 8192
  1.3 0.0 copy-done
  1.3 0.0 copy-start.1
  1.3 3.5 %collective-permute-start = (f32[1,24,128]{2,1,0:T(8,128)S(1)}, f32[1,24,128]{2,1,0:T(8,128)S(1)}, u32[]{:S(2)}, u32[]{:S(2)}) collective-permute-start(f32[1,24,128]{2,1,0:T(8,128)S(1)} %bitcast.4), channel_id=1, source_target_pairs={{0,9},{1,8},{2,11},{3,10},{4,13},{5,12},{6,15},{7,14},{8,1},{9,0},... | collective-permute-start | bytes 36872 | tf_op jit(solution)/shard_map/ppermute | solution.py:362
  4.8 0.0 copy-done.1
  4.8 0.0 copy-start.2
  4.8 1.4 %collective-permute-done = f32[1,24,128]{2,1,0:T(8,128)S(1)} collective-permute-done((f32[1,24,128]{2,1,0:T(8,128)S(1)}, f32[1,24,128]{2,1,0:T(8,128)S(1)}, u32[]{:S(2)}, u32[]{:S(2)}) %collective-permute-start) | collective-permute-done | bytes 12320 | tf_op jit(solution)/shard_map/ppermute | solution.py:362
  6.2 1.9 %collective-permute-start.1 = (f32[2,24,128]{2,1,0:T(8,128)S(1)}, f32[2,24,128]{2,1,0:T(8,128)S(1)}, u32[]{:S(2)}, u32[]{:S(2)}) collective-permute-start(f32[2,24,128]{2,1,0:T(8,128)S(1)} %pad_maximum_fusion.3), channel_id=1, source_target_pairs={{0,5},{1,4},{2,7},{3,6},{4,1},{5,0},{6,3},{7,2},{8,13},{9,12},{10,... | collective-permute-start | bytes 73736 | tf_op jit(solution)/shard_map/ppermute | solution.py:362
  8.1 0.0 copy-done.2
  8.8 0.9 %collective-permute-done.1 = f32[2,24,128]{2,1,0:T(8,128)S(1)} collective-permute-done((f32[2,24,128]{2,1,0:T(8,128)S(1)}, f32[2,24,128]{2,1,0:T(8,128)S(1)}, u32[]{:S(2)}, u32[]{:S(2)}) %collective-permute-start.1) | collective-permute-done | bytes 24608 | tf_op jit(solution)/shard_map/ppermute | solution.py:362
  9.6 1.7 %collective-permute-start.2 = (f32[4,24,128]{2,1,0:T(8,128)S(1)}, f32[4,24,128]{2,1,0:T(8,128)S(1)}, u32[]{:S(2)}, u32[]{:S(2)}) collective-permute-start(f32[4,24,128]{2,1,0:T(8,128)S(1)} %pad_maximum_fusion.2), channel_id=1, source_target_pairs={{0,17},{1,2},{2,1},{3,18},{4,7},{5,20},{6,23},{7,4},{8,11},{9,24},... | collective-permute-start | bytes 147464 | tf_op jit(solution)/shard_map/ppermute | solution.py:362
  11.3 0.1 pad_maximum_fusion.5
  11.4 0.4 %collective-permute-start.4 = (f32[24,128]{1,0:T(8,128)S(1)}, f32[24,128]{1,0:T(8,128)S(1)}, u32[]{:S(2)}, u32[]{:S(2)}) collective-permute-start(f32[24,128]{1,0:T(8,128)S(1)} %constant_dynamic-update-slice_fusion.own_ref), channel_id=1, source_target_pairs={{0,1},{1,0},{2,3},{3,2},{4,5},{5,4},{6,7},{7,6},{8,9},{9,8},{10,11... | collective-permute-start | bytes 36872 | tf_op jit(solution)/shard_map/ppermute | solution.py:362
  11.8 1.4 %collective-permute-done.2 = f32[4,24,128]{2,1,0:T(8,128)S(1)} collective-permute-done((f32[4,24,128]{2,1,0:T(8,128)S(1)}, f32[4,24,128]{2,1,0:T(8,128)S(1)}, u32[]{:S(2)}, u32[]{:S(2)}) %collective-permute-start.2) | collective-permute-done | bytes 49184 | tf_op jit(solution)/shard_map/ppermute | solution.py:362
  13.2 1.7 %collective-permute-start.3 = (f32[8,24,128]{2,1,0:T(8,128)S(1)}, f32[8,24,128]{2,1,0:T(8,128)S(1)}, u32[]{:S(2)}, u32[]{:S(2)}) collective-permute-start(f32[8,24,128]{2,1,0:T(8,128)S(1)} %pad_maximum_fusion.1.part_ref), channel_id=1, source_target_pairs={{0,3},{1,16},{2,19},{3,0},{4,21},{5,6},{6,5},{7,22},{8,25},{9,10},... | collective-permute-start | bytes 294920 | tf_op jit(solution)/shard_map/ppermute | solution.py:362
  14.9 0.1 pad_maximum_fusion.4.side_ref
  14.9 0.0 collective-permute-done.4.mate_ref
  14.9 1.0 %shard_map.68 = (f32[24,128]{1,0:T(8,128)S(1)}, f32[1,24,128]{2,1,0:T(8,128)S(1)}) custom-call(f32[10,128]{1,0:T(8,128)S(1)} %pad_maximum_fusion.4.side_ref, f32[24,128]{1,0:T(8,128)S(1)} %constant_dynamic-update-slice_fusion.own_ref, f32[24,128]{1,0:T(8,128)S(1)} %collective-permute-done.4.mate_ref, f32[8,24,128]{2,1,0:T(8,128)S(1)} %pad_maximum_fusion.1.part_ref), custom_call_target="tpu_custom_call" | custom-call | flops 15728640 | bytes 102400 | tf_op jit(solution)/shard_map/pallas_call | solution.py:309
  15.9 1.3 %collective-permute-done.3.part_ref = f32[8,24,128]{2,1,0:T(8,128)S(1)} collective-permute-done((f32[8,24,128]{2,1,0:T(8,128)S(1)}, f32[8,24,128]{2,1,0:T(8,128)S(1)}, u32[]{:S(2)}, u32[]{:S(2)}) %collective-permute-start.3) | collective-permute-done | bytes 98336 | tf_op jit(solution)/shard_map/ppermute | solution.py:362
  17.3 0.6 %collective-permute-start.5 = (f32[9,24,128]{2,1,0:T(8,128)S(1)}, f32[9,24,128]{2,1,0:T(8,128)S(1)}, u32[]{:S(2)}, u32[]{:S(2)}) collective-permute-start(f32[9,24,128]{2,1,0:T(8,128)S(1)} %pad_maximum_fusion), channel_id=1, source_target_pairs={{0,1},{1,0},{2,3},{3,2},{4,5},{5,4},{6,7},{7,6},{8,9},{9,8},{10,11... | collective-permute-start | bytes 331784 | tf_op jit(solution)/shard_map/ppermute | solution.py:362
  17.8 0.7 %shard_map.69.share_ref = f32[24,128]{1,0:T(8,128)S(1)} custom-call(f32[10,128]{1,0:T(8,128)S(1)} %pad_maximum_fusion.4.side_ref, f32[24,128]{1,0:T(8,128)S(1)} %constant_dynamic-update-slice_fusion.own_ref, f32[8,24,128]{2,1,0:T(8,128)S(1)} %collective-permute-done.3.part_ref, f32[24,128]{1,0:T(8,128)S(1)} %get-tuple-element.11.share_ref), custom_call_target="tpu_custom_call" | custom-call | flops 7864320 | bytes 102400 | tf_op jit(solution)/shard_map/pallas_call | solution.py:324
  18.6 0.2 %collective-permute-done.5.there_ref = f32[9,24,128]{2,1,0:T(8,128)S(1)} collective-permute-done((f32[9,24,128]{2,1,0:T(8,128)S(1)}, f32[9,24,128]{2,1,0:T(8,128)S(1)}, u32[]{:S(2)}, u32[]{:S(2)}) %collective-permute-start.5) | collective-permute-done | bytes 110624 | tf_op jit(solution)/shard_map/ppermute | solution.py:362
  18.8 3.8 %shard_map.70 = (f32[128,128]{1,0:T(8,128)}, f32[16,128]{1,0:T(8,128)}) custom-call(f32[10,128]{1,0:T(8,128)S(1)} %pad_maximum_fusion.4.side_ref, f32[24,128]{1,0:T(8,128)S(1)} %constant_dynamic-update-slice_fusion.own_ref, f32[9,24,128]{2,1,0:T(8,128)S(1)} %collective-permute-done.5.there_ref, f32[24,128]{1,0:T(8,128)S(1)} %shard_map.69.share_ref), custom_call_target="tpu_custom_call" | custom-call | tf_op jit(solution)/shard_map/pallas_call | solution.py:337
  (7 shorter events, 0.0 us)
Async XLA Ops:
  0.6 0.7 %copy-start = (f32[16,128]{1,0:T(8,128)S(1)}, f32[16,128]{1,0:T(8,128)}, u32[]{:S(2)}) copy-start(f32[16,128]{1,0:T(8,128)} %param.6) | copy-start | bytes 24580
  1.3 3.5 %copy-start.1 = (f32[8]{0:T(128)S(1)}, f32[8]{0:T(128)}, u32[]{:S(2)}) copy-start(f32[8]{0:T(128)} %param.7) | copy-start | bytes 100
  1.3 4.9 %collective-permute-start = (f32[1,24,128]{2,1,0:T(8,128)S(1)}, f32[1,24,128]{2,1,0:T(8,128)S(1)}, u32[]{:S(2)}, u32[]{:S(2)}) collective-permute-start(f32[1,24,128]{2,1,0:T(8,128)S(1)} %bitcast.4), channel_id=1, source_target_pairs={{0,9},{1,8},{2,11},{3,10},{4,13},{5,12},{6,15},{7,14},{8,1},{9,0},... | collective-permute-start | bytes 36872 | tf_op jit(solution)/shard_map/ppermute | solution.py:362
  4.8 3.3 %copy-start.2 = (s32[128]{0:T(128)S(1)}, s32[128]{0:T(128)}, u32[]{:S(2)}) copy-start(s32[128]{0:T(128)} %param.9) | copy-start | bytes 1540
  6.2 3.4 %collective-permute-start.1 = (f32[2,24,128]{2,1,0:T(8,128)S(1)}, f32[2,24,128]{2,1,0:T(8,128)S(1)}, u32[]{:S(2)}, u32[]{:S(2)}) collective-permute-start(f32[2,24,128]{2,1,0:T(8,128)S(1)} %pad_maximum_fusion.3), channel_id=1, source_target_pairs={{0,5},{1,4},{2,7},{3,6},{4,1},{5,0},{6,3},{7,2},{8,13},{9,12},{10,... | collective-permute-start | bytes 73736 | tf_op jit(solution)/shard_map/ppermute | solution.py:362
  9.6 3.5 %collective-permute-start.2 = (f32[4,24,128]{2,1,0:T(8,128)S(1)}, f32[4,24,128]{2,1,0:T(8,128)S(1)}, u32[]{:S(2)}, u32[]{:S(2)}) collective-permute-start(f32[4,24,128]{2,1,0:T(8,128)S(1)} %pad_maximum_fusion.2), channel_id=1, source_target_pairs={{0,17},{1,2},{2,1},{3,18},{4,7},{5,20},{6,23},{7,4},{8,11},{9,24},... | collective-permute-start | bytes 147464 | tf_op jit(solution)/shard_map/ppermute | solution.py:362
  11.4 3.6 %collective-permute-start.4 = (f32[24,128]{1,0:T(8,128)S(1)}, f32[24,128]{1,0:T(8,128)S(1)}, u32[]{:S(2)}, u32[]{:S(2)}) collective-permute-start(f32[24,128]{1,0:T(8,128)S(1)} %constant_dynamic-update-slice_fusion.own_ref), channel_id=1, source_target_pairs={{0,1},{1,0},{2,3},{3,2},{4,5},{5,4},{6,7},{7,6},{8,9},{9,8},{10,11... | collective-permute-start | bytes 36872 | tf_op jit(solution)/shard_map/ppermute | solution.py:362
  13.2 4.1 %collective-permute-start.3 = (f32[8,24,128]{2,1,0:T(8,128)S(1)}, f32[8,24,128]{2,1,0:T(8,128)S(1)}, u32[]{:S(2)}, u32[]{:S(2)}) collective-permute-start(f32[8,24,128]{2,1,0:T(8,128)S(1)} %pad_maximum_fusion.1.part_ref), channel_id=1, source_target_pairs={{0,3},{1,16},{2,19},{3,0},{4,21},{5,6},{6,5},{7,22},{8,25},{9,10},... | collective-permute-start | bytes 294920 | tf_op jit(solution)/shard_map/ppermute | solution.py:362
  17.3 1.5 %collective-permute-start.5 = (f32[9,24,128]{2,1,0:T(8,128)S(1)}, f32[9,24,128]{2,1,0:T(8,128)S(1)}, u32[]{:S(2)}, u32[]{:S(2)}) collective-permute-start(f32[9,24,128]{2,1,0:T(8,128)S(1)} %pad_maximum_fusion), channel_id=1, source_target_pairs={{0,1},{1,0},{2,3},{3,2},{4,5},{5,4},{6,7},{7,6},{8,9},{9,8},{10,11... | collective-permute-start | bytes 331784 | tf_op jit(solution)/shard_map/ppermute | solution.py:362

commit v11 on v10

--- a/solution.py
+++ b/solution.py
@@ -287,7 +287,7 @@
             pltpu.make_async_copy(rows_ref.at[rows, :], panel_ref.at[rows, :], sems.at[step])
         )
         copies[-1].start()
-        if step == steps // 2:
+        if step == steps - 2:
             copies.append(pltpu.make_async_copy(total_ref, product_ref, total_sem))
             copies[-1].start()
     for copy in copies:

time: 22.9 us -> 22.9 us (level)
  no operation moved by 1% of the time
where the time goes in v11:
time: 22.9 us; the launch traced here: 22.6 us
  starting transfers between devices  9.67 us (42%)
  Pallas kernels  5.52 us (24%)
  waiting for transfers between devices  5.24 us (23%)
  between operations  1.31 us (6%)
  local copies, waits for them, and re-layouts  0.71 us (3%)
    ppermute x6, starting transfers between devices, swap(): return lax.ppermute(value, ('blk', 'grp'), pairs)  9.67 us
    ppermute x6, waiting for transfers between devices, swap(): return lax.ppermute(value, ('blk', 'grp'), pairs)  5.24 us
    pallas_call x1, Pallas kernels, finish(): pl.pallas_call(functools.partial(last_body, layout), out_shape=(jax.Shape...  3.82 us
    pallas_call x1, Pallas kernels, early(): pl.pallas_call(functools.partial(early_body, layout), out_shape=(jax.Shap...  0.98 us
    pallas_call x1, Pallas kernels, middle(): pl.pallas_call(functools.partial(middle_body, layout, place), out_shape=j...  0.72 us
    unnamed x7, local copies, waits for them, and re-layouts  0.71 us
  transfers between devices with their start and end apart: 6, of which 5 were waited for; matrix products, arithmetic and copies ran while one was open for 1% of the time, Pallas kernels for 8%

profile of v11, /device:TPU:0, one launch (start us, length us, event | category | flops | bytes accessed | tf_op | source)
XLA Modules:
  0.0 22.6 jit_solution(14846284361018764346)
XLA Ops:
  0.6 0.0 copy-start
  0.6 0.7 %constant_dynamic-update-slice_fusion.1 = f32[24,128]{1,0:T(8,128)S(1)} fusion(f32[8,128]{1,0:T(8,128)} %param.5), kind=kLoop, calls=%fused_computation.6 | loop fusion | bytes 8192
  1.3 0.0 copy-done
  1.3 0.0 copy-start.1
  1.3 3.5 %collective-permute-start = (f32[1,24,128]{2,1,0:T(8,128)S(1)}, f32[1,24,128]{2,1,0:T(8,128)S(1)}, u32[]{:S(2)}, u32[]{:S(2)}) collective-permute-start(f32[1,24,128]{2,1,0:T(8,128)S(1)} %bitcast.4), channel_id=1, source_target_pairs={{0,9},{1,8},{2,11},{3,10},{4,13},{5,12},{6,15},{7,14},{8,1},{9,0},... | collective-permute-start | bytes 36872 | tf_op jit(solution)/shard_map/ppermute | solution.py:362
  4.8 0.0 copy-done.1
  4.8 0.0 copy-start.2
  4.8 1.4 %collective-permute-done = f32[1,24,128]{2,1,0:T(8,128)S(1)} collective-permute-done((f32[1,24,128]{2,1,0:T(8,128)S(1)}, f32[1,24,128]{2,1,0:T(8,128)S(1)}, u32[]{:S(2)}, u32[]{:S(2)}) %collective-permute-start) | collective-permute-done | bytes 12320 | tf_op jit(solution)/shard_map/ppermute | solution.py:362
  6.2 1.9 %collective-permute-start.1 = (f32[2,24,128]{2,1,0:T(8,128)S(1)}, f32[2,24,128]{2,1,0:T(8,128)S(1)}, u32[]{:S(2)}, u32[]{:S(2)}) collective-permute-start(f32[2,24,128]{2,1,0:T(8,128)S(1)} %pad_maximum_fusion.3), channel_id=1, source_target_pairs={{0,5},{1,4},{2,7},{3,6},{4,1},{5,0},{6,3},{7,2},{8,13},{9,12},{10,... | collective-permute-start | bytes 73736 | tf_op jit(solution)/shard_map/ppermute | solution.py:362
  8.1 0.0 copy-done.2
  8.8 0.9 %collective-permute-done.1 = f32[2,24,128]{2,1,0:T(8,128)S(1)} collective-permute-done((f32[2,24,128]{2,1,0:T(8,128)S(1)}, f32[2,24,128]{2,1,0:T(8,128)S(1)}, u32[]{:S(2)}, u32[]{:S(2)}) %collective-permute-start.1) | collective-permute-done | bytes 24608 | tf_op jit(solution)/shard_map/ppermute | solution.py:362
  9.6 1.7 %collective-permute-start.2 = (f32[4,24,128]{2,1,0:T(8,128)S(1)}, f32[4,24,128]{2,1,0:T(8,128)S(1)}, u32[]{:S(2)}, u32[]{:S(2)}) collective-permute-start(f32[4,24,128]{2,1,0:T(8,128)S(1)} %pad_maximum_fusion.2), channel_id=1, source_target_pairs={{0,17},{1,2},{2,1},{3,18},{4,7},{5,20},{6,23},{7,4},{8,11},{9,24},... | collective-permute-start | bytes 147464 | tf_op jit(solution)/shard_map/ppermute | solution.py:362
  11.3 0.1 pad_maximum_fusion.5
  11.4 0.4 %collective-permute-start.4 = (f32[24,128]{1,0:T(8,128)S(1)}, f32[24,128]{1,0:T(8,128)S(1)}, u32[]{:S(2)}, u32[]{:S(2)}) collective-permute-start(f32[24,128]{1,0:T(8,128)S(1)} %constant_dynamic-update-slice_fusion.own_ref), channel_id=1, source_target_pairs={{0,1},{1,0},{2,3},{3,2},{4,5},{5,4},{6,7},{7,6},{8,9},{9,8},{10,11... | collective-permute-start | bytes 36872 | tf_op jit(solution)/shard_map/ppermute | solution.py:362
  11.8 1.4 %collective-permute-done.2 = f32[4,24,128]{2,1,0:T(8,128)S(1)} collective-permute-done((f32[4,24,128]{2,1,0:T(8,128)S(1)}, f32[4,24,128]{2,1,0:T(8,128)S(1)}, u32[]{:S(2)}, u32[]{:S(2)}) %collective-permute-start.2) | collective-permute-done | bytes 49184 | tf_op jit(solution)/shard_map/ppermute | solution.py:362
  13.2 1.7 %collective-permute-start.3 = (f32[8,24,128]{2,1,0:T(8,128)S(1)}, f32[8,24,128]{2,1,0:T(8,128)S(1)}, u32[]{:S(2)}, u32[]{:S(2)}) collective-permute-start(f32[8,24,128]{2,1,0:T(8,128)S(1)} %pad_maximum_fusion.1.part_ref), channel_id=1, source_target_pairs={{0,3},{1,16},{2,19},{3,0},{4,21},{5,6},{6,5},{7,22},{8,25},{9,10},... | collective-permute-start | bytes 294920 | tf_op jit(solution)/shard_map/ppermute | solution.py:362
  14.9 0.1 pad_maximum_fusion.4.side_ref
  14.9 0.0 collective-permute-done.4.mate_ref
  14.9 1.0 %shard_map.68 = (f32[24,128]{1,0:T(8,128)S(1)}, f32[1,24,128]{2,1,0:T(8,128)S(1)}) custom-call(f32[10,128]{1,0:T(8,128)S(1)} %pad_maximum_fusion.4.side_ref, f32[24,128]{1,0:T(8,128)S(1)} %constant_dynamic-update-slice_fusion.own_ref, f32[24,128]{1,0:T(8,128)S(1)} %collective-permute-done.4.mate_ref, f32[8,24,128]{2,1,0:T(8,128)S(1)} %pad_maximum_fusion.1.part_ref), custom_call_target="tpu_custom_call" | custom-call | flops 15728640 | bytes 102400 | tf_op jit(solution)/shard_map/pallas_call | solution.py:309
  15.9 1.3 %collective-permute-done.3.part_ref = f32[8,24,128]{2,1,0:T(8,128)S(1)} collective-permute-done((f32[8,24,128]{2,1,0:T(8,128)S(1)}, f32[8,24,128]{2,1,0:T(8,128)S(1)}, u32[]{:S(2)}, u32[]{:S(2)}) %collective-permute-start.3) | collective-permute-done | bytes 98336 | tf_op jit(solution)/shard_map/ppermute | solution.py:362
  17.3 0.6 %collective-permute-start.5 = (f32[9,24,128]{2,1,0:T(8,128)S(1)}, f32[9,24,128]{2,1,0:T(8,128)S(1)}, u32[]{:S(2)}, u32[]{:S(2)}) collective-permute-start(f32[9,24,128]{2,1,0:T(8,128)S(1)} %pad_maximum_fusion), channel_id=1, source_target_pairs={{0,1},{1,0},{2,3},{3,2},{4,5},{5,4},{6,7},{7,6},{8,9},{9,8},{10,11... | collective-permute-start | bytes 331784 | tf_op jit(solution)/shard_map/ppermute | solution.py:362
  17.8 0.7 %shard_map.69.share_ref = f32[24,128]{1,0:T(8,128)S(1)} custom-call(f32[10,128]{1,0:T(8,128)S(1)} %pad_maximum_fusion.4.side_ref, f32[24,128]{1,0:T(8,128)S(1)} %constant_dynamic-update-slice_fusion.own_ref, f32[8,24,128]{2,1,0:T(8,128)S(1)} %collective-permute-done.3.part_ref, f32[24,128]{1,0:T(8,128)S(1)} %get-tuple-element.11.share_ref), custom_call_target="tpu_custom_call" | custom-call | flops 7864320 | bytes 102400 | tf_op jit(solution)/shard_map/pallas_call | solution.py:324
  18.6 0.2 %collective-permute-done.5.there_ref = f32[9,24,128]{2,1,0:T(8,128)S(1)} collective-permute-done((f32[9,24,128]{2,1,0:T(8,128)S(1)}, f32[9,24,128]{2,1,0:T(8,128)S(1)}, u32[]{:S(2)}, u32[]{:S(2)}) %collective-permute-start.5) | collective-permute-done | bytes 110624 | tf_op jit(solution)/shard_map/ppermute | solution.py:362
  18.8 3.8 %shard_map.70 = (f32[128,128]{1,0:T(8,128)}, f32[16,128]{1,0:T(8,128)}) custom-call(f32[10,128]{1,0:T(8,128)S(1)} %pad_maximum_fusion.4.side_ref, f32[24,128]{1,0:T(8,128)S(1)} %constant_dynamic-update-slice_fusion.own_ref, f32[9,24,128]{2,1,0:T(8,128)S(1)} %collective-permute-done.5.there_ref, f32[24,128]{1,0:T(8,128)S(1)} %shard_map.69.share_ref), custom_call_target="tpu_custom_call" | custom-call | tf_op jit(solution)/shard_map/pallas_call | solution.py:337
  (7 shorter events, 0.0 us)
Async XLA Ops:
  0.6 0.7 %copy-start = (f32[16,128]{1,0:T(8,128)S(1)}, f32[16,128]{1,0:T(8,128)}, u32[]{:S(2)}) copy-start(f32[16,128]{1,0:T(8,128)} %param.6) | copy-start | bytes 24580
  1.3 3.5 %copy-start.1 = (f32[8]{0:T(128)S(1)}, f32[8]{0:T(128)}, u32[]{:S(2)}) copy-start(f32[8]{0:T(128)} %param.7) | copy-start | bytes 100
  1.3 4.9 %collective-permute-start = (f32[1,24,128]{2,1,0:T(8,128)S(1)}, f32[1,24,128]{2,1,0:T(8,128)S(1)}, u32[]{:S(2)}, u32[]{:S(2)}) collective-permute-start(f32[1,24,128]{2,1,0:T(8,128)S(1)} %bitcast.4), channel_id=1, source_target_pairs={{0,9},{1,8},{2,11},{3,10},{4,13},{5,12},{6,15},{7,14},{8,1},{9,0},... | collective-permute-start | bytes 36872 | tf_op jit(solution)/shard_map/ppermute | solution.py:362
  4.8 3.3 %copy-start.2 = (s32[128]{0:T(128)S(1)}, s32[128]{0:T(128)}, u32[]{:S(2)}) copy-start(s32[128]{0:T(128)} %param.9) | copy-start | bytes 1540
  6.2 3.4 %collective-permute-start.1 = (f32[2,24,128]{2,1,0:T(8,128)S(1)}, f32[2,24,128]{2,1,0:T(8,128)S(1)}, u32[]{:S(2)}, u32[]{:S(2)}) collective-permute-start(f32[2,24,128]{2,1,0:T(8,128)S(1)} %pad_maximum_fusion.3), channel_id=1, source_target_pairs={{0,5},{1,4},{2,7},{3,6},{4,1},{5,0},{6,3},{7,2},{8,13},{9,12},{10,... | collective-permute-start | bytes 73736 | tf_op jit(solution)/shard_map/ppermute | solution.py:362
  9.6 3.5 %collective-permute-start.2 = (f32[4,24,128]{2,1,0:T(8,128)S(1)}, f32[4,24,128]{2,1,0:T(8,128)S(1)}, u32[]{:S(2)}, u32[]{:S(2)}) collective-permute-start(f32[4,24,128]{2,1,0:T(8,128)S(1)} %pad_maximum_fusion.2), channel_id=1, source_target_pairs={{0,17},{1,2},{2,1},{3,18},{4,7},{5,20},{6,23},{7,4},{8,11},{9,24},... | collective-permute-start | bytes 147464 | tf_op jit(solution)/shard_map/ppermute | solution.py:362
  11.4 3.6 %collective-permute-start.4 = (f32[24,128]{1,0:T(8,128)S(1)}, f32[24,128]{1,0:T(8,128)S(1)}, u32[]{:S(2)}, u32[]{:S(2)}) collective-permute-start(f32[24,128]{1,0:T(8,128)S(1)} %constant_dynamic-update-slice_fusion.own_ref), channel_id=1, source_target_pairs={{0,1},{1,0},{2,3},{3,2},{4,5},{5,4},{6,7},{7,6},{8,9},{9,8},{10,11... | collective-permute-start | bytes 36872 | tf_op jit(solution)/shard_map/ppermute | solution.py:362
  13.2 4.1 %collective-permute-start.3 = (f32[8,24,128]{2,1,0:T(8,128)S(1)}, f32[8,24,128]{2,1,0:T(8,128)S(1)}, u32[]{:S(2)}, u32[]{:S(2)}) collective-permute-start(f32[8,24,128]{2,1,0:T(8,128)S(1)} %pad_maximum_fusion.1.part_ref), channel_id=1, source_target_pairs={{0,3},{1,16},{2,19},{3,0},{4,21},{5,6},{6,5},{7,22},{8,25},{9,10},... | collective-permute-start | bytes 294920 | tf_op jit(solution)/shard_map/ppermute | solution.py:362
  17.3 1.5 %collective-permute-start.5 = (f32[9,24,128]{2,1,0:T(8,128)S(1)}, f32[9,24,128]{2,1,0:T(8,128)S(1)}, u32[]{:S(2)}, u32[]{:S(2)}) collective-permute-start(f32[9,24,128]{2,1,0:T(8,128)S(1)} %pad_maximum_fusion), channel_id=1, source_target_pairs={{0,1},{1,0},{2,3},{3,2},{4,5},{5,4},{6,7},{7,6},{8,9},{9,8},{10,11... | collective-permute-start | bytes 331784 | tf_op jit(solution)/shard_map/ppermute | solution.py:362
